TPU v7x, 32 devices: a whole 2x2x4 slice. The times are simulated.
32 devices in a mesh: row: 4 (over y, core), seq: 8 (over z, x).
Axes of the slice: x: 2, y: 2, z: 4, core: 2. Of those that a mesh axis runs over, the one named last changes fastest.
Arguments:
- tokens: bfloat16 [4, 2048, 1536], P('row', 'seq'), may hold values from -6 to 6
- norm_gain: bfloat16 [1536], replicated, may hold values from 0.5 to 1.5
- input_weight: bfloat16 [1536, 6144], P('row'), may hold values from -0.15625 to 0.15625
- conv_weight: bfloat16 [4, 3072], replicated, may hold values from -3 to 3
- conv_bias: bfloat16 [3072], replicated, may hold values from -3 to 3
- select_weight: bfloat16 [3072, 128], replicated, may hold values from -0.109375 to 0.109375
- step_weight: bfloat16 [96, 3072], replicated, may hold values from -0.625 to 0.625
- step_bias: float32 [3072], replicated, may hold values from -13 to -3.5
- decay_log: bfloat16 [3072, 16], replicated, may hold values from 0 to 2.765625
- skip_scale: bfloat16 [3072], replicated, may hold values from 0.5 to 1.5
- output_weight: bfloat16 [3072, 1536], replicated, may hold values from -0.21875 to 0.21875
- attn_gain: bfloat16 [1536], replicated, may hold values from 0.5 to 1.5
- attn_weight: bfloat16 [1536, 4608], replicated, may hold values from -0.15625 to 0.15625
- attn_output: bfloat16 [1536, 1536], replicated, may hold values from -0.625 to 0.625
- mlp_gain: bfloat16 [2, 1536], replicated, may hold values from 0.5 to 1.5
- mlp_up_weight: bfloat16 [2, 1536, 8192], P(None, 'row'), may hold values from -0.15625 to 0.15625
- mlp_down_weight: bfloat16 [2, 4096, 1536], P(None, 'row'), may hold values from -0.1875 to 0.1875
- doc_lengths: int32 [4, 8], P('row'), may hold values from 1 to 1920, 2048 in all within a row
- cotangent: bfloat16 [4, 2048, 1536], P('row', 'seq'), may hold values from -6 to 6
Outputs:
- output: bfloat16 [4, 2048, 1536], P('row', 'seq')
- tokens_grad: bfloat16 [4, 2048, 1536], P('row', 'seq')
- norm_gain_grad: float32 [1536], P(('row', 'seq'))
- input_weight_grad: float32 [1536, 6144], P(None, ('row', 'seq'))
- conv_weight_grad: float32 [4, 3072], P(None, ('row', 'seq'))
- conv_bias_grad: float32 [3072], P(('row', 'seq'))
- select_weight_grad: float32 [3072, 128], P(('row', 'seq'))
- step_weight_grad: float32 [96, 3072], P(None, ('row', 'seq'))
- step_bias_grad: float32 [3072], P(('row', 'seq'))
- decay_log_grad: float32 [3072, 16], P(('row', 'seq'))
- skip_scale_grad: float32 [3072], P(('row', 'seq'))
- output_weight_grad: float32 [3072, 1536], P(('row', 'seq'))
- attn_gain_grad: float32 [1536], P(('row', 'seq'))
- attn_weight_grad: float32 [1536, 4608], P(None, ('row', 'seq'))
- attn_output_grad: float32 [1536, 1536], P(('row', 'seq'))
- mlp_gain_grad: float32 [2, 1536], P(None, ('row', 'seq'))
- mlp_up_weight_grad: float32 [2, 1536, 8192], P(None, None, ('row', 'seq'))
- mlp_down_weight_grad: float32 [2, 4096, 1536], P(None, ('row', 'seq'))
All inputs are finite; a program needn't handle non-finite values.
Results may differ from a plain program's by a relative error of at most 0.028.
Values may be sent and summed in bfloat16 or wider, within the bound.
A program may use at most 512 MiB of HBM per device.

v0:
```python
import jax
import jax.numpy as jnp
from jax import lax
from jax.sharding import PartitionSpec as P

CONV = 4
HEADS = 12
HEAD_DIM = 128
WINDOW = 2048


eps = 1e-05
rope_base = 10000.0


def from_behind(x, axis, by):
    length = lax.axis_size(axis)
    pairs = [(i, i + by) for i in range(length) if 0 <= i + by < length]
    return lax.ppermute(x, axis, pairs)


def shortened(x):
    return jax.tree.map(lambda a: a.astype(jnp.bfloat16) if a.dtype == jnp.float32 else a, x)


def product(left_op, right_op):
    return jnp.dot(left_op, right_op, preferred_element_type=jnp.float32)


def left_trans(left_op, right_op):
    return lax.dot_general(
        left_op, right_op, (((0,), (0,)), ((), ())), preferred_element_type=jnp.float32
    )


def right_trans(left_op, right_op):
    return lax.dot_general(
        left_op, right_op, (((1,), (1,)), ((), ())), preferred_element_type=jnp.float32
    )


def weight_term(left_low, right_low, split_rows):
    n_row = lax.axis_size("row")
    n_seq = lax.axis_size("seq")
    rows_here = left_low.shape[0]
    if split_rows:
        moving, whole = (left_low, right_low)
    else:
        moving, whole = (right_low, left_low)
    columns = moving.shape[1]
    owned = columns // (n_row * n_seq)
    shaped = moving.reshape(rows_here, n_row, n_seq, owned)
    spread = lax.all_to_all(shaped, "seq", split_axis=2, concat_axis=0, tiled=True).reshape(
        n_seq * rows_here, n_row, owned
    )
    gathered = lax.all_gather(whole, "seq", axis=0, tiled=True)
    if split_rows:
        return jnp.einsum("tgc,tb->gcb", spread, gathered, preferred_element_type=jnp.float32)
    return jnp.einsum("ta,tgc->agc", gathered, spread, preferred_element_type=jnp.float32)


def norm_apply(values, gain_row):
    factor = lax.rsqrt(jnp.mean(values * values, axis=-1, keepdims=True) + eps)
    return (values * factor * gain_row, factor)


def norm_back(values, factor, gain_row, upstream):
    normed = values * factor
    weighted = upstream * gain_row
    gain_grad = jnp.sum(upstream * normed, axis=0)
    value_grad = factor * (weighted - normed * jnp.mean(weighted * normed, axis=-1, keepdims=True))
    return (value_grad, gain_grad)


def doc_index(positions, lengths):
    ends_at = jnp.cumsum(lengths)
    return jnp.sum((positions[:, None] >= ends_at[None, :]).astype(jnp.int32), axis=1)


def conv_masks(positions, lengths):
    own_doc = doc_index(positions, lengths)
    rows_out = []
    for tap_index in range(CONV):
        earlier = positions - (CONV - 1) + tap_index
        rows_out.append(
            ((earlier >= 0) & (doc_index(earlier, lengths) == own_doc)).astype(jnp.float32)
        )
    return jnp.stack(rows_out, axis=0)


def rotary_tables(positions):
    half_dim = HEAD_DIM // 2
    frequency = jnp.power(rope_base, -2.0 * jnp.arange(half_dim).astype(jnp.float32) / HEAD_DIM)
    angles = positions.astype(jnp.float32)[:, None] * frequency[None, :]
    return (jnp.cos(angles)[:, None, :], jnp.sin(angles)[:, None, :])


def rotate(values, cosine, sine_tab, turn_sign):
    rows_here = values.shape[0]
    shaped = values.reshape(rows_here, HEADS, 2, HEAD_DIM // 2)
    first_half = shaped[:, :, 0]
    second = shaped[:, :, 1]
    signed_sine = turn_sign * sine_tab
    turned = jnp.stack(
        [first_half * cosine - second * signed_sine, second * cosine + first_half * signed_sine],
        axis=2,
    )
    return turned.reshape(rows_here, HEADS * HEAD_DIM)


def split_heads(values):
    return values.reshape(values.shape[0], HEADS, HEAD_DIM).transpose(1, 0, 2)


def merge_heads(values):
    return values.transpose(1, 0, 2).reshape(values.shape[1], HEADS * HEAD_DIM)


def scan_blocks(start_hidden, step_size, activated, input_map, read_map, keep_flag, decays):
    rows_here = step_size.shape[0]
    block_len = min(64, rows_here)

    def one_step(hidden, entries):
        step_rate, drive_in, input_col, read_col, keep_one = entries
        hidden = (
            jnp.exp(decays * step_rate[None, :]) * keep_one * hidden
            + input_col[:, None] * drive_in[None, :]
        )
        return (hidden, jnp.sum(read_col[:, None] * hidden, axis=0))

    def one_block(hidden, entries):
        return lax.scan(one_step, hidden, entries, unroll=8)

    inputs = (step_size, step_size * activated, input_map, read_map, keep_flag)
    shaped = tuple(
        (
            member.reshape((rows_here // block_len, block_len) + member.shape[1:])
            for member in inputs
        )
    )
    end_hidden, outputs = lax.scan(jax.checkpoint(one_block), start_hidden, shaped)
    return (outputs.reshape(rows_here, activated.shape[1]), end_hidden)


def mlp_forward(values, gain_row, up_whole, down_whole):
    normed, factor = norm_apply(values, gain_row)
    low_normed = normed.astype(jnp.bfloat16)
    gate_up = product(low_normed, up_whole)
    ff_dim = down_whole.shape[0]
    gate_part = gate_up[:, :ff_dim]
    up_part = gate_up[:, ff_dim:]
    hidden = (jax.nn.silu(gate_part) * up_part).astype(jnp.bfloat16)
    return (values + product(hidden, down_whole), (factor, low_normed, gate_part, up_part, hidden))


def mlp_backward(values, gain_row, up_whole, down_whole, kept, upstream):
    factor, low_normed, gate_part, up_part, hidden = kept
    upstream_low = upstream.astype(jnp.bfloat16)
    g_down = weight_term(hidden, upstream_low, True)
    d_hidden = right_trans(upstream_low, down_whole)
    gate_sig = jax.nn.sigmoid(gate_part)
    d_gate = d_hidden * up_part * gate_sig * (1.0 + gate_part * (1.0 - gate_sig))
    d_up = d_hidden * jax.nn.silu(gate_part)
    d_gate_up = jnp.concatenate([d_gate, d_up], axis=1).astype(jnp.bfloat16)
    g_up = weight_term(low_normed, d_gate_up, False)
    d_norm, g_gain = norm_back(values, factor, gain_row, right_trans(d_gate_up, up_whole))
    return (upstream + d_norm, g_gain, g_up, g_down)


def per_device(
    tokens,
    norm_gain,
    input_weight,
    conv_weight,
    conv_bias,
    select_weight,
    step_weight,
    step_bias,
    decay_log,
    skip_scale,
    output_weight,
    attn_gain,
    attn_weight,
    attn_output,
    mlp_gain,
    mlp_up_weight,
    mlp_down_weight,
    doc_lengths,
    cotangent,
):
    rows_here = tokens.shape[1]
    width = tokens.shape[2]
    inner_dim = skip_scale.shape[0]
    rank_dim = step_weight.shape[0]
    state_dim = decay_log.shape[1]
    lengths = doc_lengths[0]
    seq_index = lax.axis_index("seq")
    positions = seq_index * rows_here + jnp.arange(rows_here, dtype=jnp.int32)
    gain_in = norm_gain.astype(jnp.float32)
    gain_attn = attn_gain.astype(jnp.float32)
    gains_mlp = mlp_gain.astype(jnp.float32)
    conv_taps = conv_weight.astype(jnp.float32)
    skip_row = skip_scale.astype(jnp.float32)
    decays = -jnp.exp(decay_log.astype(jnp.float32)).T
    source = tokens[0].astype(jnp.float32)
    own_doc = doc_index(positions, lengths)
    keep_flag = ((positions > 0) & (own_doc == doc_index(positions - 1, lengths))).astype(
        jnp.float32
    )
    tap_masks = conv_masks(positions, lengths)
    whole_in, up_both, down_both = (
        lax.all_gather(input_weight, "row", axis=0, tiled=True),
        lax.all_gather(mlp_up_weight, "row", axis=1, tiled=True),
        lax.all_gather(mlp_down_weight, "row", axis=1, tiled=True),
    )
    normed_in, factor_in = norm_apply(source, gain_in)
    low_in = normed_in.astype(jnp.bfloat16)
    mixed_in = product(low_in, whole_in)
    conv_input = mixed_in[:, :inner_dim]
    gate_input = mixed_in[:, inner_dim:]
    halo_rows = from_behind(
        conv_input[rows_here - (CONV - 1) :].astype(jnp.bfloat16), "seq", 1
    ).astype(jnp.float32)
    padded = jnp.concatenate([halo_rows, conv_input], axis=0)
    conv_pre = conv_bias.astype(jnp.float32)
    for tap_index in range(CONV):
        conv_pre = (
            conv_pre
            + conv_taps[tap_index]
            * padded[tap_index : tap_index + rows_here]
            * tap_masks[tap_index][:, None]
        )
    activated_low = jax.nn.silu(conv_pre).astype(jnp.bfloat16)
    activated = activated_low.astype(jnp.float32)
    picked = product(activated_low, select_weight)
    step_low = picked[:, :rank_dim].astype(jnp.bfloat16)
    step_pre = product(step_low, step_weight) + step_bias
    step_size = jax.nn.softplus(step_pre)
    input_map = picked[:, rank_dim : rank_dim + state_dim]
    read_map = picked[:, rank_dim + state_dim :]
    zero_hidden = jnp.zeros((state_dim, inner_dim), jnp.float32)
    local_end = scan_blocks(
        zero_hidden, step_size, activated, input_map, read_map, keep_flag, decays
    )[1]
    through = jnp.exp(decays * jnp.sum(step_size, axis=0)[None, :]) * jnp.min(keep_flag)

    def forward_hop(hop_index, carried):
        return from_behind((through * carried + local_end).astype(jnp.bfloat16), "seq", 1).astype(
            jnp.float32
        )

    start_hidden = lax.fori_loop(0, lax.axis_size("seq") - 1, forward_hop, zero_hidden)

    def scan_piece(step_in, act_in, map_in, read_in, decay_in):
        return scan_blocks(start_hidden, step_in, act_in, map_in, read_in, keep_flag, decay_in)

    scan_result, scan_pullback = jax.vjp(
        scan_piece, step_size, activated, input_map, read_map, decays
    )
    scanned = scan_result[0]
    mamba_out = scanned + skip_row * activated
    gate_act = jax.nn.silu(gate_input)
    gated = (mamba_out * gate_act).astype(jnp.bfloat16)
    first_out = source + product(gated, output_weight)
    up_first, down_first = (up_both[0], down_both[0])
    second_out, kept_first = mlp_forward(first_out, gains_mlp[0], up_first, down_first)
    normed_attn, factor_attn = norm_apply(second_out, gain_attn)
    low_attn = normed_attn.astype(jnp.bfloat16)
    triple = product(low_attn, attn_weight)
    cosine, sine_tab = rotary_tables(positions)
    query = rotate(triple[:, :width], cosine, sine_tab, 1.0).astype(jnp.bfloat16)
    key_value = jnp.concatenate(
        [rotate(triple[:, width : 2 * width], cosine, sine_tab, 1.0), triple[:, 2 * width :]],
        axis=1,
    ).astype(jnp.bfloat16)
    hop_count = min((WINDOW + rows_here - 1) // rows_here, lax.axis_size("seq") - 1)
    pieces = [key_value]
    moving = key_value
    for hop_index in range(hop_count):
        moving = from_behind(moving, "seq", 1)
        pieces.append(moving)
    context = jnp.concatenate(pieces[::-1], axis=0)
    key_pos = (seq_index - hop_count) * rows_here + jnp.arange(
        (hop_count + 1) * rows_here, dtype=jnp.int32
    )
    key_doc = doc_index(key_pos, lengths)
    allowed = (
        (key_pos[None, :] <= positions[:, None])
        & (key_pos[None, :] > positions[:, None] - WINDOW)
        & (key_pos[None, :] >= 0)
        & (key_doc[None, :] == own_doc[:, None])
    )
    inv_scale = HEAD_DIM ** (-0.5)
    query_heads = split_heads(query)
    key_heads = split_heads(context[:, :width])
    value_heads = split_heads(context[:, width:])

    def head_forward(entries):
        query_head, key_head, value_head = entries
        scores = jnp.where(allowed, right_trans(query_head, key_head) * inv_scale, -1e30)
        row_max = jnp.max(scores, axis=1, keepdims=True)
        exponent = jnp.where(allowed, jnp.exp(scores - row_max), 0.0)
        row_total = jnp.sum(exponent, axis=1, keepdims=True)
        softmax = (exponent / row_total).astype(jnp.bfloat16)
        return (product(softmax, value_head), (row_max + jnp.log(row_total))[:, 0])

    attended, log_total = lax.map(head_forward, (query_heads, key_heads, value_heads))
    attended_low = merge_heads(attended).astype(jnp.bfloat16)
    third_out = second_out + product(attended_low, attn_output)
    up_last, down_last = (up_both[1], down_both[1])
    final_out, kept_last = mlp_forward(third_out, gains_mlp[1], up_last, down_last)
    output = final_out.astype(jnp.bfloat16)
    grad_out = cotangent[0].astype(jnp.float32)
    d_third, g_gain_last, g_up_last, g_down_last = mlp_backward(
        third_out, gains_mlp[1], up_last, down_last, kept_last, grad_out
    )
    d_third_low = d_third.astype(jnp.bfloat16)
    g_attn_output = weight_term(attended_low, d_third_low, True)
    d_attended = right_trans(d_third_low, attn_output).astype(jnp.bfloat16)

    def head_backward(entries):
        query_head, key_head, value_head, d_head, log_row = entries
        scores = right_trans(query_head, key_head) * inv_scale
        softmax = jnp.where(allowed, jnp.exp(scores - log_row[:, None]), 0.0)
        d_soft = right_trans(d_head, value_head)
        center = jnp.sum(softmax * d_soft, axis=1, keepdims=True)
        d_scores = (softmax * (d_soft - center)).astype(jnp.bfloat16)
        return (
            product(d_scores, key_head) * inv_scale,
            left_trans(d_scores, query_head) * inv_scale,
            left_trans(softmax.astype(jnp.bfloat16), d_head),
        )

    d_query_heads, d_key_heads, d_value_heads = lax.map(
        head_backward, (query_heads, key_heads, value_heads, split_heads(d_attended), log_total)
    )
    d_context = jnp.concatenate([merge_heads(d_key_heads), merge_heads(d_value_heads)], axis=1)
    returned = d_context[:rows_here]
    for hop_index in range(hop_count):
        returned = (
            from_behind(returned.astype(jnp.bfloat16), "seq", -1).astype(returned.dtype)
            + d_context[(hop_index + 1) * rows_here : (hop_index + 2) * rows_here]
        )
    d_triple = jnp.concatenate(
        [
            rotate(merge_heads(d_query_heads), cosine, sine_tab, -1.0),
            rotate(returned[:, :width], cosine, sine_tab, -1.0),
            returned[:, width:],
        ],
        axis=1,
    ).astype(jnp.bfloat16)
    g_attn_weight = weight_term(low_attn, d_triple, False)
    d_attn_norm, g_attn_gain = norm_back(
        second_out, factor_attn, gain_attn, right_trans(d_triple, attn_weight)
    )
    d_second = d_third + d_attn_norm
    d_first, g_gain_first, g_up_first, g_down_first = mlp_backward(
        first_out, gains_mlp[0], up_first, down_first, kept_first, d_second
    )
    d_first_low = d_first.astype(jnp.bfloat16)
    g_output_weight = weight_term(gated, d_first_low, True)
    d_gated = right_trans(d_first_low, output_weight)
    d_scanned = d_gated * gate_act
    gate_sig = jax.nn.sigmoid(gate_input)
    d_gate = d_gated * mamba_out * gate_sig * (1.0 + gate_input * (1.0 - gate_sig))
    g_skip_scale = jnp.sum(d_scanned * activated, axis=0)

    def adjoint_step(carried, entries):
        step_rate, read_col, d_row, keep_one = entries
        adjoint = read_col[:, None] * d_row[None, :] + carried
        return (jnp.exp(decays * step_rate[None, :]) * keep_one * adjoint, None)

    back_end = lax.scan(
        adjoint_step,
        zero_hidden,
        (step_size, read_map, d_scanned, keep_flag),
        reverse=True,
        unroll=8,
    )[0]

    def backward_hop(hop_index, carried):
        return from_behind((through * carried + back_end).astype(jnp.bfloat16), "seq", -1).astype(
            jnp.float32
        )

    end_grad = lax.fori_loop(0, lax.axis_size("seq") - 1, backward_hop, zero_hidden)
    g_step, g_activated, g_input_map, g_read_map, g_decays = scan_pullback((d_scanned, end_grad))
    g_decay_log = (g_decays * decays).T
    d_step_pre = g_step * jax.nn.sigmoid(step_pre)
    g_step_bias = jnp.sum(d_step_pre, axis=0)
    d_step_low = d_step_pre.astype(jnp.bfloat16)
    g_step_weight = left_trans(step_low, d_step_low)
    d_picked = jnp.concatenate(
        [right_trans(d_step_low, step_weight), g_input_map, g_read_map], axis=1
    ).astype(jnp.bfloat16)
    g_select_weight = left_trans(activated_low, d_picked)
    d_activated = d_scanned * skip_row + g_activated + right_trans(d_picked, select_weight)
    pre_sig = jax.nn.sigmoid(conv_pre)
    d_conv_pre = d_activated * pre_sig * (1.0 + conv_pre * (1.0 - pre_sig))
    g_conv_bias = jnp.sum(d_conv_pre, axis=0)
    tap_grads = []
    d_padded = jnp.zeros((rows_here + CONV - 1, inner_dim), jnp.float32)
    for tap_index in range(CONV):
        masked = d_conv_pre * tap_masks[tap_index][:, None]
        tap_grads.append(jnp.sum(masked * padded[tap_index : tap_index + rows_here], axis=0))
        d_padded = d_padded + jnp.pad(
            masked * conv_taps[tap_index], ((tap_index, CONV - 1 - tap_index), (0, 0))
        )
    g_conv_weight = jnp.stack(tap_grads, axis=0)
    back_rows = from_behind(shortened(d_padded[: CONV - 1]), "seq", -1)
    d_conv_input = d_padded[CONV - 1 :] + jnp.pad(back_rows, ((rows_here - (CONV - 1), 0), (0, 0)))
    d_mixed = jnp.concatenate([d_conv_input, d_gate], axis=1).astype(jnp.bfloat16)
    g_input_weight = weight_term(low_in, d_mixed, False)
    d_normed_in = right_trans(d_mixed, whole_in)
    d_source, g_norm_gain = norm_back(source, factor_in, gain_in, d_normed_in)
    tokens_grad = (d_first + d_source).astype(jnp.bfloat16)
    g_mlp_gain = jnp.stack([g_gain_first, g_gain_last], axis=0)
    g_mlp_up = jnp.stack([g_up_first, g_up_last], axis=0)
    g_mlp_down = jnp.stack([g_down_first, g_down_last], axis=0)
    small = (
        lax.psum_scatter(g_norm_gain, ("row", "seq"), scatter_dimension=0, tiled=True),
        lax.psum_scatter(g_conv_weight, ("row", "seq"), scatter_dimension=1, tiled=True),
        lax.psum_scatter(g_conv_bias, ("row", "seq"), scatter_dimension=0, tiled=True),
        lax.psum_scatter(g_select_weight, ("row", "seq"), scatter_dimension=0, tiled=True),
        lax.psum_scatter(g_step_weight, ("row", "seq"), scatter_dimension=1, tiled=True),
        lax.psum_scatter(g_step_bias, ("row", "seq"), scatter_dimension=0, tiled=True),
        lax.psum_scatter(g_decay_log, ("row", "seq"), scatter_dimension=0, tiled=True),
        lax.psum_scatter(g_skip_scale, ("row", "seq"), scatter_dimension=0, tiled=True),
        lax.psum_scatter(g_attn_gain, ("row", "seq"), scatter_dimension=0, tiled=True),
        lax.psum_scatter(g_mlp_gain, ("row", "seq"), scatter_dimension=1, tiled=True),
    )
    large = (
        lax.psum_scatter(
            g_input_weight.astype(jnp.bfloat16), "row", scatter_dimension=1, tiled=True
        ).astype(jnp.float32),
        lax.psum_scatter(
            g_output_weight.astype(jnp.bfloat16), "row", scatter_dimension=0, tiled=True
        ).astype(jnp.float32),
        lax.psum_scatter(
            g_attn_weight.astype(jnp.bfloat16), "row", scatter_dimension=1, tiled=True
        ).astype(jnp.float32),
        lax.psum_scatter(
            g_attn_output.astype(jnp.bfloat16), "row", scatter_dimension=0, tiled=True
        ).astype(jnp.float32),
        lax.psum_scatter(
            g_mlp_up.astype(jnp.bfloat16), "row", scatter_dimension=2, tiled=True
        ).astype(jnp.float32),
        lax.psum_scatter(
            g_mlp_down.astype(jnp.bfloat16), "row", scatter_dimension=1, tiled=True
        ).astype(jnp.float32),
    )
    return (
        output[None],
        tokens_grad[None],
        small[0],
        large[0][:, 0],
        small[1],
        small[2],
        small[3],
        small[4],
        small[5],
        small[6],
        small[7],
        large[1][0],
        small[8],
        large[2][:, 0],
        large[3][0],
        small[9],
        large[4][:, :, 0],
        large[5][:, 0],
    )


def solution(mesh):
    return jax.shard_map(
        per_device,
        mesh=mesh,
        in_specs=(
            P("row", "seq", None),
            P(),
            P("row", None),
            P(),
            P(),
            P(),
            P(),
            P(),
            P(),
            P(),
            P(),
            P(),
            P(),
            P(),
            P(),
            P(None, "row", None),
            P(None, "row", None),
            P("row", None),
            P("row", "seq", None),
        ),
        out_specs=(
            P("row", "seq", None),
            P("row", "seq", None),
            P(("row", "seq")),
            P(None, ("row", "seq")),
            P(None, ("row", "seq")),
            P(("row", "seq")),
            P(("row", "seq"), None),
            P(None, ("row", "seq")),
            P(("row", "seq")),
            P(("row", "seq"), None),
            P(("row", "seq")),
            P(("row", "seq"), None),
            P(("row", "seq")),
            P(None, ("row", "seq")),
            P(("row", "seq"), None),
            P(None, ("row", "seq")),
            P(None, None, ("row", "seq")),
            P(None, ("row", "seq"), None),
        ),
        check_vma=False,
    )
```

profile of v0, /device:TPU:6, one launch (start us, length us, event | category | flops | bytes accessed | tf_op | source)
XLA Modules:
  0.0 5525.3 jit_solution(7988486103530587057)
XLA Ops:
  13.9 116.0 %all-gather.13.cloned.1.call-done = bf16[1536,6144]{1,0:T(8,128)(2,1)} async-done(((bf16[384,6144]{1,0:T(8,128)(2,1)}), bf16[1536,6144]{1,0:T(8,128)(2,1)}) %all-gather.13.cloned.1.call-update) | async-done | bytes 18874384 | tf_op jit(solution)/shard_map/all_gather | solution.py:212
  165.3 278.1 %while.271 = (s32[]{:T(128)}, f32[16,3072]{1,0:T(8,128)S(1)}, f32[4,64,3072]{2,1,0:T(8,128)}, f32[4,64,3072]{2,1,0:T(8,128)}, f32[4,64,16]{2,1,0:T(8,128)S(1)}, ...) while((s32[]{:T(128)}, f32[16,3072]{1,0:T(8,128)S(1)}, ...), condition=%wide.region_11.12_spmd.clone, body=%wide.region_8.0_spmd.sunk.clone | while | flops 1966091 | bytes 4337882 | solution.py:141
  498.5 422.8 %while.273 = (s32[]{:T(128)}, f32[16,3072]{1,0:T(8,128)S(1)}, f32[4,64,3072]{2,1,0:T(8,128)}, f32[4,16,3072]{2,1,0:T(8,128)}, f32[4,64,3072]{2,1,0:T(8,128)}, /*...) while((s32[]{:T(128)}, f32[16,3072]{1,0:T(8,128)S(1)}, ...), condition=%wide.region_25.26_spmd.clone, body=%wide.region_14.0_spmd.sunk.clone | while | flops 3710987 | bytes 10248738 | solution.py:141
  502.8 98.7 %while.272 = (s32[]{:T(128)}, f32[16,3072]{1,0:T(8,128)S(1)}, f32[8,8,3072]{2,1,0:T(8,128)}, f32[8,8,3072]{2,1,0:T(8,128)}, f32[16,3072]{1,0:T(8,128)S(1)}, /*in...) while((s32[]{:T(128)}, f32[16,3072]{1,0:T(8,128)S(1)}, ...), condition=%wide.region_24.24_spmd, body=%wide.region_15.23_spmd.sunk | while | flops 3710985 | bytes 4331729 | solution.py:132
  608.5 98.6 %while.272 = (s32[]{:T(128)}, f32[16,3072]{1,0:T(8,128)S(1)}, f32[8,8,3072]{2,1,0:T(8,128)}, f32[8,8,3072]{2,1,0:T(8,128)}, f32[16,3072]{1,0:T(8,128)S(1)}, /*in...) while((s32[]{:T(128)}, f32[16,3072]{1,0:T(8,128)S(1)}, ...), condition=%wide.region_24.24_spmd, body=%wide.region_15.23_spmd.sunk | while | flops 3710985 | bytes 4331729 | solution.py:132
  714.2 98.6 %while.272 = (s32[]{:T(128)}, f32[16,3072]{1,0:T(8,128)S(1)}, f32[8,8,3072]{2,1,0:T(8,128)}, f32[8,8,3072]{2,1,0:T(8,128)}, f32[16,3072]{1,0:T(8,128)S(1)}, /*in...) while((s32[]{:T(128)}, f32[16,3072]{1,0:T(8,128)S(1)}, ...), condition=%wide.region_24.24_spmd, body=%wide.region_15.23_spmd.sunk | while | flops 3710985 | bytes 4331729 | solution.py:132
  819.8 98.6 %while.272 = (s32[]{:T(128)}, f32[16,3072]{1,0:T(8,128)S(1)}, f32[8,8,3072]{2,1,0:T(8,128)}, f32[8,8,3072]{2,1,0:T(8,128)}, f32[16,3072]{1,0:T(8,128)S(1)}, /*in...) while((s32[]{:T(128)}, f32[16,3072]{1,0:T(8,128)S(1)}, ...), condition=%wide.region_24.24_spmd, body=%wide.region_15.23_spmd.sunk | while | flops 3710985 | bytes 4331729 | solution.py:132
  1255.5 90.3 %while.274 = (s32[]{:T(128)}, bf16[12,256,128]{1,2,0:T(8,128)(2,1)}, f32[12,256]{1,0:T(8,128)}, bf16[12,256,128]{2,1,0:T(8,128)(2,1)}, bf16[12,2048,128]{2,1,0:T...) while((s32[]{:T(128)}, bf16[12,256,128]{1,2,0:T(8,128)(2,1)}, ...), condition=%wide.region_32.33_spmd.clone.clone, body=%wide.region_29.32_spmd.clone.sunk.clone | while | flops 283115264 | bytes 7613561 | solution.py:307
  1398.4 197.8 %while.275 = (s32[]{:T(128)}, f32[12,256,128]{1,2,0:T(8,128)}, f32[12,2048,128]{1,2,0:T(8,128)}, f32[12,2048,128]{1,2,0:T(8,128)}, bf16[12,256,128]{2,1,0:T(8,12...) while((s32[]{:T(128)}, f32[12,256,128]{1,2,0:T(8,128)}, ...), condition=%wide.region_37.38_spmd.clone.clone, body=%wide.region_35.37_spmd.clone.sunk.clone | while | flops 679247616 | bytes 41319624 | solution.py:334
  1669.5 75.6 %collective-permute-done.11 = bf16[256,3072]{0,1:T(8,128)(2,1)S(1)} collective-permute-done((bf16[256,3072]{0,1:T(8,128)(2,1)S(1)}, bf16[256,3072]{0,1:T(8,128)(2,1)S(1)}, u32[]{:S(2)}, u32[]{:S(2)}) %collective-permute-start.11) | collective-permute-done | bytes 1572896 | tf_op jit(solution)/shard_map/ppermute | solution.py:19
  2210.4 278.8 %while.277 = (s32[]{:T(128)}, f32[16,3072]{1,0:T(8,128)S(1)}, f32[32,8,3072]{2,1,0:T(8,128)}, f32[16,3072]{1,0:T(8,128)S(1)}, f32[32,8]{1,0:T(8,128)S(1)}, /*index=5*/f32[32,8,16]{2,1,0:T(8,128)}, f32[32,8,3072]{2,1,0:T(8,128)}) while((s32[]{:T(128)}, f32[16,3072]{1,0:T(8,128)S(1)}, f32[32,8,3072]{2,1,0:T(8,128)}, ...), condition=%wide.region_41.42_spmd.clone.clone, body=%wide.region_40.41_spmd.clone.sunk.clone | while | flops 2015243 | bytes 1182591 | solution.py:373
  2495.4 96.6 %while.278 = (s32[]{:T(128)}, f32[16,3072]{1,0:T(8,128)S(1)}, f32[16,3072]{1,0:T(8,128)S(1)}, f32[16,3072]{1,0:T(8,128)S(1)}) while((s32[]{:T(128)}, f32[16,3072]{1,0:T(8,128)S(1)}, f32[16,3072]{1,0:T(8,128)S(1)}, f32[16,3072]{1,0:T(8,128)S(1)}) %tuple.897), condition=%wide.region_43.44_spmd.clone.clone, body=%wide.region_42.43_spmd.clone.sunk.clone | while | flops 245763 | bytes 1376359 | solution.py:386
  2597.3 1997.1 %while.281 = (s32[]{:T(128)}, f32[16,3072]{1,0:T(8,128)S(1)}, f32[16,3072]{1,0:T(8,128)S(1)}, f32[4,64,3072]{2,1,0:T(8,128)}, f32[4,64,3072]{2,1,0:T(8,128)}, /*...) while((s32[]{:T(128)}, f32[16,3072]{1,0:T(8,128)S(1)}, ...), condition=%wide.region_81.82_spmd.clone.clone, body=%wide.region_44.81_spmd.clone.sunk.clone | while | flops 10223381 | bytes 79371792 | solution.py:141
  2605.1 292.9 %while.279 = (s32[]{:T(128)}, f32[16,3072]{1,0:T(8,128)S(1)}, f32[8,8,16,3072]{3,2,1,0:T(8,128)}, f32[8,8,16,1]{2,1,3,0:T(8,128)S(1)}, f32[8,8,1,3072]{3,2,1,0:T...) while((s32[]{:T(128)}, f32[16,3072]{1,0:T(8,128)S(1)}, ...), condition=%wide.region_46.46_spmd, body=%wide.region_45.45_spmd.sunk | while | flops 3735558 | bytes 49795424 | solution.py:132
  2900.0 193.2 %while.280 = (s32[]{:T(128)}, f32[16,3072]{1,0:T(8,128)S(1)}, f32[16,3072]{1,0:T(8,128)}, f32[8,8,3072]{2,1,0:T(8,128)}, f32[8,8,3072]{2,1,0:T(8,128)}, /*index=...) while((s32[]{:T(128)}, f32[16,3072]{1,0:T(8,128)S(1)}, ...), condition=%wide.region_80.80_spmd.clone, body=%wide.region_47.79_spmd.clone.sunk | while | flops 6389515 | bytes 17524100 | solution.py:132
  3104.4 292.9 %while.279 = (s32[]{:T(128)}, f32[16,3072]{1,0:T(8,128)S(1)}, f32[8,8,16,3072]{3,2,1,0:T(8,128)}, f32[8,8,16,1]{2,1,3,0:T(8,128)S(1)}, f32[8,8,1,3072]{3,2,1,0:T...) while((s32[]{:T(128)}, f32[16,3072]{1,0:T(8,128)S(1)}, ...), condition=%wide.region_46.46_spmd, body=%wide.region_45.45_spmd.sunk | while | flops 3735558 | bytes 49795424 | solution.py:132
  3399.3 193.2 %while.280 = (s32[]{:T(128)}, f32[16,3072]{1,0:T(8,128)S(1)}, f32[16,3072]{1,0:T(8,128)}, f32[8,8,3072]{2,1,0:T(8,128)}, f32[8,8,3072]{2,1,0:T(8,128)}, /*index=...) while((s32[]{:T(128)}, f32[16,3072]{1,0:T(8,128)S(1)}, ...), condition=%wide.region_80.80_spmd.clone, body=%wide.region_47.79_spmd.clone.sunk | while | flops 6389515 | bytes 17524100 | solution.py:132
  3603.6 292.9 %while.279 = (s32[]{:T(128)}, f32[16,3072]{1,0:T(8,128)S(1)}, f32[8,8,16,3072]{3,2,1,0:T(8,128)}, f32[8,8,16,1]{2,1,3,0:T(8,128)S(1)}, f32[8,8,1,3072]{3,2,1,0:T...) while((s32[]{:T(128)}, f32[16,3072]{1,0:T(8,128)S(1)}, ...), condition=%wide.region_46.46_spmd, body=%wide.region_45.45_spmd.sunk | while | flops 3735558 | bytes 49795424 | solution.py:132
  3898.5 193.2 %while.280 = (s32[]{:T(128)}, f32[16,3072]{1,0:T(8,128)S(1)}, f32[16,3072]{1,0:T(8,128)}, f32[8,8,3072]{2,1,0:T(8,128)}, f32[8,8,3072]{2,1,0:T(8,128)}, /*index=...) while((s32[]{:T(128)}, f32[16,3072]{1,0:T(8,128)S(1)}, ...), condition=%wide.region_80.80_spmd.clone, body=%wide.region_47.79_spmd.clone.sunk | while | flops 6389515 | bytes 17524100 | solution.py:132
  4103.0 292.9 %while.279 = (s32[]{:T(128)}, f32[16,3072]{1,0:T(8,128)S(1)}, f32[8,8,16,3072]{3,2,1,0:T(8,128)}, f32[8,8,16,1]{2,1,3,0:T(8,128)S(1)}, f32[8,8,1,3072]{3,2,1,0:T...) while((s32[]{:T(128)}, f32[16,3072]{1,0:T(8,128)S(1)}, ...), condition=%wide.region_46.46_spmd, body=%wide.region_45.45_spmd.sunk | while | flops 3735558 | bytes 49795424 | solution.py:132
  4397.8 193.2 %while.280 = (s32[]{:T(128)}, f32[16,3072]{1,0:T(8,128)S(1)}, f32[16,3072]{1,0:T(8,128)}, f32[8,8,3072]{2,1,0:T(8,128)}, f32[8,8,3072]{2,1,0:T(8,128)}, /*index=...) while((s32[]{:T(128)}, f32[16,3072]{1,0:T(8,128)S(1)}, ...), condition=%wide.region_80.80_spmd.clone, body=%wide.region_47.79_spmd.clone.sunk | while | flops 6389515 | bytes 17524100 | solution.py:132
  5044.8 101.3 %reduce-scatter.36.cloned.1.call-done = f32[96,96]{1,0:T(8,128)} async-done(((f32[3072,96]{1,0:T(8,128)}), f32[96,96]{1,0:T(8,128)}) %reduce-scatter.36.cloned.1.call-update) | async-done | bytes 36880
  5242.0 171.8 %all-reduce.16.cloned.1.call-done = (bf16[2,1536,4,256]{3,1,2,0:T(8,128)(2,1)}, bf16[2,4,128,1536]{3,2,1,0:T(8,128)(2,1)}) async-done(((bf16[2,1536,4,256]{3,1,2,0:T(8,128)(2,1)}, bf16[2,4,128,1536]{3,2,1,0:T(8,128)(2,1)}), (bf16[2,1536,4,256]{3,1,2,0:T(8,128)(2,1)}, bf16[2,4,128,1536]{3,2,1,0:T(8,128)(2,1)})) %all-reduce.16.cloned.1.call-update) | async-done | bytes 9437200
  5420.8 97.5 %reduce-scatter.26.cloned.1.call-done = f32[96,128]{1,0:T(8,128)} async-done(((f32[3072,128]{1,0:T(8,128)}), f32[96,128]{1,0:T(8,128)}) %reduce-scatter.26.cloned.1.call-update) | async-done | bytes 49168 | tf_op jit(solution)/shard_map/reduce_scatter | solution.py:424
  (4726 shorter events, 5247.6 us)
Async XLA Ops:
  7.2 122.7 %all-gather.13.cloned.1.call-start = ((), (), s32[]{:S(2)}) async-start(), calls=%async_computation.17 | async-start | bytes 23592960 | tf_op jit(solution)/shard_map/all_gather | solution.py:212
  7.9 923.6 %all-gather.15.cloned.1.call-start = ((), (), s32[]{:S(2)}) async-start(), calls=%async_computation.18 | async-start | bytes 62914560 | tf_op jit(solution)/shard_map/all_gather | solution.py:213
  8.8 937.2 %all-gather.17.cloned.1.call-start = ((), (), s32[]{:S(2)}) async-start(), calls=%async_computation.19 | async-start | bytes 31457280 | tf_op jit(solution)/shard_map/all_gather | solution.py:214
  9.5 4671.6 %all-gather.25.cloned.1.call-start = ((), (), s32[]{:S(2)}) async-start(), calls=%async_computation.27 | async-start | bytes 7077888 | tf_op jit(solution)/shard_map/all_gather | solution.py:56
  1392.0 3367.6 %all-gather.23.cloned.1.call-start = ((), (), s32[]{:S(2)}) async-start(), calls=%async_computation.25 | async-start | bytes 7077888 | tf_op jit(solution)/shard_map/all_gather | solution.py:56
  1392.6 3381.1 %all-gather.19.cloned.1.call-start = ((), (), s32[]{:S(2)}) async-start(), calls=%async_computation.20 | async-start | bytes 7077888 | tf_op jit(solution)/shard_map/all_gather | solution.py:56
  1393.2 3401.9 %all-gather.33.cloned.1.call-start = ((), (), s32[]{:S(2)}) async-start(), calls=%async_computation.32 | async-start | bytes 7077888 | tf_op jit(solution)/shard_map/all_gather | solution.py:56
  1601.3 3229.4 %all-gather.29.cloned.1.call-start = ((), (), s32[]{:S(2)}) async-start(), calls=%async_computation.30 | async-start | bytes 7077888 | tf_op jit(solution)/shard_map/all_gather | solution.py:56
  1928.7 2918.6 %all-gather.21.cloned.1.call-start = ((), (), s32[]{:S(2)}) async-start(), calls=%async_computation.23 | async-start | bytes 7077888 | tf_op jit(solution)/shard_map/all_gather | solution.py:56
  2111.9 2742.5 %all-gather.27.cloned.1.call-start = ((), (), s32[]{:S(2)}) async-start(), calls=%async_computation.29 | async-start | bytes 7077888 | tf_op jit(solution)/shard_map/all_gather | solution.py:56
  2121.0 2747.0 %all-gather.31.cloned.1.call-start = ((), (), s32[]{:S(2)}) async-start(), calls=%async_computation.31 | async-start | bytes 7077888 | tf_op jit(solution)/shard_map/all_gather | solution.py:56
  2205.0 284.2 %all-to-all-start.7 = ((bf16[256,4,8,128]{3,1,0,2:T(4,128)(2,1)}), bf16[256,4,8,128]{3,1,0,2:T(4,128)(2,1)}, u32[]{:S(2)}, u32[]{:S(2)}) async-start(bf16[256,4,8,128]{3,1,0,2:T(4,128)(2,1)} %copy.202), calls=%async_computation.12 | async-start | bytes 4194304 | tf_op jit(solution)/shard_map/all_to_all | solution.py:53
  2489.2 2108.7 %all-to-all-start.5 = ((bf16[256,4,8,256]{3,1,0,2:T(4,128)(2,1)}), bf16[256,4,8,256]{3,1,0,2:T(4,128)(2,1)}, u32[]{:S(2)}, u32[]{:S(2)}) async-start(bf16[256,4,8,256]{3,1,0,2:T(4,128)(2,1)} %pad_maximum_fusion.2), calls=%async_computation.10 | async-start | bytes 8388608 | tf_op jit(solution)/shard_map/all_to_all | solution.py:53
  4660.4 86.7 %all-to-all-start = ((bf16[256,4,8,192]{0,3,1,2:T(8,128)(2,1)}), bf16[256,4,8,192]{0,3,1,2:T(8,128)(2,1)}, u32[]{:S(2)}, u32[]{:S(2)}) async-start(bf16[256,4,8,192]{0,3,1,2:T(8,128)(2,1)} %copy.183), calls=%async_computation | async-start | bytes 6291456 | tf_op jit(solution)/shard_map/all_to_all | solution.py:53
  4673.3 216.3 %reduce-scatter.40.cloned.1.call-start = ((), (), s32[]{:S(2)}) async-start(), calls=%async_computation.36 | async-start | bytes 811008
  4677.4 271.5 %reduce-scatter.34.cloned.1.call-start = ((), (), s32[]{:S(2)}) async-start(), calls=%async_computation.33 | async-start | bytes 1622016
  4679.2 340.7 %reduce-scatter.38.cloned.1.call-start = ((), (), s32[]{:S(2)}) async-start(), calls=%async_computation.35 | async-start | bytes 1622016
  4681.0 362.2 %reduce-scatter.32.cloned.1.call-start = ((), (), s32[]{:S(2)}) async-start(), calls=%async_computation.28 | async-start | bytes 737280 | tf_op jit(solution)/shard_map/reduce_scatter | solution.py:442
  4686.4 459.7 %reduce-scatter.36.cloned.1.call-start = ((), (), s32[]{:S(2)}) async-start(), calls=%async_computation.34 | async-start | bytes 1622016
  4755.8 420.5 %reduce-scatter.30.cloned.1.call-start = ((), (), s32[]{:S(2)}) async-start(), calls=%async_computation.26 | async-start | bytes 2211840 | tf_op jit(solution)/shard_map/reduce_scatter | solution.py:439
  4766.9 444.9 %reduce-scatter.24.cloned.1.call-start = ((), (), s32[]{:S(2)}) async-start(), calls=%async_computation.21 | async-start | bytes 2949120 | tf_op jit(solution)/shard_map/reduce_scatter | solution.py:433
  4830.7 409.5 %reduce-scatter.28.cloned.1.call-start = ((), (), s32[]{:S(2)}) async-start(), calls=%async_computation.24 | async-start | bytes 1474560 | tf_op jit(solution)/shard_map/reduce_scatter | solution.py:436
  4854.4 559.5 %all-reduce.16.cloned.1.call-start = ((), (), s32[]{:S(2)}) async-start(), calls=%async_computation.37 | async-start | bytes 18874368
  4876.6 641.7 %reduce-scatter.26.cloned.1.call-start = ((), (), s32[]{:S(2)}) async-start(), calls=%async_computation.22 | async-start | bytes 1622016 | tf_op jit(solution)/shard_map/reduce_scatter | solution.py:424
  (425 other events, 7712.9 us)
Sparse Core Ops, SparseCore 0:
  9.6 120.2 all-gather.12
  131.5 298.2 all-gather.14
  431.3 153.7 all-gather.16
  1392.1 100.3 all-gather.24
  1494.6 97.2 all-gather.22
  1593.8 139.1 all-gather.18
  1735.2 160.5 all-gather.32
  1928.8 128.2 all-gather.28
  2112.0 140.8 all-gather.20
  2255.0 97.3 all-gather.26
  2354.6 131.2 all-gather.30
  4679.5 133.9 reduce-scatter.39
  4818.7 100.0 reduce-scatter.33
  4923.8 96.0 reduce-scatter.37
  5022.9 20.2 reduce-scatter.31
  5048.3 97.8 reduce-scatter.35
  5148.6 27.6 reduce-scatter.29
  5178.8 33.0 reduce-scatter.23
  5214.5 25.6 reduce-scatter.27
  5243.4 170.3 all-reduce.15
  5420.5 97.8 reduce-scatter.25
where the time goes:
time: 5590 us; the launch traced here: 5530 us
  other arithmetic  1840 us (33%)
  waiting for transfers between devices  1530 us (27%)
  local copies, waits for them, and re-layouts  1510 us (27%)
  matrix products  420 us (8%)
  starting transfers between devices  161 us (3%)
    ppermute x30, waiting for transfers between devices, from_behind(): return lax.ppermute(x, axis, pairs)  725 us
    while x1512, local copies, waits for them, and re-layouts  437 us
    reduce_sum x192, other arithmetic, one_step(): return (hidden, jnp.sum(read_col[:, None] * hidden, axis=0))  360 us
    while x196, other arithmetic  353 us
    unnamed x26, waiting for transfers between devices  346 us
    slice x288, local copies, waits for them, and re-layouts, one_block(): return lax.scan(one_step, hidden, entries, unroll=8)  328 us
    reduce_sum x224, other arithmetic, one_step(): input_col[:, None] * drive_in[None, :]  268 us
    reduce_sum x32, other arithmetic, one_step(): decays * step_rate[None, :]  251 us

commit v1 on v0

v1 whole, which is shorter than its diff:
```python
import functools
import math

import jax
import jax.numpy as jnp
from jax import lax
from jax.experimental import pallas as pl
from jax.experimental.pallas import tpu as pltpu
from jax.sharding import PartitionSpec as P

LANES = 128
CHUNK = 32
RESET = 1e9
LOG2E = 1.4426950408889634
CONV = 4
HEADS = 12
HEAD_DIM = 128
WINDOW = 2048
GROUPS = 4
eps = 1e-05
rope_base = 10000.0


def from_behind(x, axis, by):
    length = lax.axis_size(axis)
    pairs = [(i, i + by) for i in range(length) if 0 <= i + by < length]
    return lax.ppermute(x, axis, pairs)


def product(left_op, right_op):
    return jnp.dot(left_op, right_op, preferred_element_type=jnp.float32)


def left_trans(left_op, right_op):
    return lax.dot_general(
        left_op, right_op, (((0,), (0,)), ((), ())), preferred_element_type=jnp.float32
    )


def right_trans(left_op, right_op):
    return lax.dot_general(
        left_op, right_op, (((1,), (1,)), ((), ())), preferred_element_type=jnp.float32
    )


def to_planes(tile_ref, value, group):
    for block in range(8):
        tile_ref[pl.ds(group * 64 + block * 8, 8), :] = value[:, block * LANES : (block + 1) * LANES]


def plane(tile_ref, index):
    return tile_ref[pl.ds((index // 8) * 64 + index % 8, 8, stride=8), :]


def tree_sum(terms):
    terms = list(terms)
    while len(terms) > 1:
        terms = [
            terms[i] + terms[i + 1] if i + 1 < len(terms) else terms[i]
            for i in range(0, len(terms), 2)
        ]
    return terms[0]


def scan_forward_kernel(
    with_output, states, chunk, *refs
):
    if with_output:
        (start_ref, step_ref, act_ref, keep_ref, in_ref, read_ref, decay_ref,
         out_ref, marks_ref, hidden_ref, step_t, drive_t, out_t) = refs
    else:
        (step_ref, act_ref, keep_ref, in_ref, decay_ref,
         end_ref, hidden_ref, step_t, drive_t) = refs
    index = pl.program_id(0)
    groups = step_ref.shape[1] // (8 * LANES)

    @pl.when(index == 0)
    def _():
        if with_output:
            hidden_ref[...] = start_ref[...]
        else:
            hidden_ref[...] = jnp.zeros_like(hidden_ref)

    if with_output:
        marks_ref[0] = hidden_ref[...]
    for group in range(groups):
        cols = pl.ds(group * 8 * LANES, 8 * LANES)
        for block in range(chunk // 8):
            rows = pl.ds(block * 8, 8)
            rate = step_ref[rows, cols]
            keep = keep_ref[rows, :]
            gated = jnp.where(jnp.concatenate([keep] * 8, axis=1) > 0, rate, RESET)
            to_planes(step_t, gated, block)
            to_planes(drive_t, rate * act_ref[rows, cols].astype(jnp.float32), block)
        decay = [decay_ref[n, pl.ds(group * 8, 8), :] * LOG2E for n in range(states)]

        def eight(block, hidden):
            hidden = list(hidden)
            for r in range(8):
                pos = index * chunk + block * 8 + r
                rate = step_t[pl.ds(block * 64 + r, 8, stride=8), :]
                drive = drive_t[pl.ds(block * 64 + r, 8, stride=8), :]
                terms = []
                for n in range(states):
                    hidden[n] = jnp.exp2(decay[n] * rate) * hidden[n] + drive * in_ref[pos * states + n]
                    if with_output:
                        terms.append(hidden[n] * read_ref[pos * states + n])
                if with_output:
                    out_t[pl.ds(block * 64 + r, 8, stride=8), :] = tree_sum(terms)
            return tuple(hidden)

        hidden = tuple(hidden_ref[n, pl.ds(group * 8, 8), :] for n in range(states))
        hidden = lax.fori_loop(0, chunk // 8, eight, hidden)
        for n in range(states):
            hidden_ref[n, pl.ds(group * 8, 8), :] = hidden[n]
        if with_output:
            for block in range(chunk // 8):
                for lane_block in range(8):
                    out_ref[pl.ds(block * 8, 8), pl.ds(group * 1024 + lane_block * LANES, LANES)] = out_t[
                        pl.ds(block * 64 + lane_block * 8, 8), :
                    ]
    if not with_output:
        end_ref[...] = hidden_ref[...]


def smem():
    return pl.BlockSpec(memory_space=pltpu.SMEM)


def scan_end(step, act, keep_lanes, in_flat, decay):
    rows, inner = step.shape
    states, planes, _ = decay.shape
    chunk = CHUNK
    whole = pl.BlockSpec((states, planes, LANES), lambda i: (0, 0, 0))
    rowed = pl.BlockSpec((chunk, inner), lambda i: (i, 0))
    return pl.pallas_call(
        functools.partial(scan_forward_kernel, False, states, chunk),
        out_shape=jax.ShapeDtypeStruct(decay.shape, jnp.float32),
        grid=(rows // chunk,),
        in_specs=[rowed, rowed, pl.BlockSpec((chunk, LANES), lambda i: (i, 0)), smem(), whole],
        out_specs=whole,
        scratch_shapes=[pltpu.VMEM(decay.shape, jnp.float32)]
        + [pltpu.VMEM((chunk * 8, LANES), jnp.float32)] * 2,
        compiler_params=pltpu.CompilerParams(vmem_limit_bytes=32 << 20),
        name="scan_end",
    )(step, act, keep_lanes, in_flat, decay)


def scan_out(start, step, act, keep_lanes, in_flat, read_flat, decay):
    rows, inner = step.shape
    states, planes, _ = decay.shape
    chunk = CHUNK
    whole = pl.BlockSpec((states, planes, LANES), lambda i: (0, 0, 0))
    rowed = pl.BlockSpec((chunk, inner), lambda i: (i, 0))
    return pl.pallas_call(
        functools.partial(scan_forward_kernel, True, states, chunk),
        out_shape=(
            jax.ShapeDtypeStruct((rows, inner), jnp.float32),
            jax.ShapeDtypeStruct((rows // chunk,) + decay.shape, jnp.float32),
        ),
        grid=(rows // chunk,),
        in_specs=[whole, rowed, rowed, pl.BlockSpec((chunk, LANES), lambda i: (i, 0)), smem(), smem(), whole],
        out_specs=(rowed, pl.BlockSpec((1, states, planes, LANES), lambda i: (i, 0, 0, 0))),
        scratch_shapes=[pltpu.VMEM(decay.shape, jnp.float32)]
        + [pltpu.VMEM((chunk * 8, LANES), jnp.float32)] * 3,
        compiler_params=pltpu.CompilerParams(vmem_limit_bytes=32 << 20),
        name="scan_out",
    )(start, step, act, keep_lanes, in_flat, read_flat, decay)


def adjoint_end_kernel(states, chunk, step_ref, grad_ref, keep_ref, read_ref, decay_ref, end_ref, carry_ref, step_t, grad_t):
    index = pl.program_id(0)
    last = pl.num_programs(0) - 1
    groups = step_ref.shape[1] // (8 * LANES)

    @pl.when(index == 0)
    def _():
        carry_ref[...] = jnp.zeros_like(carry_ref)

    for group in range(groups):
        cols = pl.ds(group * 8 * LANES, 8 * LANES)
        for block in range(chunk // 8):
            rows = pl.ds(block * 8, 8)
            keep = keep_ref[rows, :]
            to_planes(step_t, jnp.where(jnp.concatenate([keep] * 8, axis=1) > 0, step_ref[rows, cols], RESET), block)
            to_planes(grad_t, grad_ref[rows, cols], block)
        decay = [decay_ref[n, pl.ds(group * 8, 8), :] * LOG2E for n in range(states)]

        def eight(turn, carry):
            carry = list(carry)
            block = chunk // 8 - 1 - turn
            for r in range(7, -1, -1):
                pos = (last - index) * chunk + block * 8 + r
                rate = step_t[pl.ds(block * 64 + r, 8, stride=8), :]
                grad = grad_t[pl.ds(block * 64 + r, 8, stride=8), :]
                for n in range(states):
                    carry[n] = jnp.exp2(decay[n] * rate) * (carry[n] + grad * read_ref[pos * states + n])
            return tuple(carry)

        carry = tuple(carry_ref[n, pl.ds(group * 8, 8), :] for n in range(states))
        carry = lax.fori_loop(0, chunk // 8, eight, carry)
        for n in range(states):
            carry_ref[n, pl.ds(group * 8, 8), :] = carry[n]
    end_ref[...] = carry_ref[...]


def adjoint_end(step, grad, keep_lanes, read_flat, decay):
    rows, inner = step.shape
    states, planes, _ = decay.shape
    chunk = CHUNK
    count = rows // chunk
    whole = pl.BlockSpec((states, planes, LANES), lambda i: (0, 0, 0))
    rowed = pl.BlockSpec((chunk, inner), lambda i: (count - 1 - i, 0))
    return pl.pallas_call(
        functools.partial(adjoint_end_kernel, states, chunk),
        out_shape=jax.ShapeDtypeStruct(decay.shape, jnp.float32),
        grid=(count,),
        in_specs=[rowed, rowed, pl.BlockSpec((chunk, LANES), lambda i: (count - 1 - i, 0)), smem(), whole],
        out_specs=whole,
        scratch_shapes=[pltpu.VMEM(decay.shape, jnp.float32)]
        + [pltpu.VMEM((chunk * 8, LANES), jnp.float32)] * 2,
        compiler_params=pltpu.CompilerParams(vmem_limit_bytes=32 << 20),
        name="adjoint_end",
    )(step, grad, keep_lanes, read_flat, decay)


def adjoint_full_kernel(
    states, chunk,
    end_ref, marks_ref, step_ref, act_ref, grad_ref, keep_ref, in_ref, read_ref, decay_ref,
    d_step_ref, d_act_ref, d_in_ref, d_read_ref, d_decay_ref,
    carry_ref, step_t, rate_t, act_t, grad_t, d_step_t, d_act_t, factor_t, held_t, in_t, read_t,
):
    index = pl.program_id(0)
    last = pl.num_programs(0) - 1
    groups = step_ref.shape[1] // (8 * LANES)

    @pl.when(index == 0)
    def _():
        carry_ref[...] = end_ref[...]
        d_decay_ref[...] = jnp.zeros_like(d_decay_ref)

    for group in range(groups):
        cols = pl.ds(group * 8 * LANES, 8 * LANES)
        for block in range(chunk // 8):
            rows = pl.ds(block * 8, 8)
            rate = step_ref[rows, cols]
            keep = keep_ref[rows, :]
            to_planes(step_t, jnp.where(jnp.concatenate([keep] * 8, axis=1) > 0, rate, RESET), block)
            to_planes(rate_t, rate, block)
            to_planes(act_t, act_ref[rows, cols].astype(jnp.float32), block)
            to_planes(grad_t, grad_ref[rows, cols], block)

        def replay(block, hidden):
            hidden = list(hidden)
            for r in range(8):
                local = block * 8 + r
                pos = (last - index) * chunk + local
                view = pl.ds(block * 64 + r, 8, stride=8)
                gated = step_t[view, :]
                drive = rate_t[view, :] * act_t[view, :]
                grad = grad_t[view, :]
                for n in range(states):
                    slot = pl.ds((local * states + n) * 8, 8)
                    factor = jnp.exp2(decay_ref[n, pl.ds(group * 8, 8), :] * LOG2E * gated)
                    held = factor * hidden[n]
                    hidden[n] = held + drive * in_ref[pos * states + n]
                    factor_t[slot, :] = factor
                    held_t[slot, :] = held
                    if group == 0:
                        read_t[slot, :] = grad * hidden[n]
                    else:
                        read_t[slot, :] += grad * hidden[n]
            return tuple(hidden)

        lax.fori_loop(
            0, chunk // 8, replay,
            tuple(marks_ref[0, n, pl.ds(group * 8, 8), :] for n in range(states)),
        )

        def back(turn, carried):
            carry, d_decay = list(carried[0]), list(carried[1])
            block = chunk // 8 - 1 - turn
            for r in range(7, -1, -1):
                local = block * 8 + r
                pos = (last - index) * chunk + local
                view = pl.ds(block * 64 + r, 8, stride=8)
                rate = rate_t[view, :]
                act = act_t[view, :]
                grad = grad_t[view, :]
                drive = rate * act
                inner_terms = []
                step_terms = []
                for n in range(states):
                    slot = pl.ds((local * states + n) * 8, 8)
                    adjoint = carry[n] + grad * read_ref[pos * states + n]
                    moved = adjoint * held_t[slot, :]
                    step_terms.append(moved * decay_ref[n, pl.ds(group * 8, 8), :])
                    d_decay[n] = d_decay[n] + moved * rate
                    inner_terms.append(adjoint * in_ref[pos * states + n])
                    if group == 0:
                        in_t[slot, :] = adjoint * drive
                    else:
                        in_t[slot, :] += adjoint * drive
                    carry[n] = adjoint * factor_t[slot, :]
                inner_sum = tree_sum(inner_terms)
                d_step_t[view, :] = tree_sum(step_terms) + act * inner_sum
                d_act_t[view, :] = rate * inner_sum
            return (tuple(carry), tuple(d_decay))

        carry, d_decay = lax.fori_loop(
            0, chunk // 8, back,
            (
                tuple(carry_ref[n, pl.ds(group * 8, 8), :] for n in range(states)),
                tuple(d_decay_ref[n, pl.ds(group * 8, 8), :] for n in range(states)),
            ),
        )
        for n in range(states):
            carry_ref[n, pl.ds(group * 8, 8), :] = carry[n]
            d_decay_ref[n, pl.ds(group * 8, 8), :] = d_decay[n]
        for block in range(chunk // 8):
            for lane_block in range(8):
                where = (pl.ds(block * 8, 8), pl.ds(group * 1024 + lane_block * LANES, LANES))
                tile = pl.ds(block * 64 + lane_block * 8, 8)
                d_step_ref[where] = d_step_t[tile, :]
                d_act_ref[where] = d_act_t[tile, :]

    def shrink(block, _):
        for source, target in ((in_t, d_in_ref), (read_t, d_read_ref)):
            total = source[pl.ds(block * 64, 8, stride=8), :]
            for s in range(1, 8):
                total = total + source[pl.ds(block * 64 + s, 8, stride=8), :]
            target[pl.ds(block * 8, 8), :] = total
        return 0

    lax.fori_loop(0, chunk * states // 8, shrink, 0, unroll=4)


def adjoint_full(end_grad, marks, step, act, grad, keep_lanes, in_flat, read_flat, decay):
    rows, inner = step.shape
    states, planes, _ = decay.shape
    chunk = CHUNK
    count = rows // chunk
    whole = pl.BlockSpec((states, planes, LANES), lambda i: (0, 0, 0))
    rowed = pl.BlockSpec((chunk, inner), lambda i: (count - 1 - i, 0))
    maps = pl.BlockSpec((chunk * states, LANES), lambda i: (count - 1 - i, 0))
    big = pltpu.VMEM((chunk * states * 8, LANES), jnp.float32)
    return pl.pallas_call(
        functools.partial(adjoint_full_kernel, states, chunk),
        out_shape=(
            jax.ShapeDtypeStruct((rows, inner), jnp.float32),
            jax.ShapeDtypeStruct((rows, inner), jnp.float32),
            jax.ShapeDtypeStruct((rows * states, LANES), jnp.float32),
            jax.ShapeDtypeStruct((rows * states, LANES), jnp.float32),
            jax.ShapeDtypeStruct(decay.shape, jnp.float32),
        ),
        grid=(count,),
        in_specs=[
            whole,
            pl.BlockSpec((1, states, planes, LANES), lambda i: (count - 1 - i, 0, 0, 0)),
            rowed, rowed, rowed,
            pl.BlockSpec((chunk, LANES), lambda i: (count - 1 - i, 0)),
            smem(), smem(), whole,
        ],
        out_specs=(rowed, rowed, maps, maps, whole),
        scratch_shapes=[pltpu.VMEM(decay.shape, jnp.float32)]
        + [pltpu.VMEM((chunk * 8, LANES), jnp.float32)] * 6
        + [big] * 4,
        compiler_params=pltpu.CompilerParams(vmem_limit_bytes=48 << 20),
        name="adjoint_full",
    )(end_grad, marks, step, act, grad, keep_lanes, in_flat, read_flat, decay)


KEYS = 512


def turn_half(values):
    return pltpu.roll(values, HEAD_DIM // 2, 1)


def project_kernel(rotated, ctx_ref, weight_ref, cos_ref, sin_ref, out_ref):
    cosine, sine = cos_ref[...], sin_ref[...]
    ctx = ctx_ref[...]
    step = 3 * HEAD_DIM
    for start in range(0, weight_ref.shape[1], step):
        triple = product(ctx, weight_ref[:, start : start + step])
        for head in range(0, step, HEAD_DIM):
            part = triple[:, head : head + HEAD_DIM]
            if start + head < rotated:
                part = part * cosine + turn_half(part) * sine
            out_ref[:, start + head : start + head + HEAD_DIM] = part.astype(jnp.bfloat16)


def project_heads(ctx, weight, cosine, sine, rotated):
    length, width = ctx.shape
    columns = weight.shape[1]
    rows = min(256, length)
    return pl.pallas_call(
        functools.partial(project_kernel, rotated),
        out_shape=jax.ShapeDtypeStruct((length, columns), jnp.bfloat16),
        grid=(length // rows,),
        in_specs=[
            pl.BlockSpec((rows, width), lambda i: (i, 0)),
            pl.BlockSpec((width, columns), lambda i: (0, 0)),
            pl.BlockSpec((rows, HEAD_DIM), lambda i: (i, 0)),
            pl.BlockSpec((rows, HEAD_DIM), lambda i: (i, 0)),
        ],
        out_specs=pl.BlockSpec((rows, columns), lambda i: (i, 0)),
        compiler_params=pltpu.CompilerParams(vmem_limit_bytes=40 << 20),
        cost_estimate=pl.CostEstimate(
            flops=2 * length * width * columns, bytes_accessed=2 * (length * width + width * columns), transcendentals=0
        ),
        name="project_heads",
    )(ctx, weight, cosine, sine)


def mask_keys(scores_shape, chunk, first_key, q_pos):
    key_pos = chunk * KEYS + lax.broadcasted_iota(jnp.int32, scores_shape, 1)
    return (key_pos >= first_key) & (key_pos <= q_pos)


def attend_kernel(
    n_x, heads, scale, x_ref, low_ref, q_ref, k_ref, v_ref, first_ref, out_ref, lse_ref, score_t
):
    block = pl.program_id(1)
    rows = q_ref.shape[0]
    base = (block * n_x + x_ref[0]) * rows
    low_chunk = low_ref[block] // KEYS
    high_chunk = (base + rows - 1) // KEYS + 1
    q_pos = base + lax.broadcasted_iota(jnp.int32, (rows, KEYS), 0)
    first_key = first_ref[...]
    query = q_ref[...]

    def scores_of(chunk, top):
        where = pl.ds(pl.multiple_of(chunk * KEYS, KEYS), KEYS)
        scores = right_trans(query, k_ref[where, :]) * scale
        scores = jnp.where(mask_keys(scores.shape, chunk, first_key, q_pos), scores, -1e30)
        score_t[:, where] = scores
        for part in range(0, KEYS, LANES):
            top = jnp.maximum(top, scores[:, part : part + LANES])
        return top

    top = lax.fori_loop(low_chunk, high_chunk, scores_of, jnp.full((rows, LANES), -1e30, jnp.float32))
    top = jnp.max(top, axis=1, keepdims=True)

    def weigh(chunk, carried):
        total, mixed = carried
        where = pl.ds(pl.multiple_of(chunk * KEYS, KEYS), KEYS)
        weights = jnp.exp2(score_t[:, where] - top)
        for part in range(0, KEYS, LANES):
            total = total + weights[:, part : part + LANES]
        return (total, mixed + product(weights.astype(jnp.bfloat16), v_ref[where, :]))

    total, mixed = lax.fori_loop(
        low_chunk,
        high_chunk,
        weigh,
        (jnp.zeros((rows, LANES), jnp.float32), jnp.zeros((rows, HEAD_DIM), jnp.float32)),
    )
    total = jnp.sum(total, axis=1, keepdims=True)
    out_ref[...] = (mixed / total).astype(jnp.bfloat16)
    lse_ref[0] = top + jnp.log2(total)


def attend(x_index, lows, triple, first_key, n_x, heads, rows):
    length = triple.shape[0]
    blocks = length // (rows * n_x)
    scale = HEAD_DIM ** (-0.5) * LOG2E
    return pl.pallas_call(
        functools.partial(attend_kernel, n_x, heads, scale),
        out_shape=(
            jax.ShapeDtypeStruct((blocks * rows, heads * HEAD_DIM), jnp.bfloat16),
            jax.ShapeDtypeStruct((heads, blocks * rows, 1), jnp.float32),
        ),
        grid_spec=pltpu.PrefetchScalarGridSpec(
            num_scalar_prefetch=2,
            grid=(heads, blocks),
            in_specs=[
                pl.BlockSpec((rows, HEAD_DIM), lambda h, b, x, low: (b * n_x + x[0], h)),
                pl.BlockSpec((length, HEAD_DIM), lambda h, b, x, low: (0, heads + h)),
                pl.BlockSpec((length, HEAD_DIM), lambda h, b, x, low: (0, 2 * heads + h)),
                pl.BlockSpec((rows, 1), lambda h, b, x, low: (b, 0)),
            ],
            out_specs=(
                pl.BlockSpec((rows, HEAD_DIM), lambda h, b, x, low: (b, h)),
                pl.BlockSpec((1, rows, 1), lambda h, b, x, low: (h, b, 0)),
            ),
            scratch_shapes=[pltpu.VMEM((rows, length), jnp.float32)],
        ),
        compiler_params=pltpu.CompilerParams(vmem_limit_bytes=40 << 20),
        cost_estimate=pl.CostEstimate(
            flops=2 * heads * blocks * rows * length * HEAD_DIM, bytes_accessed=4 * length * heads * HEAD_DIM, transcendentals=0
        ),
        name="attend",
    )(x_index, lows, triple, triple, triple, first_key)


def attend_back_kernel(
    n_x, heads, scale,
    x_ref, low_ref, q_ref, k_ref, v_ref, out_ref, d_ref, lse_ref, first_ref, cos_ref, sin_ref, cos_all, sin_all,
    dq_ref, dk_ref, dv_ref, dk_t, dv_t,
):
    block = pl.program_id(1)
    rows = q_ref.shape[0]
    base = (block * n_x + x_ref[0]) * rows
    low_chunk = low_ref[block] // KEYS
    high_chunk = (base + rows - 1) // KEYS + 1
    q_pos = base + lax.broadcasted_iota(jnp.int32, (rows, KEYS), 0)
    first_key = first_ref[...]
    query = q_ref[...]
    d_out = d_ref[...]
    log_total = lse_ref[0]
    center = jnp.sum(d_out.astype(jnp.float32) * out_ref[...].astype(jnp.float32), axis=1, keepdims=True)

    @pl.when(block == 0)
    def _():
        dk_t[...] = jnp.zeros_like(dk_t)
        dv_t[...] = jnp.zeros_like(dv_t)

    def one(chunk, d_query):
        where = pl.ds(pl.multiple_of(chunk * KEYS, KEYS), KEYS)
        keys = k_ref[where, :]
        scores = right_trans(query, keys) * scale
        allowed = mask_keys(scores.shape, chunk, first_key, q_pos)
        weights = jnp.where(allowed, jnp.exp2(scores - log_total), 0.0)
        d_soft = right_trans(d_out, v_ref[where, :])
        d_scores = (weights * (d_soft - center)).astype(jnp.bfloat16)
        dv_t[where, :] += left_trans(weights.astype(jnp.bfloat16), d_out)
        dk_t[where, :] += left_trans(d_scores, query)
        return d_query + product(d_scores, keys)

    d_query = lax.fori_loop(low_chunk, high_chunk, one, jnp.zeros((rows, HEAD_DIM), jnp.float32))
    inv_scale = HEAD_DIM ** (-0.5)
    d_query = d_query * inv_scale
    dq_ref[...] = (d_query * cos_ref[...] - turn_half(d_query) * sin_ref[...]).astype(jnp.bfloat16)

    @pl.when(block == pl.num_programs(1) - 1)
    def _():
        def finish(chunk, _):
            where = pl.ds(pl.multiple_of(chunk * KEYS, KEYS), KEYS)
            d_keys = dk_t[where, :] * inv_scale
            dk_ref[where, :] = (d_keys * cos_all[where, :] - turn_half(d_keys) * sin_all[where, :]).astype(jnp.bfloat16)
            dv_ref[where, :] = dv_t[where, :].astype(jnp.bfloat16)
            return 0

        lax.fori_loop(0, k_ref.shape[0] // KEYS, finish, 0)


def attend_back(x_index, lows, triple, attended, d_attended, lse, first_key, cosine, sine, n_x, heads, rows):
    length = triple.shape[0]
    blocks = length // (rows * n_x)
    scale = HEAD_DIM ** (-0.5) * LOG2E
    q_spec = pl.BlockSpec((rows, HEAD_DIM), lambda h, b, x, low: (b * n_x + x[0], h))
    own = pl.BlockSpec((rows, HEAD_DIM), lambda h, b, x, low: (b, h))
    table_q = pl.BlockSpec((rows, HEAD_DIM), lambda h, b, x, low: (b * n_x + x[0], 0))
    table = pl.BlockSpec((length, HEAD_DIM), lambda h, b, x, low: (0, 0))
    column = pl.BlockSpec((length, HEAD_DIM), lambda h, b, x, low: (0, h))
    return pl.pallas_call(
        functools.partial(attend_back_kernel, n_x, heads, scale),
        out_shape=(
            jax.ShapeDtypeStruct((blocks * rows, heads * HEAD_DIM), jnp.bfloat16),
            jax.ShapeDtypeStruct((length, heads * HEAD_DIM), jnp.bfloat16),
            jax.ShapeDtypeStruct((length, heads * HEAD_DIM), jnp.bfloat16),
        ),
        grid_spec=pltpu.PrefetchScalarGridSpec(
            num_scalar_prefetch=2,
            grid=(heads, blocks),
            in_specs=[
                q_spec,
                pl.BlockSpec((length, HEAD_DIM), lambda h, b, x, low: (0, heads + h)),
                pl.BlockSpec((length, HEAD_DIM), lambda h, b, x, low: (0, 2 * heads + h)),
                own,
                own,
                pl.BlockSpec((1, rows, 1), lambda h, b, x, low: (h, b, 0)),
                pl.BlockSpec((rows, 1), lambda h, b, x, low: (b, 0)),
                table_q,
                table_q,
                table,
                table,
            ],
            out_specs=(own, column, column),
            scratch_shapes=[pltpu.VMEM((length, HEAD_DIM), jnp.float32)] * 2,
        ),
        compiler_params=pltpu.CompilerParams(vmem_limit_bytes=40 << 20),
        cost_estimate=pl.CostEstimate(
            flops=5 * heads * blocks * rows * length * HEAD_DIM, bytes_accessed=8 * length * heads * HEAD_DIM, transcendentals=0
        ),
        name="attend_back",
    )(x_index, lows, triple, triple, triple, attended, d_attended, lse, first_key, cosine, sine, cosine, sine)


def line_groups():
    n_seq = lax.axis_size("seq")
    n_x = n_seq // GROUPS
    return [[z * n_x + x for z in range(GROUPS)] for x in range(n_x)]


def plane_groups():
    n_seq = lax.axis_size("seq")
    n_x = n_seq // GROUPS
    n_row = lax.axis_size("row")
    return [
        [r * n_seq + z * n_x + x for r in range(n_row) for x in range(n_x)] for z in range(GROUPS)
    ]


def gather_rows(block):
    return lax.all_gather(block, "row", axis=0, tiled=True)


def reduce_rows(partial):
    return lax.psum_scatter(partial, "row", scatter_dimension=0, tiled=True)


def gather_seq(block):
    return lax.all_gather(block, "seq", axis=0, tiled=True)


def reduce_seq(partial):
    return lax.psum_scatter(partial, "seq", scatter_dimension=0, tiled=True)


def weight_term(moving, whole_gathered, split_rows):
    n_row = lax.axis_size("row")
    n_seq = lax.axis_size("seq")
    rows_here = moving.shape[0]
    columns = moving.shape[1]
    owned = columns // (n_row * n_seq)
    shaped = moving.reshape(rows_here, n_row, n_seq, owned)
    spread = lax.all_to_all(shaped, "seq", split_axis=2, concat_axis=0, tiled=True).reshape(
        n_seq * rows_here, n_row, owned
    )
    if split_rows:
        return jnp.einsum("tgc,tb->gcb", spread, whole_gathered, preferred_element_type=jnp.float32)
    return jnp.einsum("ta,tgc->agc", whole_gathered, spread, preferred_element_type=jnp.float32)


def norm_apply(values, gain_row):
    factor = lax.rsqrt(jnp.mean(values * values, axis=-1, keepdims=True) + eps)
    return (values * factor * gain_row, factor)


def norm_back(values, factor, gain_row, upstream):
    normed = values * factor
    weighted = upstream * gain_row
    gain_grad = jnp.sum(upstream * normed, axis=0)
    value_grad = factor * (weighted - normed * jnp.mean(weighted * normed, axis=-1, keepdims=True))
    return (value_grad, gain_grad)


def doc_index(positions, lengths):
    ends_at = jnp.cumsum(lengths)
    return jnp.sum((positions[:, None] >= ends_at[None, :]).astype(jnp.int32), axis=1)


def first_allowed(positions, lengths):
    ends_at = jnp.cumsum(lengths)
    begins = jnp.max(jnp.where(positions[:, None] >= ends_at[None, :], ends_at[None, :], 0), axis=1)
    return jnp.maximum(begins, positions - (WINDOW - 1)).astype(jnp.int32)


def conv_masks(positions, lengths):
    own_doc = doc_index(positions, lengths)
    rows_out = []
    for tap_index in range(CONV):
        earlier = positions - (CONV - 1) + tap_index
        rows_out.append(
            ((earlier >= 0) & (doc_index(earlier, lengths) == own_doc)).astype(jnp.float32)
        )
    return jnp.stack(rows_out, axis=0)


def rotary_tables(positions):
    half_dim = HEAD_DIM // 2
    frequency = jnp.power(rope_base, -2.0 * jnp.arange(half_dim).astype(jnp.float32) / HEAD_DIM)
    angles = positions.astype(jnp.float32)[:, None] * frequency[None, :]
    cosine, sine_tab = (jnp.cos(angles), jnp.sin(angles))
    return (
        jnp.concatenate([cosine, cosine], axis=1),
        jnp.concatenate([-sine_tab, sine_tab], axis=1),
    )


def own_up_columns(up_local):
    n_row = lax.axis_size("row")
    row = lax.axis_index("row")
    depth, both = up_local.shape
    ff_dim = both // 2
    ff_row = ff_dim // n_row
    width = depth * n_row

    def slab(dest):
        odd = dest % 2
        first = lax.dynamic_slice(up_local, (0, odd * ff_dim + dest * ff_row), (depth, ff_row))
        second = lax.dynamic_slice(up_local, (0, (1 - odd) * ff_dim + dest * ff_row), (depth, ff_row))
        return jnp.concatenate([first, second], axis=1)

    whole = jnp.zeros((width, 2 * ff_row), up_local.dtype)
    for turn in range(n_row):
        other = row ^ turn
        piece = slab(other)
        if turn:
            piece = lax.ppermute(piece, "row", [(i, i ^ turn) for i in range(n_row)])
        whole = lax.dynamic_update_slice(whole, piece, (other * depth, 0))
    return whole


def mlp_forward(values, gain_row, up_own, down_own):
    odd = lax.axis_index("row") % 2 == 1
    ff_row = down_own.shape[0]
    normed, factor = norm_apply(values, gain_row)
    spread = gather_rows(normed.astype(jnp.bfloat16))
    gate_up = product(spread, up_own)
    first, second = (gate_up[:, :ff_row], gate_up[:, ff_row:])
    gate_part = jnp.where(odd, second, first)
    up_part = jnp.where(odd, first, second)
    hidden = (jax.nn.silu(gate_part) * up_part).astype(jnp.bfloat16)
    partial = product(hidden, down_own).astype(jnp.bfloat16)
    return (values + reduce_rows(partial).astype(jnp.float32), (factor, spread, gate_part, up_part, hidden))


def place_up_grad(grad):
    n_row = lax.axis_size("row")
    n_seq = lax.axis_size("seq")
    half = n_seq // 2
    pairs = []
    for r in range(n_row):
        for s in range(n_seq):
            if s // half == r % 2:
                owner = (r // 2, s)
            else:
                owner = (n_row // 2 + r // 2, (r % 2) * half + s % half)
            pairs.append((r * n_seq + s, owner[0] * n_seq + owner[1]))
    return lax.ppermute(grad, ("row", "seq"), pairs)


def mlp_backward(values, gain_row, up_own, down_own, kept, upstream, upstream_all):
    factor, spread, gate_part, up_part, hidden = kept
    odd = lax.axis_index("row") % 2 == 1
    g_down = reduce_seq(left_trans(hidden, upstream_all).astype(jnp.bfloat16)).astype(jnp.float32)
    d_hidden = right_trans(upstream_all, down_own)
    gate_sig = jax.nn.sigmoid(gate_part)
    d_gate = d_hidden * up_part * gate_sig * (1.0 + gate_part * (1.0 - gate_sig))
    d_up = d_hidden * gate_part * gate_sig
    d_gate_up = jnp.concatenate(
        [jnp.where(odd, d_up, d_gate), jnp.where(odd, d_gate, d_up)], axis=1
    ).astype(jnp.bfloat16)
    d_normed = reduce_rows(right_trans(d_gate_up, up_own).astype(jnp.bfloat16)).astype(jnp.float32)
    g_up = place_up_grad(reduce_seq(left_trans(d_gate_up, spread).astype(jnp.bfloat16)))
    d_norm, g_gain = norm_back(values, factor, gain_row, d_normed)
    return (upstream + d_norm, g_gain, g_up.astype(jnp.float32).T, g_down)


def matchings(edges, size):
    rounds = []
    left = list(range(len(edges)))
    while left:
        taken = {}

        def assign(source, seen):
            for e in left:
                if edges[e][0] == source and edges[e][1] not in seen:
                    seen.add(edges[e][1])
                    if edges[e][1] not in taken or assign(edges[taken[edges[e][1]]][0], seen):
                        taken[edges[e][1]] = e
                        return True
            return False

        for source in range(size):
            assign(source, set())
        chosen = sorted(taken.values())
        rounds.append(chosen)
        left = [e for e in left if e not in chosen]
    return rounds


def place_attn_grad(piece, width):
    n_row = lax.axis_size("row")
    n_seq = lax.axis_size("seq")
    n_x = n_seq // GROUPS
    size = n_row * n_seq
    me = lax.axis_index("row") * n_seq + lax.axis_index("seq")
    group_cols = width // GROUPS
    owned = piece.shape[0]
    unit = math.gcd(owned, group_cols)
    count = owned // unit
    edges, slots = [], []
    for r in range(n_row):
        for z in range(GROUPS):
            for x in range(n_x):
                for u in range(count):
                    local = (r * n_x + x) * owned + u * unit
                    column = (local // group_cols) * width + z * group_cols + local % group_cols
                    edges.append((r * n_seq + z * n_x + x, column // owned))
                    slots.append((u, column % owned // unit))
    result = jnp.zeros_like(piece)
    for chosen in matchings(edges, size):
        send_slot = [0] * size
        recv_slot = [0] * size
        for e in chosen:
            send_slot[edges[e][0]] = slots[e][0]
            recv_slot[edges[e][1]] = slots[e][1]
        taken = lax.dynamic_slice(
            piece, (jnp.array(send_slot, jnp.int32)[me] * unit, 0), (unit, piece.shape[1])
        )
        moved = lax.ppermute(taken, ("row", "seq"), [edges[e] for e in chosen])
        result = lax.dynamic_update_slice(
            result, moved, (jnp.array(recv_slot, jnp.int32)[me] * unit, 0)
        )
    return result


def place_out_grad(piece):
    n_row = lax.axis_size("row")
    n_seq = lax.axis_size("seq")
    n_x = n_seq // GROUPS
    pairs = []
    for r in range(n_row):
        for z in range(GROUPS):
            for x in range(n_x):
                pairs.append((r * n_seq + z * n_x + x, z * n_row * n_x + r * n_x + x))
    return lax.ppermute(piece, ("row", "seq"), pairs)


def exchange_states(through, end_state, forward):
    n_seq = lax.axis_size("seq")
    me = lax.axis_index("seq")
    both = lax.all_gather(
        jnp.stack([through, end_state]).astype(jnp.bfloat16), "seq", axis=0
    ).astype(jnp.float32)
    carried = jnp.zeros_like(end_state)
    order = range(n_seq) if forward else range(n_seq - 1, -1, -1)
    for other in order:
        used = other < me if forward else other > me
        carried = jnp.where(used, both[other, 0] * carried + both[other, 1], carried)
    return carried


def per_device(
    tokens,
    norm_gain,
    input_weight,
    conv_weight,
    conv_bias,
    select_weight,
    step_weight,
    step_bias,
    decay_log,
    skip_scale,
    output_weight,
    attn_gain,
    attn_weight,
    attn_output,
    mlp_gain,
    mlp_up_weight,
    mlp_down_weight,
    doc_lengths,
    cotangent,
):
    n_row = lax.axis_size("row")
    n_seq = lax.axis_size("seq")
    n_x = n_seq // GROUPS
    rows_here = tokens.shape[1]
    width = tokens.shape[2]
    inner_dim = skip_scale.shape[0]
    rank_dim = step_weight.shape[0]
    state_dim = decay_log.shape[1]
    head_count = HEADS // GROUPS
    group_cols = head_count * HEAD_DIM
    lengths = doc_lengths[0]
    seq_index = lax.axis_index("seq")
    z_index = seq_index // n_x
    x_index = seq_index % n_x
    positions = seq_index * rows_here + jnp.arange(rows_here, dtype=jnp.int32)
    gain_in = norm_gain.astype(jnp.float32)
    gain_attn = attn_gain.astype(jnp.float32)
    gains_mlp = mlp_gain.astype(jnp.float32)
    conv_taps = conv_weight.astype(jnp.float32)
    skip_row = skip_scale.astype(jnp.float32)
    decays = -jnp.exp(decay_log.astype(jnp.float32)).T
    decay_planes = decays.reshape(state_dim, inner_dim // LANES, LANES)
    source = tokens[0].astype(jnp.float32)
    own_doc = doc_index(positions, lengths)
    keep_flag = ((positions > 0) & (own_doc == doc_index(positions - 1, lengths))).astype(
        jnp.float32
    )
    keep_lanes = jnp.broadcast_to(keep_flag[:, None], (rows_here, LANES))
    tap_masks = conv_masks(positions, lengths)
    whole_in = lax.all_gather(input_weight, "row", axis=0, tiled=True)
    up_local, grad_start = lax.optimization_barrier((mlp_up_weight, whole_in))[0], None
    up_first = own_up_columns(up_local[0])
    up_last = own_up_columns(up_local[1])
    down_first, down_last = (mlp_down_weight[0], mlp_down_weight[1])
    normed_in, factor_in = norm_apply(source, gain_in)
    low_in = normed_in.astype(jnp.bfloat16)
    mixed_in = product(low_in, whole_in)
    conv_input = mixed_in[:, :inner_dim]
    gate_input = mixed_in[:, inner_dim:]
    halo_rows = from_behind(
        conv_input[rows_here - (CONV - 1) :].astype(jnp.bfloat16), "seq", 1
    ).astype(jnp.float32)
    padded = jnp.concatenate([halo_rows, conv_input], axis=0)
    conv_pre = conv_bias.astype(jnp.float32)
    for tap_index in range(CONV):
        conv_pre = (
            conv_pre
            + conv_taps[tap_index]
            * padded[tap_index : tap_index + rows_here]
            * tap_masks[tap_index][:, None]
        )
    activated_low = jax.nn.silu(conv_pre).astype(jnp.bfloat16)
    activated = activated_low.astype(jnp.float32)
    picked = product(activated_low, select_weight)
    step_low = picked[:, :rank_dim].astype(jnp.bfloat16)
    step_pre = product(step_low, step_weight) + step_bias
    step_size = jax.nn.softplus(step_pre)
    in_flat = picked[:, rank_dim : rank_dim + state_dim].reshape(-1)
    read_flat = picked[:, rank_dim + state_dim :].reshape(-1)
    local_end = scan_end(step_size, activated_low, keep_lanes, in_flat, decay_planes)
    through = (
        jnp.exp(decay_planes * jnp.sum(step_size, axis=0).reshape(1, -1, LANES))
        * jnp.min(keep_flag)
    )
    start_hidden = exchange_states(through, local_end, True)
    scanned, marks = scan_out(
        start_hidden, step_size, activated_low, keep_lanes, in_flat, read_flat, decay_planes
    )
    mamba_out = scanned + skip_row * activated
    gate_act = jax.nn.silu(gate_input)
    gated = (mamba_out * gate_act).astype(jnp.bfloat16)
    first_out = source + product(gated, output_weight)
    second_out, kept_first = mlp_forward(first_out, gains_mlp[0], up_first, down_first)
    normed_attn, factor_attn = norm_apply(second_out, gain_attn)
    context = gather_seq(normed_attn.astype(jnp.bfloat16))
    length = context.shape[0]
    head_weight = jnp.concatenate(
        [
            lax.dynamic_slice(
                attn_weight, (0, part * width + z_index * group_cols), (width, group_cols)
            )
            for part in range(3)
        ],
        axis=1,
    )
    output_rows = lax.dynamic_slice(attn_output, (z_index * group_cols, 0), (group_cols, width))
    cosine, sine_tab = rotary_tables(jnp.arange(length, dtype=jnp.int32))
    block_starts = (jnp.arange(GROUPS, dtype=jnp.int32) * n_x + x_index) * rows_here
    query_pos = (
        block_starts[:, None] + jnp.arange(rows_here, dtype=jnp.int32)[None, :]
    ).reshape(-1)
    first_key = first_allowed(query_pos, lengths)
    lows = jnp.min(first_key.reshape(GROUPS, rows_here), axis=1)
    x_array = x_index.reshape(1).astype(jnp.int32)
    triple = project_heads(context, head_weight, cosine, sine_tab, 2 * group_cols)
    attended, log_total = attend(
        x_array, lows, triple, first_key[:, None], n_x, head_count, rows_here
    )
    attended_own = lax.all_to_all(
        attended.reshape(GROUPS, rows_here, group_cols),
        "seq",
        split_axis=0,
        concat_axis=0,
        axis_index_groups=line_groups(),
        tiled=True,
    )
    attended_low = attended_own.transpose(1, 0, 2).reshape(rows_here, width)
    third_out = second_out + product(attended_low, attn_output)
    final_out, kept_last = mlp_forward(third_out, gains_mlp[1], up_last, down_last)
    output = final_out.astype(jnp.bfloat16)
    grad_low = cotangent[0]
    d_third, g_gain_last, g_up_last, g_down_last = mlp_backward(
        third_out,
        gains_mlp[1],
        up_last,
        down_last,
        kept_last,
        grad_low.astype(jnp.float32),
        gather_rows(grad_low),
    )
    d_third_low = d_third.astype(jnp.bfloat16)
    d_third_line = lax.all_gather(
        d_third_low, "seq", axis=0, tiled=True, axis_index_groups=line_groups()
    )
    d_attended = right_trans(d_third_line, output_rows).astype(jnp.bfloat16)
    g_attn_output = place_out_grad(
        lax.psum_scatter(
            left_trans(attended, d_third_line).astype(jnp.bfloat16),
            ("row", "seq"),
            scatter_dimension=0,
            tiled=True,
            axis_index_groups=plane_groups(),
        )
    ).astype(jnp.float32)
    d_query, d_keys, d_values = attend_back(
        x_array,
        lows,
        triple,
        attended,
        d_attended,
        log_total,
        first_key[:, None],
        cosine,
        sine_tab,
        n_x,
        head_count,
        rows_here,
    )
    own_x = (jnp.arange(n_x) == x_index)[None, :, None, None]
    d_query_full = jnp.where(
        own_x, d_query.reshape(GROUPS, 1, rows_here, group_cols), jnp.bfloat16(0)
    ).reshape(length, group_cols)
    d_triple = jnp.concatenate([d_query_full, d_keys, d_values], axis=1)
    d_attn_normed = reduce_seq(right_trans(d_triple, head_weight).astype(jnp.bfloat16))
    g_attn_weight = (
        place_attn_grad(
            lax.psum_scatter(
                left_trans(d_triple, context).astype(jnp.bfloat16),
                ("row", "seq"),
                scatter_dimension=0,
                tiled=True,
                axis_index_groups=plane_groups(),
            ),
            width,
        )
        .astype(jnp.float32)
        .T
    )
    d_attn_norm, g_attn_gain = norm_back(
        second_out, factor_attn, gain_attn, d_attn_normed.astype(jnp.float32)
    )
    d_second = d_third + d_attn_norm
    d_first, g_gain_first, g_up_first, g_down_first = mlp_backward(
        first_out,
        gains_mlp[0],
        up_first,
        down_first,
        kept_first,
        d_second,
        gather_rows(d_second.astype(jnp.bfloat16)),
    )
    d_first_low = d_first.astype(jnp.bfloat16)
    g_output_weight = weight_term(gated, gather_seq(d_first_low), True)
    d_gated = right_trans(d_first_low, output_weight)
    d_scanned = d_gated * gate_act
    gate_sig = jax.nn.sigmoid(gate_input)
    d_gate = d_gated * mamba_out * gate_sig * (1.0 + gate_input * (1.0 - gate_sig))
    g_skip_scale = jnp.sum(d_scanned * activated, axis=0)
    back_end = adjoint_end(step_size, d_scanned, keep_lanes, read_flat, decay_planes)
    end_grad = exchange_states(through, back_end, False)
    g_step, g_activated, in_lanes, read_lanes, g_decays = adjoint_full(
        end_grad, marks, step_size, activated_low, d_scanned, keep_lanes, in_flat, read_flat, decay_planes
    )
    g_input_map = jnp.sum(in_lanes.reshape(rows_here, state_dim, LANES), axis=2)
    g_read_map = jnp.sum(read_lanes.reshape(rows_here, state_dim, LANES), axis=2)
    g_decay_log = (g_decays.reshape(state_dim, inner_dim) * decays).T
    d_step_pre = g_step * jax.nn.sigmoid(step_pre)
    g_step_bias = jnp.sum(d_step_pre, axis=0)
    d_step_low = d_step_pre.astype(jnp.bfloat16)
    g_step_weight = left_trans(step_low, d_step_low)
    d_picked = jnp.concatenate(
        [right_trans(d_step_low, step_weight), g_input_map, g_read_map], axis=1
    ).astype(jnp.bfloat16)
    g_select_weight = left_trans(activated_low, d_picked)
    d_activated = d_scanned * skip_row + g_activated + right_trans(d_picked, select_weight)
    pre_sig = jax.nn.sigmoid(conv_pre)
    d_conv_pre = d_activated * pre_sig * (1.0 + conv_pre * (1.0 - pre_sig))
    g_conv_bias = jnp.sum(d_conv_pre, axis=0)
    tap_grads = []
    d_padded = jnp.zeros((rows_here + CONV - 1, inner_dim), jnp.float32)
    for tap_index in range(CONV):
        masked = d_conv_pre * tap_masks[tap_index][:, None]
        tap_grads.append(jnp.sum(masked * padded[tap_index : tap_index + rows_here], axis=0))
        d_padded = d_padded + jnp.pad(
            masked * conv_taps[tap_index], ((tap_index, CONV - 1 - tap_index), (0, 0))
        )
    g_conv_weight = jnp.stack(tap_grads, axis=0)
    back_rows = from_behind(d_padded[: CONV - 1].astype(jnp.bfloat16), "seq", -1)
    d_conv_input = d_padded[CONV - 1 :] + jnp.pad(back_rows, ((rows_here - (CONV - 1), 0), (0, 0)))
    d_mixed = jnp.concatenate([d_conv_input, d_gate], axis=1).astype(jnp.bfloat16)
    g_input_weight = weight_term(d_mixed, gather_seq(low_in), False)
    d_normed_in = right_trans(d_mixed, whole_in)
    d_source, g_norm_gain = norm_back(source, factor_in, gain_in, d_normed_in)
    tokens_grad = (d_first + d_source).astype(jnp.bfloat16)

    owners = n_row * n_seq
    small_parts = (
        g_select_weight,
        g_step_weight.T,
        g_decay_log,
        g_conv_weight.T,
        g_conv_bias[:, None],
        g_step_bias[:, None],
        g_skip_scale[:, None],
    )
    gain_parts = (g_norm_gain, g_attn_gain, g_gain_first, g_gain_last)
    packed = jnp.concatenate(
        [part.reshape(owners, -1) for part in small_parts + gain_parts], axis=1
    )
    summed = lax.psum_scatter(packed, ("row", "seq"), scatter_dimension=0, tiled=True)[0]
    small = []
    at = 0
    for part in small_parts + gain_parts:
        size = part.size // owners
        piece = summed[at : at + size]
        small.append(piece.reshape((-1,) + part.shape[1:]))
        at += size
    g_input_weight = lax.psum_scatter(
        g_input_weight.astype(jnp.bfloat16), "row", scatter_dimension=1, tiled=True
    ).astype(jnp.float32)
    g_output_weight = lax.psum_scatter(
        g_output_weight.astype(jnp.bfloat16), "row", scatter_dimension=0, tiled=True
    ).astype(jnp.float32)
    return (
        output[None],
        tokens_grad[None],
        small[7],
        g_input_weight[:, 0],
        small[3].T,
        small[4][:, 0],
        small[0],
        small[1].T,
        small[5][:, 0],
        small[2],
        small[6][:, 0],
        g_output_weight[0],
        small[8],
        g_attn_weight,
        g_attn_output,
        jnp.stack([small[9], small[10]], axis=0),
        jnp.stack([g_up_first, g_up_last], axis=0),
        jnp.stack([g_down_first, g_down_last], axis=0),
    )


def solution(mesh):
    return jax.shard_map(
        per_device,
        mesh=mesh,
        in_specs=(
            P("row", "seq", None),
            P(),
            P("row", None),
            P(),
            P(),
            P(),
            P(),
            P(),
            P(),
            P(),
            P(),
            P(),
            P(),
            P(),
            P(),
            P(None, "row", None),
            P(None, "row", None),
            P("row", None),
            P("row", "seq", None),
        ),
        out_specs=(
            P("row", "seq", None),
            P("row", "seq", None),
            P(("row", "seq")),
            P(None, ("row", "seq")),
            P(None, ("row", "seq")),
            P(("row", "seq")),
            P(("row", "seq"), None),
            P(None, ("row", "seq")),
            P(("row", "seq")),
            P(("row", "seq"), None),
            P(("row", "seq")),
            P(("row", "seq"), None),
            P(("row", "seq")),
            P(None, ("row", "seq")),
            P(("row", "seq"), None),
            P(None, ("row", "seq")),
            P(None, None, ("row", "seq")),
            P(None, ("row", "seq"), None),
        ),
        check_vma=False,
    )
```

time: 5590 us -> 2190 us (0.39)
  other arithmetic: 1840 us -> 94.4 us
  local copies, waits for them, and re-layouts: 1510 us -> 117 us
  matrix products: 420 us -> 217 us
  Pallas kernels: 0 us -> 158 us
  starting transfers between devices: 161 us -> 41.9 us
    reduce_sum x460 -> x5, other arithmetic: 892 us -> 10.5 us  [the longest x3 6.06 us: norm_back(): gain_grad = jnp.sum(upstream * normed, axis=0)]
    ppermute x30 -> x2, waiting for transfers between devices: 725 us -> 1.43 us  [from_behind(): return lax.ppermute(x, axis, pairs)]
    while x1514 -> x0, local copies, waits for them, and re-layouts: 438 us -> none
    reduce_scatter x3 -> x11, waiting for transfers between devices: 148 us -> 577 us  [the longest x5 441 us: reduce_seq(): return lax.psum_scatter(partial, 'seq', scatter_dimension=0, tiled=True)]
    slice x363 -> x11, local copies, waits for them, and re-layouts: 442 us -> 15.1 us  [the longest x6 7.29 us: per_device(): piece = summed[at:at + size]]
    while x196 -> x0, other arithmetic: 353 us -> none
    all_gather x11, waiting for transfers between devices: 116 us -> 435 us  [the longest x3 181 us: gather_seq(): return lax.all_gather(block, 'seq', axis=0, tiled=True)]
    dynamic_update_slice x332 -> x9, local copies, waits for them, and re-layouts: 320 us -> 12.1 us  [the longest x6 12 us: own_up_columns(): whole = lax.dynamic_update_slice(whole, piece, (other * depth, 0))]
where the time goes in v1:
time: 2190 us; the launch traced here: 2180 us
  waiting for transfers between devices  1500 us (68%)
  matrix products  217 us (10%)
  Pallas kernels  158 us (7%)
  local copies, waits for them, and re-layouts  117 us (5%)
  other arithmetic  94.4 us (4%)
  starting transfers between devices  41.9 us (2%)
  blocking collectives  23.3 us (1%)
    reduce_scatter x5, waiting for transfers between devices, reduce_seq(): return lax.psum_scatter(partial, 'seq', scatter_dimension=0, tiled=True)  441 us
    all_gather x3, waiting for transfers between devices, gather_seq(): return lax.all_gather(block, 'seq', axis=0, tiled=True)  181 us
    ppermute x6, waiting for transfers between devices, own_up_columns(): piece = lax.ppermute(piece, 'row', [(i, i ^ turn) for i in range(n_row)])  163 us
    unnamed x26, waiting for transfers between devices  142 us
    reduce_scatter x4, waiting for transfers between devices, reduce_rows(): return lax.psum_scatter(partial, 'row', scatter_dimension=0, tiled=True)  136 us
    all_gather x1, waiting for transfers between devices, per_device(): whole_in = lax.all_gather(input_weight, 'row', axis=0, tiled=True)  121 us
    all_to_all x2, waiting for transfers between devices, weight_term(): lax.all_to_all(shaped, 'seq', split_axis=2, concat_axis=0, tiled=True)  102 us
    dot_general x10, matrix products, right_trans(): lax.dot_general(left_op, right_op, (((1,), (1,)), ((), ())), preferred_el...  86.5 us
  transfers between devices with their start and end apart: 41, of which 28 were waited for; matrix products, arithmetic and copies ran while one was open for 12% of the time, Pallas kernels for 2%

profile of v1, /device:TPU:6, one launch (start us, length us, event | category | flops | bytes accessed | tf_op | source)
XLA Modules:
  0.0 2177.2 jit_solution(711256391394639830)
XLA Ops:
  9.2 120.8 %all-gather.13.cloned.1.call-done = bf16[1536,6144]{1,0:T(8,128)(2,1)} async-done(((bf16[384,6144]{1,0:T(8,128)(2,1)}), bf16[1536,6144]{1,0:T(8,128)(2,1)}) %all-gather.13.cloned.1.call-update) | async-done | bytes 18874384 | tf_op jit(solution)/shard_map/all_gather | solution.py:888
  176.2 42.0 %all-gather.15.cloned.1.call-done = bf16[8,2,16,24,128]{4,3,2,1,0:T(8,128)(2,1)} async-done(((bf16[1,2,16,24,128]{4,3,2,1,0:T(8,128)(2,1)}), bf16[8,2,16,24,128]{4,3,2,1,0:T(8,128)(2,1)}) %all-gather.15.cloned.1.call-update) | async-done | bytes 1572880 | tf_op jit(solution)/shard_map/all_gather | solution.py:827
  271.1 37.7 %collective-permute-done.2 = bf16[384,2048]{1,0:T(8,128)(2,1)} collective-permute-done((bf16[384,2048]{1,0:T(8,128)(2,1)}, bf16[384,2048]{1,0:T(8,128)(2,1)}, u32[]{:S(2)}, u32[]{:S(2)}) %collective-permute-start.2) | collective-permute-done | bytes 1572896 | tf_op jit(solution)/shard_map/ppermute | solution.py:702
  311.5 30.7 %collective-permute-done.3 = bf16[384,2048]{1,0:T(8,128)(2,1)} collective-permute-done((bf16[384,2048]{1,0:T(8,128)(2,1)}, bf16[384,2048]{1,0:T(8,128)(2,1)}, u32[]{:S(2)}, u32[]{:S(2)}) %collective-permute-start.3) | collective-permute-done | bytes 1572896 | tf_op jit(solution)/shard_map/ppermute | solution.py:702
  368.0 37.4 %reduce-scatter.14.cloned.1.call-done = bf16[256,1536]{1,0:T(8,128)(2,1)} async-done(((bf16[1024,1536]{1,0:T(8,128)(2,1)}), bf16[256,1536]{1,0:T(8,128)(2,1)}) %reduce-scatter.14.cloned.1.call-update) | async-done | bytes 786448 | tf_op jit(solution)/shard_map/reduce_scatter | solution.py:611
  420.4 88.0 %all-gather.19.cloned.1.call-done.ctx_ref = bf16[2048,1536]{1,0:T(8,128)(2,1)} async-done(((bf16[256,1536]{1,0:T(8,128)(2,1)}), bf16[2048,1536]{1,0:T(8,128)(2,1)}) %all-gather.19.cloned.1.call-update) | async-done | bytes 6291472 | tf_op jit(solution)/shard_map/all_gather | solution.py:615
  588.8 47.2 %collective-permute-done.5 = bf16[384,2048]{1,0:T(8,128)(2,1)S(1)} collective-permute-done((bf16[384,2048]{1,0:T(8,128)(2,1)S(1)}, bf16[384,2048]{1,0:T(8,128)(2,1)S(1)}, u32[]{:S(2)}, u32[]{:S(2)}) %collective-permute-start.5) | collective-permute-done | bytes 1572896 | tf_op jit(solution)/shard_map/ppermute | solution.py:702
  637.2 47.0 %collective-permute-done.6 = bf16[384,2048]{1,0:T(8,128)(2,1)S(1)} collective-permute-done((bf16[384,2048]{1,0:T(8,128)(2,1)S(1)}, bf16[384,2048]{1,0:T(8,128)(2,1)S(1)}, u32[]{:S(2)}, u32[]{:S(2)}) %collective-permute-start.6) | collective-permute-done | bytes 1572896 | tf_op jit(solution)/shard_map/ppermute | solution.py:702
  759.0 38.3 %reduce-scatter.16.cloned.1.call-done = bf16[256,1536]{1,0:T(8,128)(2,1)} async-done(((bf16[1024,1536]{1,0:T(8,128)(2,1)}), bf16[256,1536]{1,0:T(8,128)(2,1)}) %reduce-scatter.16.cloned.1.call-update) | async-done | bytes 786448 | tf_op jit(solution)/shard_map/reduce_scatter | solution.py:611
  801.8 64.4 %all-gather.23.cloned.1.call-done = bf16[1024,1536]{1,0:T(8,128)(2,1)} async-done(((bf16[256,1536]{1,0:T(8,128)(2,1)}), bf16[1024,1536]{1,0:T(8,128)(2,1)}) %all-gather.23.cloned.1.call-update) | async-done | bytes 3145744 | tf_op jit(solution)/shard_map/all_gather | solution.py:980
  872.8 29.5 %attend_back.1 = (bf16[1024,384]{1,0:T(8,128)(2,1)S(1)}, bf16[2048,384]{1,0:T(8,128)(2,1)S(1)}, bf16[2048,384]{1,0:T(8,128)(2,1)S(1)}) custom-call(s32[1]{0:T(128)} %bitcast.36.x_ref, s32[4]{0:T(128)S(1)} %get-tuple-element.224.low_ref, bf16[2048,1152]{1,0:T(8,128)(2,1)S(1)} %copy-done.2, bf16[2048,1152]{1,0:T(8,128)(2,1)S(1)} %copy-done.2, ...), custom_call_target="tpu_custom_call" | custom-call | flops 4026531840 | bytes 6291456 | tf_op jit(solution)/shard_map/attend_back/pallas_call | solution.py:557
  914.7 116.7 %reduce-scatter.20.cloned.1.call-done = bf16[256,1536]{1,0:T(8,128)(2,1)} async-done(((bf16[2048,1536]{1,0:T(8,128)(2,1)}), bf16[256,1536]{1,0:T(8,128)(2,1)}) %reduce-scatter.20.cloned.1.call-update) | async-done | bytes 786448 | tf_op jit(solution)/shard_map/reduce_scatter | solution.py:619
  1035.3 26.5 %all-gather.25.cloned.1.call-done = bf16[1024,1536]{1,0:T(8,128)(2,1)} async-done(((bf16[256,1536]{1,0:T(8,128)(2,1)}), bf16[1024,1536]{1,0:T(8,128)(2,1)}) %all-gather.25.cloned.1.call-update) | async-done | bytes 3145744 | tf_op jit(solution)/shard_map/all_gather | solution.py:607
  1084.8 38.1 %reduce-scatter.22.cloned.1.call-done = bf16[256,1536]{1,0:T(8,128)(2,1)} async-done(((bf16[1024,1536]{1,0:T(8,128)(2,1)}), bf16[256,1536]{1,0:T(8,128)(2,1)}) %reduce-scatter.22.cloned.1.call-update) | async-done | bytes 786448 | tf_op jit(solution)/shard_map/reduce_scatter | solution.py:611
  1201.6 48.9 %adjoint_full.1 = (f32[256,3072]{1,0:T(8,128)}, f32[256,3072]{1,0:T(8,128)}, f32[4096,128]{1,0:T(8,128)S(1)}, f32[4096,128]{1,0:T(8,128)}, f32[16,24,128]{2,1,0:T(8,128)S(1)}) custom-call(f32[16,24,128]{2,1,0:T(8,128)S(1)} %fusion.72.end_ref, f32[8,16,24,128]{3,2,1,0:T(8,128)S(1)} %copy-done.20, f32[256,3072]{1,0:T(8,128)} %copy-done.5, ...), custom_call_target="tpu_custom_call" | custom-call | tf_op jit(solution)/shard_map/adjoint_full/pallas_call | solution.py:347
  1339.7 65.8 %all-to-all-done.1 = bf16[256,4,8,192]{0,3,1,2:T(8,128)(2,1)} async-done(((bf16[256,4,8,192]{0,3,1,2:T(8,128)(2,1)}), bf16[256,4,8,192]{0,3,1,2:T(8,128)(2,1)}, u32[]{:S(2)}, u32[]{:S(2)}) %all-to-all-start.1) | async-done | bytes 3145760 | tf_op jit(solution)/shard_map/all_to_all | solution.py:629
  1442.7 36.3 %all-to-all-done.2 = bf16[256,4,8,96]{0,3,1,2:T(8,128)(2,1)S(1)} async-done(((bf16[256,4,8,96]{0,3,1,2:T(8,128)(2,1)}), bf16[256,4,8,96]{0,3,1,2:T(8,128)(2,1)S(1)}, u32[]{:S(2)}, u32[]{:S(2)}) %all-to-all-start.2) | async-done | bytes 1572896 | tf_op jit(solution)/shard_map/all_to_all | solution.py:629
  1484.8 82.7 %reduce-scatter.34.cloned.1.call-done = bf16[256,1536]{1,0:T(8,128)(2,1)} async-done(((bf16[2048,1536]{1,0:T(8,128)(2,1)}), bf16[256,1536]{1,0:T(8,128)(2,1)}) %reduce-scatter.34.cloned.1.call-update) | async-done | bytes 786448 | tf_op jit(solution)/shard_map/reduce_scatter | solution.py:619
  1577.6 26.3 %collective-permute-done.9 = bf16[48,1536]{1,0:T(8,128)(2,1)S(1)} collective-permute-done((bf16[48,1536]{1,0:T(8,128)(2,1)}, bf16[48,1536]{1,0:T(8,128)(2,1)S(1)}, u32[]{:S(2)}, u32[]{:S(2)}) %collective-permute-start.9) | collective-permute-done | bytes 147488 | tf_op jit(solution)/shard_map/ppermute | solution.py:805
  1611.0 52.5 %reduce-scatter.38.cloned.1.call-done = bf16[128,1536]{1,0:T(8,128)(2,1)} async-done(((bf16[1024,1536]{1,0:T(8,128)(2,1)}), bf16[128,1536]{1,0:T(8,128)(2,1)}) %reduce-scatter.38.cloned.1.call-update) | async-done | bytes 393232 | tf_op jit(solution)/shard_map/reduce_scatter | solution.py:619
  1663.6 77.5 %reduce-scatter.36.cloned.1.call-done = bf16[128,1536]{1,0:T(8,128)(2,1)} async-done(((bf16[1024,1536]{1,0:T(8,128)(2,1)}), bf16[128,1536]{1,0:T(8,128)(2,1)}) %reduce-scatter.36.cloned.1.call-update) | async-done | bytes 393232 | tf_op jit(solution)/shard_map/reduce_scatter | solution.py:619
  1744.9 138.8 %all-reduce.8.cloned.1.call-done = f32[32,23904]{1,0:T(8,128)} async-done(((f32[32,23904]{1,0:T(8,128)}), f32[32,23904]{1,0:T(8,128)}) %all-reduce.8.cloned.1.call-update) | async-done | bytes 3059728
  1890.2 93.5 %all-gather.31.cloned.1.call-done = bf16[2048,1536]{1,0:T(8,128)(2,1)} async-done(((bf16[256,1536]{1,0:T(8,128)(2,1)}), bf16[2048,1536]{1,0:T(8,128)(2,1)}) %all-gather.31.cloned.1.call-update) | async-done | bytes 6291472 | tf_op jit(solution)/shard_map/all_gather | solution.py:615
  1992.6 111.8 %reduce-scatter.32.cloned.1.call-done = bf16[256,1536]{1,0:T(8,128)(2,1)} async-done(((bf16[2048,1536]{1,0:T(8,128)(2,1)}), bf16[256,1536]{1,0:T(8,128)(2,1)}) %reduce-scatter.32.cloned.1.call-update) | async-done | bytes 786448 | tf_op jit(solution)/shard_map/reduce_scatter | solution.py:619
  (541 shorter events, 658.3 us)
Async XLA Ops:
  7.2 122.7 %all-gather.13.cloned.1.call-start = ((), (), s32[]{:S(2)}) async-start(), calls=%async_computation.16 | async-start | bytes 23592960 | tf_op jit(solution)/shard_map/all_gather | solution.py:888
  8.0 210.1 %all-gather.15.cloned.1.call-start = ((), (), s32[]{:S(2)}) async-start(), calls=%async_computation.17 | async-start | bytes 1769472 | tf_op jit(solution)/shard_map/all_gather | solution.py:827
  173.8 171.2 %all-gather.17.cloned.1.call-start = ((), (), s32[]{:S(2)}) async-start(), calls=%async_computation.18 | async-start | bytes 3932160 | tf_op jit(solution)/shard_map/all_gather | solution.py:607
  248.9 156.5 %reduce-scatter.14.cloned.1.call-start = ((), (), s32[]{:S(2)}) async-start(), calls=%async_computation.19 | async-start | bytes 3932160 | tf_op jit(solution)/shard_map/reduce_scatter | solution.py:611
  367.3 141.0 %all-gather.19.cloned.1.call-start = ((), (), s32[]{:S(2)}) async-start(), calls=%async_computation.20 | async-start | bytes 7077888 | tf_op jit(solution)/shard_map/all_gather | solution.py:615
  409.2 276.4 %all-gather.21.cloned.1.call-start = ((), (), s32[]{:S(2)}) async-start(), calls=%async_computation.21 | async-start | bytes 3932160 | tf_op jit(solution)/shard_map/all_gather | solution.py:607
  578.3 178.4 %reduce-scatter.18.cloned.1.call-start = ((), (), s32[]{:S(2)}) async-start(), calls=%async_computation.23 | async-start | bytes 3932160 | tf_op jit(solution)/shard_map/reduce_scatter | solution.py:611
  734.8 131.4 %all-gather.23.cloned.1.call-start = ((), (), s32[]{:S(2)}) async-start(), calls=%async_computation.24 | async-start | bytes 3932160 | tf_op jit(solution)/shard_map/all_gather | solution.py:980
  801.6 229.8 %reduce-scatter.20.cloned.1.call-start = ((), (), s32[]{:S(2)}) async-start(), calls=%async_computation.25 | async-start | bytes 7077888 | tf_op jit(solution)/shard_map/reduce_scatter | solution.py:619
  914.6 147.2 %all-gather.25.cloned.1.call-start = ((), (), s32[]{:S(2)}) async-start(), calls=%async_computation.26 | async-start | bytes 3932160 | tf_op jit(solution)/shard_map/all_gather | solution.py:607
  1154.2 262.0 %all-gather.29.cloned.1.call-start = ((), (), s32[]{:S(2)}) async-start(), calls=%async_computation.29 | async-start | bytes 7077888 | tf_op jit(solution)/shard_map/all_gather | solution.py:615
  1154.8 275.1 %reduce-scatter.30.cloned.1.call-start = ((), (), s32[]{:S(2)}) async-start(), calls=%async_computation.34 | async-start | bytes 1327104 | tf_op jit(solution)/shard_map/reduce_scatter | solution.py:985
  1159.3 275.6 %reduce-scatter.28.cloned.1.call-start = ((), (), s32[]{:S(2)}) async-start(), calls=%async_computation.33 | async-start | bytes 3981312 | tf_op jit(solution)/shard_map/reduce_scatter | solution.py:1015
  1171.9 395.6 %reduce-scatter.34.cloned.1.call-start = ((), (), s32[]{:S(2)}) async-start(), calls=%async_computation.36 | async-start | bytes 7077888 | tf_op jit(solution)/shard_map/reduce_scatter | solution.py:619
  1183.4 480.1 %reduce-scatter.38.cloned.1.call-start = ((), (), s32[]{:S(2)}) async-start(), calls=%async_computation.38 | async-start | bytes 3538944 | tf_op jit(solution)/shard_map/reduce_scatter | solution.py:619
  1191.1 549.9 %reduce-scatter.36.cloned.1.call-start = ((), (), s32[]{:S(2)}) async-start(), calls=%async_computation.37 | async-start | bytes 3538944 | tf_op jit(solution)/shard_map/reduce_scatter | solution.py:619
  1199.3 684.4 %all-reduce.8.cloned.1.call-start = ((), (), s32[]{:S(2)}) async-start(), calls=%async_computation.40 | async-start | bytes 6127616
  1308.1 675.6 %all-gather.31.cloned.1.call-start = ((), (), s32[]{:S(2)}) async-start(), calls=%async_computation.31 | async-start | bytes 7077888 | tf_op jit(solution)/shard_map/all_gather | solution.py:615
  1308.9 795.5 %reduce-scatter.32.cloned.1.call-start = ((), (), s32[]{:S(2)}) async-start(), calls=%async_computation.35 | async-start | bytes 7077888 | tf_op jit(solution)/shard_map/reduce_scatter | solution.py:619
  1409.7 732.8 %reduce-scatter.24.cloned.1.call-start = ((), (), s32[]{:S(2)}) async-start(), calls=%async_computation.30 | async-start | bytes 2949120 | tf_op jit(solution)/shard_map/reduce_scatter | solution.py:1106
  1426.0 742.7 %reduce-scatter.26.cloned.1.call-start = ((), (), s32[]{:S(2)}) async-start(), calls=%async_computation.32 | async-start | bytes 1474560 | tf_op jit(solution)/shard_map/reduce_scatter | solution.py:1109
  1429.8 139.5 %collective-permute-start.11 = (bf16[48,1536]{1,0:T(8,128)(2,1)}, bf16[48,1536]{1,0:T(8,128)(2,1)S(1)}, u32[]{:S(2)}, u32[]{:S(2)}) collective-permute-start(bf16[48,1536]{1,0:T(8,128)(2,1)} %reduce-scatter.30.cloned.1.call-done), channel_id=1, source_target_pairs={{0,0},{1,1},{2,8},{3,9},{4,16},{5,17},{6,24},{7,25},{8,2},{9,3},{1... | collective-permute-start | bytes 442376 | tf_op jit(solution)/shard_map/ppermute | solution.py:821
  1436.8 140.7 %collective-permute-start.8 = (bf16[48,1536]{1,0:T(8,128)(2,1)}, bf16[48,1536]{1,0:T(8,128)(2,1)S(1)}, u32[]{:S(2)}, u32[]{:S(2)}) collective-permute-start(bf16[48,1536]{1,0:T(8,128)(2,1)} %get-tuple-element.210), channel_id=1, source_target_pairs={{0,0},{1,1},{2,2},{3,3},{4,5},{5,6},{6,8},{7,9},{8,10},{9,11},{10,... | collective-permute-start | bytes 442376 | tf_op jit(solution)/shard_map/ppermute | solution.py:805
  1567.5 540.5 %collective-permute-start.13 = (bf16[256,1536]{1,0:T(8,128)(2,1)}, bf16[256,1536]{1,0:T(8,128)(2,1)}, u32[]{:S(2)}, u32[]{:S(2)}) collective-permute-start(bf16[256,1536]{1,0:T(8,128)(2,1)} %reduce-scatter.34.cloned.1.call-done), channel_id=1, source_target_pairs={{0,0},{1,1},{2,2},{3,3},{4,16},{5,17},{6,18},{7,19},{8,20},{9,21},... | collective-permute-start | bytes 2359304 | tf_op jit(solution)/shard_map/ppermute | solution.py:733
  (143 other events, 4584.7 us)
Sparse Core Ops, SparseCore 0:
  9.7 120.2 all-gather.12
  173.9 44.1 all-gather.14
  249.0 38.4 all-gather.16
  367.5 37.9 reduce-scatter.13
  409.3 99.0 all-gather.18
  577.7 43.6 all-gather.20
  623.1 45.5 all-gather.32
  720.6 36.0 reduce-scatter.17
  759.3 37.9 reduce-scatter.15
  801.7 64.4 all-gather.22
  914.7 116.6 reduce-scatter.19
  1035.0 26.7 all-gather.24
  1084.8 37.9 reduce-scatter.21
  1154.3 44.1 all-gather.26
  1200.6 97.8 all-gather.28
  1301.5 34.9 reduce-scatter.29
  1340.2 62.7 reduce-scatter.27
  1406.9 160.5 reduce-scatter.33
  1571.5 92.0 reduce-scatter.37
  1667.4 73.5 reduce-scatter.35
  1747.4 136.1 all-reduce.7
  1885.9 97.8 all-gather.30
  1987.3 117.0 reduce-scatter.31
  2106.8 35.6 reduce-scatter.23
  (1 shorter events, 23.3 us)

commit v2 on v1

--- a/solution.py
+++ b/solution.py
@@ -588,10 +588,534 @@
     )(x_index, lows, triple, triple, triple, attended, d_attended, lse, first_key, cosine, sine, cosine, sine)
 
 
-def line_groups():
+MESH = pl.DeviceIdType.MESH
+
+
+def greet(peers):
+    barrier = pltpu.get_barrier_semaphore()
+    for peer in peers:
+        pl.semaphore_signal(barrier, inc=1, device_id=peer, device_id_type=MESH)
+    pl.semaphore_wait(barrier, len(peers))
+
+
+def send(source, target, send_sem, recv_sem, peer):
+    return pltpu.make_async_remote_copy(
+        src_ref=source,
+        dst_ref=target,
+        send_sem=send_sem,
+        recv_sem=recv_sem,
+        device_id=peer,
+        device_id_type=MESH,
+    )
+
+
+def span(start, size):
+    return pl.ds(pl.multiple_of(start, 16), size)
+
+
+def ring_place(seq, n_x):
+    z, x = seq // n_x, lax.rem(seq, n_x)
+    side = lax.min(x, 1)
+    turn = GROUPS - 1 - z
+    odd = lax.rem(turn, 2)
+    back = GROUPS + turn * (n_x - 1) + (1 - odd) * (x - 1) + odd * (n_x - 1 - x)
+    return (1 - side) * z + side * back
+
+
+def ring_member(place, n_x):
+    side = lax.min(place // GROUPS, 1)
+    late = lax.max(place - GROUPS, 0)
+    turn = late // (n_x - 1)
+    step = lax.rem(late, n_x - 1)
+    odd = lax.rem(turn, 2)
+    x = (1 - odd) * (1 + step) + odd * (n_x - 1 - step)
+    return (1 - side) * place * n_x + side * ((GROUPS - 1 - turn) * n_x + x)
+
+
+def remote_params(collective, limit):
+    return pltpu.CompilerParams(
+        collective_id=collective, has_side_effects=True, vmem_limit_bytes=limit << 20
+    )
+
+
+def vmem():
+    return pl.BlockSpec(memory_space=pltpu.VMEM)
+
+
+def gather_rows_kernel(n_row, parts, x_ref, out_ref, send_y, recv_y, send_f, recv_f, own_sem):
+    row, seq = lax.axis_index("row"), lax.axis_index("seq")
+    y, core = row // 2, lax.rem(row, 2)
+    n_y = n_row // 2
+    rows = x_ref.shape[0]
+    piece = rows // parts
+    sibling = (y * 2 + 1 - core, seq)
+    across = [(lax.rem(y + d, n_y) * 2 + core, seq) for d in range(1, n_y)]
+    greet([sibling] + across)
+    pending = []
+    for d in range(n_y - 1):
+        for c in range(parts):
+            copy = send(
+                x_ref.at[pl.ds(c * piece, piece)],
+                out_ref.at[span(row * rows + c * piece, piece)],
+                send_y.at[d, c],
+                recv_y.at[d, c],
+                across[d],
+            )
+            copy.start()
+            pending.append(copy)
+    own = send(x_ref, out_ref.at[span(row * rows, rows)], own_sem.at[0], own_sem.at[1], sibling)
+    own.start()
+    out_ref[span(row * rows, rows), :] = x_ref[...]
+    forwards = []
+    for d in range(n_y - 1):
+        origin = lax.rem(y + n_y - 1 - d, n_y) * 2 + core
+        for c in range(parts):
+            pending[d * parts + c].wait_recv()
+            where = out_ref.at[span(origin * rows + c * piece, piece)]
+            copy = send(where, where, send_f.at[d, c], recv_f.at[d, c], sibling)
+            copy.start()
+            forwards.append(copy)
+    own.wait()
+    for copy in pending:
+        copy.wait_send()
+    for copy in forwards:
+        copy.wait()
+
+
+def gather_rows(block, collective=1):
+    n_row = lax.axis_size("row")
+    rows, width = block.shape
+    parts = 4 if rows % 64 == 0 else 1
+    n_y = n_row // 2
+    return pl.pallas_call(
+        functools.partial(gather_rows_kernel, n_row, parts),
+        out_shape=jax.ShapeDtypeStruct((n_row * rows, width), block.dtype),
+        in_specs=[vmem()],
+        out_specs=vmem(),
+        scratch_shapes=[pltpu.SemaphoreType.DMA((n_y - 1, parts))] * 4
+        + [pltpu.SemaphoreType.DMA((2,))],
+        compiler_params=remote_params(collective, 40),
+        name="gather_rows",
+    )(block)
+
+
+def reduce_rows_kernel(
+    n_row, parts, x_ref, out_ref, near, stage, far, send_c, recv_c, send_y, recv_y
+):
+    row, seq = lax.axis_index("row"), lax.axis_index("seq")
+    y, core = row // 2, lax.rem(row, 2)
+    n_y = n_row // 2
+    rows = out_ref.shape[0]
+    piece = rows // parts
+    other = 1 - core
+    sibling = (y * 2 + other, seq)
+    across = [(lax.rem(y + d, n_y) * 2 + core, seq) for d in range(1, n_y)]
+    greet([sibling] + across)
+    order = [(d + 1) % n_y for d in range(n_y)]
+    crossing = {}
+    for d in order:
+        block = lax.rem(y + d, n_y)
+        for c in range(parts):
+            copy = send(
+                x_ref.at[span((block * 2 + other) * rows + c * piece, piece)],
+                near.at[d, pl.ds(c * piece, piece)],
+                send_c.at[d, c],
+                recv_c.at[d, c],
+                sibling,
+            )
+            copy.start()
+            crossing[d, c] = copy
+    sent = {}
+    for d in order[:-1]:
+        block = lax.rem(y + d, n_y)
+        for c in range(parts):
+            crossing[d, c].wait_recv()
+            where = pl.ds(c * piece, piece)
+            total = x_ref[span((block * 2 + core) * rows + c * piece, piece), :].astype(
+                jnp.float32
+            ) + near[d, where, :].astype(jnp.float32)
+            stage[d - 1, where, :] = total.astype(stage.dtype)
+            copy = send(
+                stage.at[d - 1, where],
+                far.at[d - 1, where],
+                send_y.at[d - 1, c],
+                recv_y.at[d - 1, c],
+                across[d - 1],
+            )
+            copy.start()
+            sent[d, c] = copy
+    for c in range(parts):
+        where = pl.ds(c * piece, piece)
+        crossing[0, c].wait_recv()
+        total = x_ref[span(row * rows + c * piece, piece), :].astype(jnp.float32) + near[
+            0, where, :
+        ].astype(jnp.float32)
+        for d in order[:-1]:
+            sent[d, c].wait_recv()
+            total = total + far[d - 1, where, :].astype(jnp.float32)
+        out_ref[where, :] = total.astype(out_ref.dtype)
+    for copy in crossing.values():
+        copy.wait_send()
+    for copy in sent.values():
+        copy.wait_send()
+
+
+def reduce_rows(partial, collective=2, dtype=jnp.float32):
+    n_row = lax.axis_size("row")
+    n_y = n_row // 2
+    rows, width = partial.shape[0] // n_row, partial.shape[1]
+    parts = 4 if rows % 64 == 0 else 2 if rows % 32 == 0 else 1
+    buffer = (rows, width)
+    return pl.pallas_call(
+        functools.partial(reduce_rows_kernel, n_row, parts),
+        out_shape=jax.ShapeDtypeStruct(buffer, dtype),
+        in_specs=[vmem()],
+        out_specs=vmem(),
+        scratch_shapes=[
+            pltpu.VMEM((n_y,) + buffer, partial.dtype),
+            pltpu.VMEM((n_y - 1,) + buffer, partial.dtype),
+            pltpu.VMEM((n_y - 1,) + buffer, partial.dtype),
+        ]
+        + [pltpu.SemaphoreType.DMA((n_y, parts))] * 2
+        + [pltpu.SemaphoreType.DMA((n_y - 1, parts))] * 2,
+        compiler_params=remote_params(collective, 40),
+        name="reduce_rows",
+    )(partial)
+
+
+def ring_neighbours(n_seq):
+    n_x = n_seq // GROUPS
+    row, seq = lax.axis_index("row"), lax.axis_index("seq")
+    place = ring_place(seq, n_x)
+    after = (row, ring_member(lax.rem(place + 1, n_seq), n_x))
+    before = (row, ring_member(lax.rem(place + n_seq - 1, n_seq), n_x))
+    return row, seq, place, after, before
+
+
+def ring_gather(n_seq, parts, rows, out_ref, send_sem, recv_sem, place, after, before):
+    n_x = n_seq // GROUPS
+    half = rows // 2
+    piece = half // parts
+    sent = {}
+    for step in range(n_seq - 1):
+        for c in range(parts):
+            for way in range(2):
+                if step:
+                    sent[step - 1, c, way].wait_recv()
+                shift = n_seq - step if way == 0 else step
+                member = ring_member(lax.rem(place + shift, n_seq), n_x)
+                where = out_ref.at[span(member * rows + way * half + c * piece, piece)]
+                copy = send(
+                    where,
+                    where,
+                    send_sem.at[way, step, c],
+                    recv_sem.at[way, step, c],
+                    after if way == 0 else before,
+                )
+                copy.start()
+                sent[step, c, way] = copy
+    for c in range(parts):
+        for way in range(2):
+            sent[n_seq - 2, c, way].wait_recv()
+    for copy in sent.values():
+        copy.wait_send()
+
+
+def gather_seq_kernel(n_seq, parts, x_ref, out_ref, send_sem, recv_sem):
+    _, seq, place, after, before = ring_neighbours(n_seq)
+    rows = x_ref.shape[0]
+    greet([after, before])
+    out_ref[span(seq * rows, rows), :] = x_ref[...]
+    ring_gather(n_seq, parts, rows, out_ref, send_sem, recv_sem, place, after, before)
+
+
+def gather_seq(block, collective=3):
     n_seq = lax.axis_size("seq")
+    rows, width = block.shape
+    parts = 2 if rows % 64 == 0 else 1
+    return pl.pallas_call(
+        functools.partial(gather_seq_kernel, n_seq, parts),
+        out_shape=jax.ShapeDtypeStruct((n_seq * rows, width), block.dtype),
+        in_specs=[vmem()],
+        out_specs=vmem(),
+        scratch_shapes=[pltpu.SemaphoreType.DMA((2, n_seq - 1, parts))] * 2,
+        compiler_params=remote_params(collective, 48),
+        name="gather_seq",
+    )(block)
+
+
+def reduce_seq_kernel(n_seq, parts, x_ref, out_ref, held, send_sem, recv_sem):
     n_x = n_seq // GROUPS
-    return [[z * n_x + x for z in range(GROUPS)] for x in range(n_x)]
+    _, seq, place, after, before = ring_neighbours(n_seq)
+    rows = out_ref.shape[0]
+    half = rows // 2
+    piece = half // parts
+    greet([after, before])
+    sent = {}
+    for step in range(n_seq - 1):
+        for c in range(parts):
+            for way in range(2):
+                shift = 2 * n_seq - 1 - step if way == 0 else 1 + step
+                member = ring_member(lax.rem(place + shift, n_seq), n_x)
+                own = span(member * rows + way * half + c * piece, piece)
+                where = pl.ds(c * piece, piece)
+                if step:
+                    sent[step - 1, c, way].wait_recv()
+                    held[way, step - 1, where, :] = (
+                        held[way, step - 1, where, :].astype(jnp.float32)
+                        + x_ref[own, :].astype(jnp.float32)
+                    ).astype(held.dtype)
+                    source = held.at[way, step - 1, where]
+                else:
+                    source = x_ref.at[own]
+                copy = send(
+                    source,
+                    held.at[way, step, where],
+                    send_sem.at[way, step, c],
+                    recv_sem.at[way, step, c],
+                    after if way == 0 else before,
+                )
+                copy.start()
+                sent[step, c, way] = copy
+    for c in range(parts):
+        for way in range(2):
+            sent[n_seq - 2, c, way].wait_recv()
+            where = pl.ds(c * piece, piece)
+            start = way * half + c * piece
+            out_ref[pl.ds(start, piece), :] = (
+                held[way, n_seq - 2, where, :].astype(jnp.float32)
+                + x_ref[span(seq * rows + start, piece), :].astype(jnp.float32)
+            ).astype(out_ref.dtype)
+    for copy in sent.values():
+        copy.wait_send()
+
+
+def reduce_seq(partial, collective=4, dtype=jnp.float32):
+    n_seq = lax.axis_size("seq")
+    rows, width = partial.shape[0] // n_seq, partial.shape[1]
+    if rows % 32:
+        return lax.psum_scatter(partial, "seq", scatter_dimension=0, tiled=True).astype(dtype)
+    parts = 2 if rows % 64 == 0 else 1
+    return pl.pallas_call(
+        functools.partial(reduce_seq_kernel, n_seq, parts),
+        out_shape=jax.ShapeDtypeStruct((rows, width), dtype),
+        in_specs=[vmem()],
+        out_specs=vmem(),
+        scratch_shapes=[pltpu.VMEM((2, n_seq - 1, rows // 2, width), partial.dtype)]
+        + [pltpu.SemaphoreType.DMA((2, n_seq - 1, parts))] * 2,
+        compiler_params=remote_params(collective, 48),
+        name="reduce_seq",
+    )(partial)
+
+
+def exchange_kernel(n_seq, forward, x_ref, decay_ref, out_ref, all_ref, send_sem, recv_sem):
+    _, seq, place, after, before = ring_neighbours(n_seq)
+    rows = x_ref.shape[0]
+    states, planes, _ = decay_ref.shape
+    greet([after, before])
+    all_ref[span(seq * rows, rows), :] = x_ref[...]
+    ring_gather(n_seq, 1, rows, all_ref, send_sem, recv_sem, place, after, before)
+    out_ref[...] = jnp.zeros_like(out_ref)
+
+    def take(turn, _):
+        other = turn if forward else n_seq - 1 - turn
+        used = other < seq if forward else other > seq
+        block = all_ref[span(other * rows, rows), :].astype(jnp.float32)
+        base = states * planes
+        summed = block[base : base + planes] + block[base + planes : base + 2 * planes]
+        for n in range(states):
+            kept = jnp.exp(decay_ref[n] * summed) * out_ref[n]
+            ended = block[n * planes : (n + 1) * planes]
+            out_ref[n] = jnp.where(used, kept + ended, out_ref[n])
+        return 0
+
+    lax.fori_loop(0, n_seq, take, 0)
+
+
+def exchange_states(summed, end_state, decay, forward, collective):
+    n_seq = lax.axis_size("seq")
+    states, planes, _ = decay.shape
+    high = summed.astype(jnp.bfloat16)
+    lower = (summed - high.astype(jnp.float32)).astype(jnp.bfloat16)
+    rows = -(-(states + 2) * planes // 32) * 32
+    payload = jnp.concatenate(
+        [
+            end_state.astype(jnp.bfloat16).reshape(states * planes, LANES),
+            high,
+            lower,
+            jnp.zeros((rows - (states + 2) * planes, LANES), jnp.bfloat16),
+        ],
+        axis=0,
+    )
+    return pl.pallas_call(
+        functools.partial(exchange_kernel, n_seq, forward),
+        out_shape=jax.ShapeDtypeStruct(decay.shape, jnp.float32),
+        in_specs=[vmem(), vmem()],
+        out_specs=vmem(),
+        scratch_shapes=[pltpu.VMEM((n_seq * rows, LANES), jnp.bfloat16)]
+        + [pltpu.SemaphoreType.DMA((2, n_seq - 1, 1))] * 2,
+        compiler_params=remote_params(collective, 32),
+        name="exchange_states",
+    )(payload, decay)
+
+
+def collect_heads_kernel(n_x, x_ref, out_ref, send_sem, recv_sem):
+    row, seq = lax.axis_index("row"), lax.axis_index("seq")
+    z, x = seq // n_x, lax.rem(seq, n_x)
+    rows, cols = out_ref.shape[0], x_ref.shape[1]
+    peers = [lax.rem(z + d, GROUPS) for d in range(1, GROUPS)]
+    greet([(row, peer * n_x + x) for peer in peers])
+    mine = pl.ds(pl.multiple_of(z * cols, LANES), cols)
+    sent = []
+    for d, peer in enumerate(peers):
+        copy = send(
+            x_ref.at[span(peer * rows, rows)],
+            out_ref.at[:, mine],
+            send_sem.at[d],
+            recv_sem.at[d],
+            (row, peer * n_x + x),
+        )
+        copy.start()
+        sent.append(copy)
+    out_ref[:, mine] = x_ref[span(z * rows, rows), :]
+    for copy in sent:
+        copy.wait()
+
+
+def spread_heads_kernel(n_x, x_ref, out_ref, send_sem, recv_sem):
+    row, seq = lax.axis_index("row"), lax.axis_index("seq")
+    z, x = seq // n_x, lax.rem(seq, n_x)
+    rows, cols = x_ref.shape[0], out_ref.shape[1]
+    peers = [lax.rem(z + d, GROUPS) for d in range(1, GROUPS)]
+    greet([(row, peer * n_x + x) for peer in peers])
+    mine = span(z * rows, rows)
+    sent = []
+    for d, peer in enumerate(peers):
+        copy = send(
+            x_ref.at[:, pl.ds(pl.multiple_of(peer * cols, LANES), cols)],
+            out_ref.at[mine],
+            send_sem.at[d],
+            recv_sem.at[d],
+            (row, peer * n_x + x),
+        )
+        copy.start()
+        sent.append(copy)
+    out_ref[mine, :] = x_ref[:, pl.ds(pl.multiple_of(z * cols, LANES), cols)]
+    for copy in sent:
+        copy.wait()
+
+
+def swap_heads(values, collect, collective):
+    n_x = lax.axis_size("seq") // GROUPS
+    rows, cols = values.shape
+    shape = (rows // GROUPS, cols * GROUPS) if collect else (rows * GROUPS, cols // GROUPS)
+    return pl.pallas_call(
+        functools.partial(collect_heads_kernel if collect else spread_heads_kernel, n_x),
+        out_shape=jax.ShapeDtypeStruct(shape, values.dtype),
+        in_specs=[vmem()],
+        out_specs=vmem(),
+        scratch_shapes=[pltpu.SemaphoreType.DMA((GROUPS - 1,))] * 2,
+        compiler_params=remote_params(collective, 32),
+        name="collect_heads" if collect else "spread_heads",
+    )(values)
+
+
+def swap_seq_kernel(n_seq, x_ref, out_ref, send_sem, recv_sem):
+    row, seq = lax.axis_index("row"), lax.axis_index("seq")
+    peers = [lax.rem(seq + d, n_seq) for d in range(1, n_seq)]
+    greet([(row, peer) for peer in peers])
+    sent = []
+    for d, peer in enumerate(peers):
+        copy = send(x_ref.at[peer], out_ref.at[seq], send_sem.at[d], recv_sem.at[d], (row, peer))
+        copy.start()
+        sent.append(copy)
+    out_ref[seq] = x_ref[seq]
+    for copy in sent:
+        copy.wait()
+
+
+def swap_seq(blocks, collective):
+    n_seq = lax.axis_size("seq")
+    return pl.pallas_call(
+        functools.partial(swap_seq_kernel, n_seq),
+        out_shape=jax.ShapeDtypeStruct(blocks.shape, blocks.dtype),
+        in_specs=[vmem()],
+        out_specs=vmem(),
+        scratch_shapes=[pltpu.SemaphoreType.DMA((n_seq - 1,))] * 2,
+        compiler_params=remote_params(collective, 32),
+        name="swap_seq",
+    )(blocks)
+
+
+def gather_input_kernel(
+    parts, x_ref, out_ref, local_sem, own_sem, send_y, recv_y, send_f, recv_f, send_x, recv_x, send_g, recv_g
+):
+    row, seq = lax.axis_index("row"), lax.axis_index("seq")
+    y, core = row // 2, lax.rem(row, 2)
+    z, x = seq // 2, lax.rem(seq, 2)
+    rows = x_ref.shape[0]
+    half = rows // 2
+    piece = half // parts
+    sibling = (y * 2 + 1 - core, seq)
+    over_y = ((1 - y) * 2 + core, seq)
+    over_x = (row, z * 2 + 1 - x)
+    greet([sibling, over_y, over_x])
+    origin = (1 - y) * 2 + core
+    first = []
+    for c in range(parts):
+        copy = send(
+            x_ref.at[span(x * half + c * piece, piece)],
+            out_ref.at[span(row * rows + x * half + c * piece, piece)],
+            send_y.at[c],
+            recv_y.at[c],
+            over_y,
+        )
+        copy.start()
+        first.append(copy)
+    own = send(x_ref, out_ref.at[span(row * rows, rows)], own_sem.at[0], own_sem.at[1], sibling)
+    own.start()
+    local = pltpu.make_async_copy(x_ref, out_ref.at[span(row * rows, rows)], local_sem)
+    local.start()
+    rest = []
+    side = []
+    for c in range(parts):
+        first[c].wait_recv()
+        where = out_ref.at[span(origin * rows + x * half + c * piece, piece)]
+        copy = send(where, where, send_x.at[c], recv_x.at[c], over_x)
+        copy.start()
+        side.append(copy)
+        copy = send(where, where, send_f.at[c], recv_f.at[c], sibling)
+        copy.start()
+        rest.append(copy)
+    for c in range(parts):
+        side[c].wait_recv()
+        where = out_ref.at[span(origin * rows + (1 - x) * half + c * piece, piece)]
+        copy = send(where, where, send_g.at[c], recv_g.at[c], sibling)
+        copy.start()
+        rest.append(copy)
+    local.wait()
+    own.wait()
+    for copy in first + side:
+        copy.wait_send()
+    for copy in rest:
+        copy.wait()
+
+
+def gather_input(shard, collective):
+    n_row, n_seq = lax.axis_size("row"), lax.axis_size("seq")
+    if n_row != 4 or n_seq != 2 * GROUPS:
+        return lax.all_gather(shard, "row", axis=0, tiled=True)
+    parts = 4
+    sem = pltpu.SemaphoreType.DMA
+    return pl.pallas_call(
+        functools.partial(gather_input_kernel, parts),
+        out_shape=jax.ShapeDtypeStruct((n_row * shard.shape[0], shard.shape[1]), shard.dtype),
+        in_specs=[pl.BlockSpec(memory_space=pl.ANY)],
+        out_specs=pl.BlockSpec(memory_space=pl.ANY),
+        scratch_shapes=[sem, sem((2,))] + [sem((parts,))] * 8,
+        compiler_params=remote_params(collective, 16),
+        name="gather_input",
+    )(shard)
 
 
 def plane_groups():
@@ -603,35 +1127,59 @@
     ]
 
 
-def gather_rows(block):
-    return lax.all_gather(block, "row", axis=0, tiled=True)
-
-
-def reduce_rows(partial):
-    return lax.psum_scatter(partial, "row", scatter_dimension=0, tiled=True)
-
-
-def gather_seq(block):
-    return lax.all_gather(block, "seq", axis=0, tiled=True)
-
-
-def reduce_seq(partial):
-    return lax.psum_scatter(partial, "seq", scatter_dimension=0, tiled=True)
-
-
-def weight_term(moving, whole_gathered, split_rows):
+def swap_rows(values):
     n_row = lax.axis_size("row")
+    row = lax.axis_index("row")
+    rows, columns = values.shape
+    owned = columns // n_row
+    whole = jnp.zeros((n_row * rows, owned), values.dtype)
+    for turn in range(n_row):
+        other = row ^ turn
+        piece = lax.dynamic_slice(values, (0, other * owned), (rows, owned))
+        if turn:
+            piece = lax.ppermute(piece, "row", [(i, i ^ turn) for i in range(n_row)])
+        whole = lax.dynamic_update_slice(whole, piece, (other * rows, 0))
+    return whole
+
+
+def reduce_background(parts):
     n_seq = lax.axis_size("seq")
-    rows_here = moving.shape[0]
-    columns = moving.shape[1]
-    owned = columns // (n_row * n_seq)
-    shaped = moving.reshape(rows_here, n_row, n_seq, owned)
-    spread = lax.all_to_all(shaped, "seq", split_axis=2, concat_axis=0, tiled=True).reshape(
-        n_seq * rows_here, n_row, owned
-    )
-    if split_rows:
-        return jnp.einsum("tgc,tb->gcb", spread, whole_gathered, preferred_element_type=jnp.float32)
-    return jnp.einsum("ta,tgc->agc", whole_gathered, spread, preferred_element_type=jnp.float32)
+    shaped = [part.astype(jnp.bfloat16).reshape(n_seq, -1, part.shape[1]) for part in parts]
+    merged = jnp.concatenate(shaped, axis=1)
+    merged = merged.reshape(-1, merged.shape[2])
+    summed = lax.psum_scatter(merged, "seq", scatter_dimension=0, tiled=True)
+    pieces = []
+    at = 0
+    for part in shaped:
+        pieces.append(summed[at : at + part.shape[1]])
+        at += part.shape[1]
+    return pieces
+
+
+def owner_blocks(half):
+    n_row, n_seq = lax.axis_size("row"), lax.axis_size("seq")
+    rows, columns = half.shape
+    owned = columns // (n_row // 2 * n_seq)
+    shaped = half.reshape(rows, n_row // 2, n_seq, owned).transpose(2, 0, 1, 3)
+    return shaped.reshape(n_seq, rows, n_row // 2 * owned)
+
+
+def input_term(spread, gathered):
+    flat = spread.reshape(-1, spread.shape[2])
+    return left_trans(flat, gathered).astype(jnp.bfloat16)
+
+
+def swap_seq_async(blocks):
+    n_seq = lax.axis_size("seq")
+    seq = lax.axis_index("seq")
+    whole = jnp.zeros_like(blocks)
+    for turn in range(n_seq):
+        other = seq ^ turn
+        piece = lax.dynamic_index_in_dim(blocks, other, 0)
+        if turn:
+            piece = lax.ppermute(piece, "seq", [(i, i ^ turn) for i in range(n_seq)])
+        whole = lax.dynamic_update_slice(whole, piece, (other, 0, 0))
+    return whole
 
 
 def norm_apply(values, gain_row):
@@ -715,7 +1263,7 @@
     up_part = jnp.where(odd, first, second)
     hidden = (jax.nn.silu(gate_part) * up_part).astype(jnp.bfloat16)
     partial = product(hidden, down_own).astype(jnp.bfloat16)
-    return (values + reduce_rows(partial).astype(jnp.float32), (factor, spread, gate_part, up_part, hidden))
+    return (values + reduce_rows(partial), (factor, spread, gate_part, up_part, hidden))
 
 
 def place_up_grad(grad):
@@ -736,7 +1284,7 @@
 def mlp_backward(values, gain_row, up_own, down_own, kept, upstream, upstream_all):
     factor, spread, gate_part, up_part, hidden = kept
     odd = lax.axis_index("row") % 2 == 1
-    g_down = reduce_seq(left_trans(hidden, upstream_all).astype(jnp.bfloat16)).astype(jnp.float32)
+    g_down = left_trans(hidden, upstream_all)
     d_hidden = right_trans(upstream_all, down_own)
     gate_sig = jax.nn.sigmoid(gate_part)
     d_gate = d_hidden * up_part * gate_sig * (1.0 + gate_part * (1.0 - gate_sig))
@@ -744,10 +1292,10 @@
     d_gate_up = jnp.concatenate(
         [jnp.where(odd, d_up, d_gate), jnp.where(odd, d_gate, d_up)], axis=1
     ).astype(jnp.bfloat16)
-    d_normed = reduce_rows(right_trans(d_gate_up, up_own).astype(jnp.bfloat16)).astype(jnp.float32)
-    g_up = place_up_grad(reduce_seq(left_trans(d_gate_up, spread).astype(jnp.bfloat16)))
+    d_normed = reduce_rows(right_trans(d_gate_up, up_own).astype(jnp.bfloat16))
+    g_up = left_trans(d_gate_up, spread)
     d_norm, g_gain = norm_back(values, factor, gain_row, d_normed)
-    return (upstream + d_norm, g_gain, g_up.astype(jnp.float32).T, g_down)
+    return (upstream + d_norm, g_gain, g_up, g_down)
 
 
 def matchings(edges, size):
@@ -819,20 +1367,6 @@
             for x in range(n_x):
                 pairs.append((r * n_seq + z * n_x + x, z * n_row * n_x + r * n_x + x))
     return lax.ppermute(piece, ("row", "seq"), pairs)
-
-
-def exchange_states(through, end_state, forward):
-    n_seq = lax.axis_size("seq")
-    me = lax.axis_index("seq")
-    both = lax.all_gather(
-        jnp.stack([through, end_state]).astype(jnp.bfloat16), "seq", axis=0
-    ).astype(jnp.float32)
-    carried = jnp.zeros_like(end_state)
-    order = range(n_seq) if forward else range(n_seq - 1, -1, -1)
-    for other in order:
-        used = other < me if forward else other > me
-        carried = jnp.where(used, both[other, 0] * carried + both[other, 1], carried)
-    return carried
 
 
 def per_device(
@@ -885,13 +1419,15 @@
     )
     keep_lanes = jnp.broadcast_to(keep_flag[:, None], (rows_here, LANES))
     tap_masks = conv_masks(positions, lengths)
-    whole_in = lax.all_gather(input_weight, "row", axis=0, tiled=True)
-    up_local, grad_start = lax.optimization_barrier((mlp_up_weight, whole_in))[0], None
+    whole_in = gather_input(input_weight, 10)
+    up_local = lax.optimization_barrier((mlp_up_weight, whole_in))[0]
     up_first = own_up_columns(up_local[0])
     up_last = own_up_columns(up_local[1])
     down_first, down_last = (mlp_down_weight[0], mlp_down_weight[1])
     normed_in, factor_in = norm_apply(source, gain_in)
     low_in = normed_in.astype(jnp.bfloat16)
+    gathered_in = lax.all_gather(low_in, "seq", axis=0, tiled=True)
+    gathered_grad = lax.all_gather(cotangent[0], "row", axis=0, tiled=True)
     mixed_in = product(low_in, whole_in)
     conv_input = mixed_in[:, :inner_dim]
     gate_input = mixed_in[:, inner_dim:]
@@ -916,17 +1452,17 @@
     in_flat = picked[:, rank_dim : rank_dim + state_dim].reshape(-1)
     read_flat = picked[:, rank_dim + state_dim :].reshape(-1)
     local_end = scan_end(step_size, activated_low, keep_lanes, in_flat, decay_planes)
-    through = (
-        jnp.exp(decay_planes * jnp.sum(step_size, axis=0).reshape(1, -1, LANES))
-        * jnp.min(keep_flag)
-    )
-    start_hidden = exchange_states(through, local_end, True)
+    summed_steps = jnp.where(
+        jnp.min(keep_flag) > 0, jnp.sum(step_size, axis=0), RESET
+    ).reshape(-1, LANES)
+    start_hidden = exchange_states(summed_steps, local_end, decay_planes, True, 5)
     scanned, marks = scan_out(
         start_hidden, step_size, activated_low, keep_lanes, in_flat, read_flat, decay_planes
     )
     mamba_out = scanned + skip_row * activated
     gate_act = jax.nn.silu(gate_input)
     gated = (mamba_out * gate_act).astype(jnp.bfloat16)
+    gated_rows = swap_rows(gated)
     first_out = source + product(gated, output_weight)
     second_out, kept_first = mlp_forward(first_out, gains_mlp[0], up_first, down_first)
     normed_attn, factor_attn = norm_apply(second_out, gain_attn)
@@ -941,7 +1477,6 @@
         ],
         axis=1,
     )
-    output_rows = lax.dynamic_slice(attn_output, (z_index * group_cols, 0), (group_cols, width))
     cosine, sine_tab = rotary_tables(jnp.arange(length, dtype=jnp.int32))
     block_starts = (jnp.arange(GROUPS, dtype=jnp.int32) * n_x + x_index) * rows_here
     query_pos = (
@@ -954,15 +1489,8 @@
     attended, log_total = attend(
         x_array, lows, triple, first_key[:, None], n_x, head_count, rows_here
     )
-    attended_own = lax.all_to_all(
-        attended.reshape(GROUPS, rows_here, group_cols),
-        "seq",
-        split_axis=0,
-        concat_axis=0,
-        axis_index_groups=line_groups(),
-        tiled=True,
-    )
-    attended_low = attended_own.transpose(1, 0, 2).reshape(rows_here, width)
+    attended_low = swap_heads(attended, True, 7)
+    attended_rows = swap_rows(attended_low)
     third_out = second_out + product(attended_low, attn_output)
     final_out, kept_last = mlp_forward(third_out, gains_mlp[1], up_last, down_last)
     output = final_out.astype(jnp.bfloat16)
@@ -974,22 +1502,14 @@
         down_last,
         kept_last,
         grad_low.astype(jnp.float32),
-        gather_rows(grad_low),
+        gathered_grad,
     )
     d_third_low = d_third.astype(jnp.bfloat16)
-    d_third_line = lax.all_gather(
-        d_third_low, "seq", axis=0, tiled=True, axis_index_groups=line_groups()
-    )
-    d_attended = right_trans(d_third_line, output_rows).astype(jnp.bfloat16)
-    g_attn_output = place_out_grad(
-        lax.psum_scatter(
-            left_trans(attended, d_third_line).astype(jnp.bfloat16),
-            ("row", "seq"),
-            scatter_dimension=0,
-            tiled=True,
-            axis_index_groups=plane_groups(),
-        )
-    ).astype(jnp.float32)
+    d_third_rows = lax.all_gather(d_third_low, "row", axis=0, tiled=True)
+    d_attended = swap_heads(right_trans(d_third_low, attn_output).astype(jnp.bfloat16), False, 8)
+    up_piece, down_piece = reduce_background([g_up_last, g_down_last])
+    g_up_last = place_up_grad(up_piece).astype(jnp.float32).T
+    g_down_last = down_piece.astype(jnp.float32)
     d_query, d_keys, d_values = attend_back(
         x_array,
         lows,
@@ -1025,7 +1545,7 @@
         .T
     )
     d_attn_norm, g_attn_gain = norm_back(
-        second_out, factor_attn, gain_attn, d_attn_normed.astype(jnp.float32)
+        second_out, factor_attn, gain_attn, d_attn_normed
     )
     d_second = d_third + d_attn_norm
     d_first, g_gain_first, g_up_first, g_down_first = mlp_backward(
@@ -1038,14 +1558,28 @@
         gather_rows(d_second.astype(jnp.bfloat16)),
     )
     d_first_low = d_first.astype(jnp.bfloat16)
-    g_output_weight = weight_term(gated, gather_seq(d_first_low), True)
+    d_first_rows = gather_rows(d_first_low)
+    up_piece, down_piece, output_piece, attn_piece = reduce_background(
+        [
+            g_up_first,
+            g_down_first,
+            left_trans(gated_rows, d_first_rows),
+            left_trans(attended_rows, d_third_rows),
+        ]
+    )
+    g_up_first = place_up_grad(up_piece).astype(jnp.float32).T
+    g_down_first = down_piece.astype(jnp.float32)
+    g_output_weight = output_piece.astype(jnp.float32)
+    g_attn_output = attn_piece.astype(jnp.float32)
     d_gated = right_trans(d_first_low, output_weight)
     d_scanned = d_gated * gate_act
     gate_sig = jax.nn.sigmoid(gate_input)
     d_gate = d_gated * mamba_out * gate_sig * (1.0 + gate_input * (1.0 - gate_sig))
+    d_gate_low = d_gate.astype(jnp.bfloat16)
+    g_input_gate = input_term(swap_seq_async(owner_blocks(d_gate_low)), gathered_in)
     g_skip_scale = jnp.sum(d_scanned * activated, axis=0)
     back_end = adjoint_end(step_size, d_scanned, keep_lanes, read_flat, decay_planes)
-    end_grad = exchange_states(through, back_end, False)
+    end_grad = exchange_states(summed_steps, back_end, decay_planes, False, 6)
     g_step, g_activated, in_lanes, read_lanes, g_decays = adjoint_full(
         end_grad, marks, step_size, activated_low, d_scanned, keep_lanes, in_flat, read_flat, decay_planes
     )
@@ -1055,7 +1589,6 @@
     d_step_pre = g_step * jax.nn.sigmoid(step_pre)
     g_step_bias = jnp.sum(d_step_pre, axis=0)
     d_step_low = d_step_pre.astype(jnp.bfloat16)
-    g_step_weight = left_trans(step_low, d_step_low)
     d_picked = jnp.concatenate(
         [right_trans(d_step_low, step_weight), g_input_map, g_read_map], axis=1
     ).astype(jnp.bfloat16)
@@ -1075,45 +1608,47 @@
     g_conv_weight = jnp.stack(tap_grads, axis=0)
     back_rows = from_behind(d_padded[: CONV - 1].astype(jnp.bfloat16), "seq", -1)
     d_conv_input = d_padded[CONV - 1 :] + jnp.pad(back_rows, ((rows_here - (CONV - 1), 0), (0, 0)))
-    d_mixed = jnp.concatenate([d_conv_input, d_gate], axis=1).astype(jnp.bfloat16)
-    g_input_weight = weight_term(d_mixed, gather_seq(low_in), False)
+    d_conv_low = d_conv_input.astype(jnp.bfloat16)
+    g_input_conv = input_term(swap_seq(owner_blocks(d_conv_low), 9), gathered_in)
+    d_mixed = jnp.concatenate([d_conv_low, d_gate_low], axis=1)
     d_normed_in = right_trans(d_mixed, whole_in)
     d_source, g_norm_gain = norm_back(source, factor_in, gain_in, d_normed_in)
     tokens_grad = (d_first + d_source).astype(jnp.bfloat16)
 
     owners = n_row * n_seq
-    small_parts = (
+    g_input_weight = (
+        reduce_rows(jnp.concatenate([g_input_conv, g_input_gate], axis=0), 13).T
+    )
+    gains = jnp.stack([g_norm_gain, g_attn_gain, g_gain_first, g_gain_last], axis=0)
+    gain_cols = gains.size // inner_dim
+    columns = [
         g_select_weight,
-        g_step_weight.T,
+        left_trans(d_step_low, step_low),
         g_decay_log,
         g_conv_weight.T,
         g_conv_bias[:, None],
         g_step_bias[:, None],
         g_skip_scale[:, None],
-    )
-    gain_parts = (g_norm_gain, g_attn_gain, g_gain_first, g_gain_last)
+        gains.reshape(4, owners, -1).transpose(1, 0, 2).reshape(inner_dim, gain_cols),
+    ]
+    used = sum(part.shape[1] for part in columns)
     packed = jnp.concatenate(
-        [part.reshape(owners, -1) for part in small_parts + gain_parts], axis=1
-    )
-    summed = lax.psum_scatter(packed, ("row", "seq"), scatter_dimension=0, tiled=True)[0]
+        [part.astype(jnp.bfloat16) for part in columns]
+        + [jnp.zeros((inner_dim, -used % LANES), jnp.bfloat16)],
+        axis=1,
+    )
+    summed = reduce_seq(reduce_rows(packed, 11, jnp.bfloat16), 12)
     small = []
     at = 0
-    for part in small_parts + gain_parts:
-        size = part.size // owners
-        piece = summed[at : at + size]
-        small.append(piece.reshape((-1,) + part.shape[1:]))
-        at += size
-    g_input_weight = lax.psum_scatter(
-        g_input_weight.astype(jnp.bfloat16), "row", scatter_dimension=1, tiled=True
-    ).astype(jnp.float32)
-    g_output_weight = lax.psum_scatter(
-        g_output_weight.astype(jnp.bfloat16), "row", scatter_dimension=0, tiled=True
-    ).astype(jnp.float32)
+    for part in columns:
+        small.append(summed[:, at : at + part.shape[1]])
+        at += part.shape[1]
+    gain_sums = small[7].reshape(4, -1)
     return (
         output[None],
         tokens_grad[None],
-        small[7],
-        g_input_weight[:, 0],
+        gain_sums[0],
+        g_input_weight,
         small[3].T,
         small[4][:, 0],
         small[0],
@@ -1121,11 +1656,11 @@
         small[5][:, 0],
         small[2],
         small[6][:, 0],
-        g_output_weight[0],
-        small[8],
+        g_output_weight,
+        gain_sums[1],
         g_attn_weight,
         g_attn_output,
-        jnp.stack([small[9], small[10]], axis=0),
+        gain_sums[2:],
         jnp.stack([g_up_first, g_up_last], axis=0),
         jnp.stack([g_down_first, g_down_last], axis=0),
     )

time: 2190 us -> 1390 us (0.63)
  waiting for transfers between devices: 1500 us -> 58.9 us
  Pallas kernels: 158 us -> 795 us
  local copies, waits for them, and re-layouts: 117 us -> 156 us
  blocking collectives: 23.3 us -> 0 us
  matrix products: 217 us -> 194 us
    pallas_call x0 -> x19, Pallas kernels: none -> 636 us  [the longest x2 156 us: reduce_seq(): pl.pallas_call(functools.partial(reduce_seq_kernel, n_seq, parts), out_sh...]
    reduce_scatter x12 -> x2, waiting for transfers between devices: 608 us -> 0.04 us  [reduce_background(): summed = lax.psum_scatter(merged, 'seq', scatter_dimension=0, tiled=True)]
    all_gather x11 -> x3, waiting for transfers between devices: 435 us -> 0.02 us  [the longest x1 0.02 us: per_device(): d_third_rows = lax.all_gather(d_third_low, 'row', axis=0, tiled=True)]
    ppermute x6, waiting for transfers between devices: 163 us -> 0.02 us  [own_up_columns(): piece = lax.ppermute(piece, 'row', [(i, i ^ turn) for i in range(n_row)])]
    unnamed x26 -> x6, waiting for transfers between devices: 142 us -> 0.6 us
    all_to_all x2 -> x0, waiting for transfers between devices: 102 us -> none  [weight_term(): lax.all_to_all(shaped, 'seq', split_axis=2, concat_axis=0, tiled=True)]
    ppermute x3, waiting for transfers between devices: 32.4 us -> 6.12 us  [place_attn_grad(): moved = lax.ppermute(taken, ('row', 'seq'), [edges[e] for e in chosen])]
    ppermute x1 -> x13, waiting for transfers between devices: 0.01 us -> 24.5 us  [the longest x6 24.5 us: swap_rows(): piece = lax.ppermute(piece, 'row', [(i, i ^ turn) for i in range(n_row)])]
  transfers between devices with their start and end apart: 41 -> 32, of which waited for: 28 -> 8; matrix products, arithmetic and copies ran while one was open for 12% -> 26% of each run, Pallas kernels for 2% -> 51%
where the time goes in v2:
time: 1390 us; the launch traced here: 1380 us
  Pallas kernels  795 us (57%)
  matrix products  194 us (14%)
  local copies, waits for them, and re-layouts  156 us (11%)
  other arithmetic  97.7 us (7%)
  waiting for transfers between devices  58.9 us (4%)
  starting transfers between devices  52.2 us (4%)
  between operations  22.3 us (2%)
    pallas_call x2, Pallas kernels, reduce_seq(): pl.pallas_call(functools.partial(reduce_seq_kernel, n_seq, parts), out_sh...  156 us
    pallas_call x6, Pallas kernels, reduce_rows(): pl.pallas_call(functools.partial(reduce_rows_kernel, n_row, parts), out_s...  122 us
    dot_general x10, matrix products, right_trans(): lax.dot_general(left_op, right_op, (((1,), (1,)), ((), ())), preferred_el...  83.8 us
    pallas_call x4, Pallas kernels, gather_rows(): pl.pallas_call(functools.partial(gather_rows_kernel, n_row, parts), out_s...  82.5 us
    pallas_call x2, Pallas kernels, exchange_states(): pl.pallas_call(functools.partial(exchange_kernel, n_seq, forward), out_sh...  78.9 us
    pallas_call x1, Pallas kernels, gather_input(): pl.pallas_call(functools.partial(gather_input_kernel, parts), out_shape=j...  67.9 us
    pallas_call x1, Pallas kernels, gather_seq(): pl.pallas_call(functools.partial(gather_seq_kernel, n_seq, parts), out_sh...  64.5 us
    dot_general x11, matrix products, left_trans(): lax.dot_general(left_op, right_op, (((0,), (0,)), ((), ())), preferred_el...  58.3 us
  transfers between devices with their start and end apart: 32, of which 8 were waited for; matrix products, arithmetic and copies ran while one was open for 26% of the time, Pallas kernels for 51%

profile of v2, /device:TPU:6, one launch (start us, length us, event | category | flops | bytes accessed | tf_op | source)
XLA Modules:
  0.0 1376.1 jit_solution(9476707078624062221)
XLA Ops:
  9.8 67.9 %gather_input.1 = bf16[1536,6144]{1,0:T(8,128)(2,1)S(1)} custom-call(bf16[384,6144]{1,0:T(8,128)(2,1)S(1)} %copy-done.15), custom_call_target="tpu_custom_call" | custom-call | tf_op jit(solution)/shard_map/gather_input/pallas_call | solution.py:1110
  184.9 26.2 %exchange_states.2.refs_0_ = f32[16,24,128]{2,1,0:T(8,128)S(1)} custom-call(bf16[448,128]{1,0:T(8,128)(2,1)S(1)} %fusion.43.x_ref, f32[16,24,128]{2,1,0:T(8,128)S(1)} %copy.230.refs_4_.decay_ref.refs_6_), custom_call_target="tpu_custom_call" | custom-call | tf_op jit(solution)/shard_map/exchange_states/pallas_call | solution.py:950
  214.7 19.5 %scan_out.1 = (f32[256,3072]{1,0:T(8,128)S(1)}, f32[8,16,24,128]{3,2,1,0:T(8,128)S(1)}) custom-call(f32[16,24,128]{2,1,0:T(8,128)S(1)} %exchange_states.2.refs_0_, f32[256,3072]{1,0:T(8,128)S(1)} %copy-done.6, bf16[256,3072]{1,0:T(8,128)(2,1)S(1)} %get-tuple-element.193.refs_1_.refs_2_.act_ref, f32[256,128]{1,0:T(8,128)S(1)} %broadcast_in_dim.51.refs_2_.refs_3_.keep_ref, ...), custom_call_target="tpu_custom_call" | custom-call | tf_op jit(solution)/shard_map/scan_out/pallas_call | solution.py:155
  245.4 20.1 %gather_rows.4 = bf16[1024,1536]{1,0:T(8,128)(2,1)S(1)} custom-call(bf16[256,1536]{1,0:T(8,128)(2,1)S(1)} %multiply_convert_fusion.7.x_ref), custom_call_target="tpu_custom_call" | custom-call | tf_op jit(solution)/shard_map/gather_rows/pallas_call | solution.py:690
  289.9 29.5 %reduce_rows.6 = f32[256,1536]{1,0:T(8,128)S(1)} custom-call(bf16[1024,1536]{1,0:T(8,128)(2,1)S(1)} %convolution_convert_fusion.9.x_ref), custom_call_target="tpu_custom_call" | custom-call | tf_op jit(solution)/shard_map/reduce_rows/pallas_call | solution.py:769
  320.0 64.5 %gather_seq.1.ctx_ref = bf16[2048,1536]{1,0:T(8,128)(2,1)} custom-call(bf16[256,1536]{1,0:T(8,128)(2,1)S(1)} %multiply_convert_fusion.6.x_ref), custom_call_target="tpu_custom_call" | custom-call | tf_op jit(solution)/shard_map/gather_seq/pallas_call | solution.py:836
  396.9 20.9 %attend.1 = (bf16[1024,384]{1,0:T(8,128)(2,1)S(1)}, f32[3,1024,1]{2,1,0:T(8,128)S(1)}) custom-call(s32[1]{0:T(128)} %bitcast.22.x_ref, s32[4]{0:T(128)S(1)} %get-tuple-element.258.low_ref, bf16[2048,1152]{1,0:T(8,128)(2,1)S(1)} %project_heads.1.q_ref.k_ref.v_ref, bf16[2048,1152]{1,0:T(8,128)(2,1)S(1)} %project_heads.1.q_ref.k_ref.v_ref, ...), custom_call_target="tpu_custom_call" | custom-call | flops 1610612736 | bytes 3145728 | tf_op jit(solution)/shard_map/attend/pallas_call | solution.py:468
  417.8 16.1 %collect_heads.1 = bf16[256,1536]{1,0:T(8,128)(2,1)S(1)} custom-call(bf16[1024,384]{1,0:T(8,128)(2,1)S(1)} %get-tuple-element.33.x_ref.out_ref), custom_call_target="tpu_custom_call" | custom-call | tf_op jit(solution)/shard_map/collect_heads/pallas_call | solution.py:1012
  438.3 20.9 %gather_rows.5 = bf16[1024,1536]{1,0:T(8,128)(2,1)S(1)} custom-call(bf16[256,1536]{1,0:T(8,128)(2,1)S(1)} %multiply_convert_fusion.5.x_ref), custom_call_target="tpu_custom_call" | custom-call | tf_op jit(solution)/shard_map/gather_rows/pallas_call | solution.py:690
  497.6 21.5 %reduce_rows.8 = f32[256,1536]{1,0:T(8,128)S(1)} custom-call(bf16[1024,1536]{1,0:T(8,128)(2,1)S(1)} %convolution_convert_fusion.5.x_ref), custom_call_target="tpu_custom_call" | custom-call | tf_op jit(solution)/shard_map/reduce_rows/pallas_call | solution.py:769
  526.1 19.4 %spread_heads.1.d_ref = bf16[1024,384]{1,0:T(8,128)(2,1)S(1)} custom-call(bf16[256,1536]{1,0:T(8,128)(2,1)S(1)} %convolution_convert_fusion.16.x_ref), custom_call_target="tpu_custom_call" | custom-call | tf_op jit(solution)/shard_map/spread_heads/pallas_call | solution.py:1012
  548.0 29.5 %attend_back.1 = (bf16[1024,384]{1,0:T(8,128)(2,1)S(1)}, bf16[2048,384]{1,0:T(8,128)(2,1)S(1)}, bf16[2048,384]{1,0:T(8,128)(2,1)S(1)}) custom-call(s32[1]{0:T(128)} %bitcast.22.x_ref, s32[4]{0:T(128)S(1)} %get-tuple-element.258.low_ref, bf16[2048,1152]{1,0:T(8,128)(2,1)S(1)} %copy-done.2, bf16[2048,1152]{1,0:T(8,128)(2,1)S(1)} %copy-done.2, ...), custom_call_target="tpu_custom_call" | custom-call | flops 4026531840 | bytes 6291456 | tf_op jit(solution)/shard_map/attend_back/pallas_call | solution.py:557
  663.2 21.5 %reduce_rows.7 = f32[256,1536]{1,0:T(8,128)S(1)} custom-call(bf16[1024,1536]{1,0:T(8,128)(2,1)S(1)} %convolution_convert_fusion.8.x_ref), custom_call_target="tpu_custom_call" | custom-call | tf_op jit(solution)/shard_map/reduce_rows/pallas_call | solution.py:769
  695.1 125.6 %reduce_seq.2 = f32[256,1536]{1,0:T(8,128)S(1)} custom-call(bf16[2048,1536]{1,0:T(8,128)(2,1)} %convolution_convert_fusion.3.x_ref), custom_call_target="tpu_custom_call" | custom-call | tf_op jit(solution)/shard_map/reduce_seq/pallas_call | solution.py:899
  824.1 20.8 %gather_rows.6 = bf16[1024,1536]{1,0:T(8,128)(2,1)S(1)} custom-call(bf16[256,1536]{1,0:T(8,128)(2,1)S(1)} %get-tuple-element.182.x_ref), custom_call_target="tpu_custom_call" | custom-call | tf_op jit(solution)/shard_map/gather_rows/pallas_call | solution.py:690
  865.9 21.5 %reduce_rows.9 = f32[256,1536]{1,0:T(8,128)S(1)} custom-call(bf16[1024,1536]{1,0:T(8,128)(2,1)S(1)} %convolution_convert_fusion.4.x_ref), custom_call_target="tpu_custom_call" | custom-call | tf_op jit(solution)/shard_map/reduce_rows/pallas_call | solution.py:769
  889.5 20.7 %gather_rows.7 = bf16[1024,1536]{1,0:T(8,128)(2,1)S(1)} custom-call(bf16[256,1536]{1,0:T(8,128)(2,1)S(1)} %get-tuple-element.178.x_ref), custom_call_target="tpu_custom_call" | custom-call | tf_op jit(solution)/shard_map/gather_rows/pallas_call | solution.py:690
  978.0 13.8 %adjoint_end.1 = f32[16,24,128]{2,1,0:T(8,128)S(1)} custom-call(f32[256,3072]{1,0:T(8,128)S(1)} %copy-done.7, f32[256,3072]{1,0:T(8,128)S(1)} %copy-done.9, f32[256,128]{1,0:T(8,128)S(1)} %broadcast_in_dim.51.refs_2_.refs_3_.keep_ref, f32[4096]{0:T(1024)S(1)} %copy-done.36, f32[16,24,128]{2,1,0:T(8,128)S(1)} %copy.230.refs_4_.decay_ref.refs_6_), custom_call_target="tpu_custom_call" | custom-call | tf_op jit(solution)/shard_map/adjoint_end/pallas_call | solution.py:214
  991.9 52.7 %exchange_states.3.end_ref = f32[16,24,128]{2,1,0:T(8,128)S(1)} custom-call(bf16[448,128]{1,0:T(8,128)(2,1)S(1)} %fusion.44.x_ref, f32[16,24,128]{2,1,0:T(8,128)S(1)} %copy.230.refs_4_.decay_ref.refs_6_), custom_call_target="tpu_custom_call" | custom-call | tf_op jit(solution)/shard_map/exchange_states/pallas_call | solution.py:950
  1044.6 48.9 %adjoint_full.1 = (f32[256,3072]{1,0:T(8,128)}, f32[256,3072]{1,0:T(8,128)}, f32[4096,128]{1,0:T(8,128)S(1)}, f32[4096,128]{1,0:T(8,128)}, f32[16,24,128]{2,1,0:T(8,128)S(1)}) custom-call(f32[16,24,128]{2,1,0:T(8,128)S(1)} %exchange_states.3.end_ref, f32[8,16,24,128]{3,2,1,0:T(8,128)S(1)} %copy-done.28, ...), custom_call_target="tpu_custom_call" | custom-call | tf_op jit(solution)/shard_map/adjoint_full/pallas_call | solution.py:347
  1179.8 30.7 %reduce_seq.3 = f32[96,256]{1,0:T(8,128)S(1)} custom-call(bf16[768,256]{1,0:T(8,128)(2,1)S(1)} %reduce_rows.10.x_ref), custom_call_target="tpu_custom_call" | custom-call | tf_op jit(solution)/shard_map/reduce_seq/pallas_call | solution.py:899
  1221.4 29.3 %swap_seq.1 = bf16[8,256,384]{2,1,0:T(8,128)(2,1)S(1)} custom-call(bf16[8,256,384]{2,1,0:T(8,128)(2,1)S(1)} %copy.255.x_ref), custom_call_target="tpu_custom_call" | custom-call | tf_op jit(solution)/shard_map/swap_seq/pallas_call | solution.py:1039
  1303.9 15.9 %reduce_rows.11 = f32[192,1536]{1,0:T(8,128)S(1)} custom-call(bf16[768,1536]{1,0:T(8,128)(2,1)S(1)} %pad_maximum_fusion.11.x_ref), custom_call_target="tpu_custom_call" | custom-call | tf_op jit(solution)/shard_map/reduce_rows/pallas_call | solution.py:769
  1335.1 19.1 %collective-permute-done.25 = bf16[256,1536]{1,0:T(8,128)(2,1)S(1)} collective-permute-done((bf16[256,1536]{1,0:T(8,128)(2,1)}, bf16[256,1536]{1,0:T(8,128)(2,1)S(1)}, u32[]{:S(2)}, u32[]{:S(2)}) %collective-permute-start.25) | collective-permute-done | bytes 786464 | tf_op jit(solution)/shard_map/ppermute | solution.py:1281
  (644 shorter events, 577.4 us)
Async XLA Ops:
  7.2 468.3 %all-gather.9.cloned.1.call-start = ((), (), s32[]{:S(2)}) async-start(), calls=%async_computation.8 | async-start | bytes 3932160 | tf_op jit(solution)/shard_map/all_gather | solution.py:1430
  98.2 172.0 %collective-permute-start.3 = (bf16[384,2048]{1,0:T(8,128)(2,1)}, bf16[384,2048]{1,0:T(8,128)(2,1)}, u32[]{:S(2)}, u32[]{:S(2)}) collective-permute-start(bf16[384,2048]{1,0:T(8,128)(2,1)} %pad_maximum_fusion.16), channel_id=1, source_target_pairs={{0,24},{8,16},{16,8},{24,0},{1,25},{9,17},{17,9},{25,1},{2,26},{10... | collective-permute-start | bytes 4718600 | tf_op jit(solution)/shard_map/ppermute | solution.py:1250
  101.0 167.6 %collective-permute-start.2 = (bf16[384,2048]{1,0:T(8,128)(2,1)}, bf16[384,2048]{1,0:T(8,128)(2,1)}, u32[]{:S(2)}, u32[]{:S(2)}) collective-permute-start(bf16[384,2048]{1,0:T(8,128)(2,1)} %pad_maximum_fusion.15), channel_id=1, source_target_pairs={{0,16},{8,24},{16,0},{24,8},{1,17},{9,25},{17,1},{25,9},{2,18},{10... | collective-permute-start | bytes 4718600 | tf_op jit(solution)/shard_map/ppermute | solution.py:1250
  102.8 162.7 %collective-permute-start.1 = (bf16[384,2048]{1,0:T(8,128)(2,1)}, bf16[384,2048]{1,0:T(8,128)(2,1)}, u32[]{:S(2)}, u32[]{:S(2)}) collective-permute-start(bf16[384,2048]{1,0:T(8,128)(2,1)} %pad_maximum_fusion.14), channel_id=1, source_target_pairs={{0,8},{8,0},{16,24},{24,16},{1,9},{9,1},{17,25},{25,17},{2,10},{10... | collective-permute-start | bytes 4718600 | tf_op jit(solution)/shard_map/ppermute | solution.py:1250
  116.4 36.0 %collective-permute-start = (bf16[3,3072]{1,0:T(4,128)(2,1)S(1)}, bf16[3,3072]{1,0:T(4,128)(2,1)S(1)}, u32[]{:S(2)}, u32[]{:S(2)}) collective-permute-start(bf16[3,3072]{1,0:T(4,128)(2,1)S(1)} %slice.306), channel_id=1, source_target_pairs={{0,1},{1,2},{2,3},{3,4},{4,5},{5,6},{6,7},{8,9},{9,10},{10,11},{11... | collective-permute-start | bytes 55304 | tf_op jit(solution)/shard_map/ppermute | solution.py:27
  122.3 337.0 %collective-permute-start.4 = (bf16[384,2048]{1,0:T(8,128)(2,1)}, bf16[384,2048]{1,0:T(8,128)(2,1)}, u32[]{:S(2)}, u32[]{:S(2)}) collective-permute-start(bf16[384,2048]{1,0:T(8,128)(2,1)} %pad_maximum_fusion.17), channel_id=1, source_target_pairs={{0,8},{8,0},{16,24},{24,16},{1,9},{9,1},{17,25},{25,17},{2,10},{10... | collective-permute-start | bytes 4718600 | tf_op jit(solution)/shard_map/ppermute | solution.py:1250
  122.5 807.7 %all-gather.7.cloned.1.call-start = ((), (), s32[]{:S(2)}) async-start(), calls=%async_computation.4 | async-start | bytes 3932160 | tf_op jit(solution)/shard_map/all_gather | solution.py:1508
  152.4 309.6 %collective-permute-start.5 = (bf16[384,2048]{1,0:T(8,128)(2,1)}, bf16[384,2048]{1,0:T(8,128)(2,1)}, u32[]{:S(2)}, u32[]{:S(2)}) collective-permute-start(bf16[384,2048]{1,0:T(8,128)(2,1)} %pad_maximum_fusion.18), channel_id=1, source_target_pairs={{0,16},{8,24},{16,0},{24,8},{1,17},{9,25},{17,1},{25,9},{2,18},{10... | collective-permute-start | bytes 4718600 | tf_op jit(solution)/shard_map/ppermute | solution.py:1250
  265.5 198.2 %collective-permute-start.6 = (bf16[384,2048]{1,0:T(8,128)(2,1)S(1)}, bf16[384,2048]{1,0:T(8,128)(2,1)S(1)}, u32[]{:S(2)}, u32[]{:S(2)}) collective-permute-start(bf16[384,2048]{1,0:T(8,128)(2,1)S(1)} %copy-done.93), channel_id=1, source_target_pairs={{0,24},{8,16},{16,8},{24,0},{1,25},{9,17},{17,9},{25,1},{2,26},{10... | collective-permute-start | bytes 4718600 | tf_op jit(solution)/shard_map/ppermute | solution.py:1250
  521.6 751.1 %reduce-scatter.6.cloned.1.call-start = ((), (), s32[]{:S(2)}) async-start(), calls=%async_computation.6 | async-start | bytes 3981312 | tf_op jit(solution)/shard_map/reduce_scatter | solution.py:1535
  590.8 704.3 %all-gather.5.cloned.1.call-start = ((), (), s32[]{:S(2)}) async-start(), calls=%async_computation.3 | async-start | bytes 7077888 | tf_op jit(solution)/shard_map/all_gather | solution.py:1429
  591.4 728.5 %reduce-scatter.8.cloned.1.call-start = ((), (), s32[]{:S(2)}) async-start(), calls=%async_computation.7 | async-start | bytes 10616832 | tf_op jit(solution)/shard_map/reduce_scatter | solution.py:1150
  613.8 711.5 %reduce-scatter.4.cloned.1.call-start = ((), (), s32[]{:S(2)}) async-start(), calls=%async_computation.5 | async-start | bytes 14598144 | tf_op jit(solution)/shard_map/reduce_scatter | solution.py:1150
  618.6 27.9 %collective-permute-start.17 = (bf16[256,768]{1,0:T(8,128)(2,1)}, bf16[256,768]{1,0:T(8,128)(2,1)}, u32[]{:S(2)}, u32[]{:S(2)}) collective-permute-start(bf16[256,768]{1,0:T(8,128)(2,1)} %get-tuple-element.223), channel_id=1, source_target_pairs={{0,24},{8,16},{16,8},{24,0},{1,25},{9,17},{17,9},{25,1},{2,26},{10... | collective-permute-start | bytes 1179656 | tf_op jit(solution)/shard_map/ppermute | solution.py:1140
  623.7 26.3 %collective-permute-start.18 = (bf16[256,384]{1,0:T(8,128)(2,1)S(1)}, bf16[256,384]{1,0:T(8,128)(2,1)S(1)}, u32[]{:S(2)}, u32[]{:S(2)}) collective-permute-start(bf16[256,384]{1,0:T(8,128)(2,1)S(1)} %get-tuple-element.238), channel_id=1, source_target_pairs={{0,8},{8,0},{16,24},{24,16},{1,9},{9,1},{17,25},{25,17},{2,10},{10... | collective-permute-start | bytes 589832 | tf_op jit(solution)/shard_map/ppermute | solution.py:1140
  969.2 244.7 %collective-permute-start.8 = (bf16[1,256,384]{1,2,0:T(8,128)(2,1)}, bf16[1,256,384]{1,2,0:T(8,128)(2,1)}, u32[]{:S(2)}, u32[]{:S(2)}) collective-permute-start(bf16[1,256,384]{1,2,0:T(8,128)(2,1)} %get-tuple-element.233), channel_id=1, source_target_pairs={{0,1},{1,0},{2,3},{3,2},{4,5},{5,4},{6,7},{7,6},{8,9},{9,8},{10,11... | collective-permute-start | bytes 589832 | tf_op jit(solution)/shard_map/ppermute | solution.py:1180
  971.4 286.2 %collective-permute-start.9 = (bf16[1,256,384]{1,2,0:T(8,128)(2,1)}, bf16[1,256,384]{1,2,0:T(8,128)(2,1)}, u32[]{:S(2)}, u32[]{:S(2)}) collective-permute-start(bf16[1,256,384]{1,2,0:T(8,128)(2,1)} %get-tuple-element.232), channel_id=1, source_target_pairs={{0,2},{1,3},{2,0},{3,1},{4,6},{5,7},{6,4},{7,5},{8,10},{9,11},{10,... | collective-permute-start | bytes 589832 | tf_op jit(solution)/shard_map/ppermute | solution.py:1180
  973.6 293.1 %collective-permute-start.10 = (bf16[1,256,384]{1,2,0:T(8,128)(2,1)}, bf16[1,256,384]{1,2,0:T(8,128)(2,1)}, u32[]{:S(2)}, u32[]{:S(2)}) collective-permute-start(bf16[1,256,384]{1,2,0:T(8,128)(2,1)} %get-tuple-element.231), channel_id=1, source_target_pairs={{0,3},{1,2},{2,1},{3,0},{4,7},{5,6},{6,5},{7,4},{8,11},{9,10},{10,... | collective-permute-start | bytes 589832 | tf_op jit(solution)/shard_map/ppermute | solution.py:1180
  973.6 294.2 %collective-permute-start.11 = (bf16[1,256,384]{1,2,0:T(8,128)(2,1)}, bf16[1,256,384]{1,2,0:T(8,128)(2,1)}, u32[]{:S(2)}, u32[]{:S(2)}) collective-permute-start(bf16[1,256,384]{1,2,0:T(8,128)(2,1)} %get-tuple-element.230), channel_id=1, source_target_pairs={{0,4},{1,5},{2,6},{3,7},{4,0},{5,1},{6,2},{7,3},{8,12},{9,13},{10,... | collective-permute-start | bytes 589832 | tf_op jit(solution)/shard_map/ppermute | solution.py:1180
  1143.0 125.9 %collective-permute-start.12 = (bf16[1,256,384]{1,2,0:T(8,128)(2,1)}, bf16[1,256,384]{1,2,0:T(8,128)(2,1)S(1)}, u32[]{:S(2)}, u32[]{:S(2)}) collective-permute-start(bf16[1,256,384]{1,2,0:T(8,128)(2,1)} %get-tuple-element.229), channel_id=1, source_target_pairs={{0,5},{1,4},{2,7},{3,6},{4,1},{5,0},{6,3},{7,2},{8,13},{9,12},{10,... | collective-permute-start | bytes 589832 | tf_op jit(solution)/shard_map/ppermute | solution.py:1180
  1213.9 55.1 %collective-permute-start.13 = (bf16[1,256,384]{1,2,0:T(8,128)(2,1)S(1)}, bf16[1,256,384]{1,2,0:T(8,128)(2,1)S(1)}, u32[]{:S(2)}, u32[]{:S(2)}) collective-permute-start(bf16[1,256,384]{1,2,0:T(8,128)(2,1)S(1)} %copy-done.103), channel_id=1, source_target_pairs={{0,6},{1,7},{2,4},{3,5},{4,2},{5,3},{6,0},{7,1},{8,14},{9,15},{10,... | collective-permute-start | bytes 589832 | tf_op jit(solution)/shard_map/ppermute | solution.py:1180
  1257.6 19.4 %collective-permute-start.14 = (bf16[1,256,384]{1,2,0:T(8,128)(2,1)S(1)}, bf16[1,256,384]{1,2,0:T(8,128)(2,1)S(1)}, u32[]{:S(2)}, u32[]{:S(2)}) collective-permute-start(bf16[1,256,384]{1,2,0:T(8,128)(2,1)S(1)} %copy-done.102), channel_id=1, source_target_pairs={{0,7},{1,6},{2,5},{3,4},{4,3},{5,2},{6,1},{7,0},{8,15},{9,14},{10,... | collective-permute-start | bytes 589832 | tf_op jit(solution)/shard_map/ppermute | solution.py:1180
  1321.9 32.2 %collective-permute-start.25 = (bf16[256,1536]{1,0:T(8,128)(2,1)}, bf16[256,1536]{1,0:T(8,128)(2,1)S(1)}, u32[]{:S(2)}, u32[]{:S(2)}) collective-permute-start(bf16[256,1536]{1,0:T(8,128)(2,1)} %slice.212), channel_id=1, source_target_pairs={{0,0},{1,1},{2,2},{3,3},{4,16},{5,17},{6,18},{7,19},{8,20},{9,21},... | collective-permute-start | bytes 2359304 | tf_op jit(solution)/shard_map/ppermute | solution.py:1281
  1326.5 36.1 %collective-permute-start.24 = (bf16[256,1536]{1,0:T(8,128)(2,1)S(1)}, bf16[256,1536]{1,0:T(8,128)(2,1)S(1)}, u32[]{:S(2)}, u32[]{:S(2)}) collective-permute-start(bf16[256,1536]{1,0:T(8,128)(2,1)S(1)} %slice.211), channel_id=1, source_target_pairs={{0,0},{1,1},{2,2},{3,3},{4,16},{5,17},{6,18},{7,19},{8,20},{9,21},... | collective-permute-start | bytes 2359304 | tf_op jit(solution)/shard_map/ppermute | solution.py:1281
  (177 other events, 3540.1 us)
Sparse Core Ops, SparseCore 0:
  122.6 44.7 all-gather.8
  521.7 29.7 all-gather.6
  590.9 59.7 reduce-scatter.5
  652.7 123.8 all-gather.4
  780.1 182.9 reduce-scatter.7
  966.6 242.1 reduce-scatter.3

commit v3 on v2

--- a/solution.py
+++ b/solution.py
@@ -168,7 +168,8 @@
     )(start, step, act, keep_lanes, in_flat, read_flat, decay)
 
 
-def adjoint_end_kernel(states, chunk, step_ref, grad_ref, keep_ref, read_ref, decay_ref, end_ref, carry_ref, step_t, grad_t):
+def adjoint_end_kernel(states, chunk, step_ref, grad_ref, keep_ref, read_ref, decay_ref, *refs):
+    end_ref, carry_ref, step_t, grad_t = refs[-4:]
     index = pl.program_id(0)
     last = pl.num_programs(0) - 1
     groups = step_ref.shape[1] // (8 * LANES)
@@ -204,7 +205,7 @@
     end_ref[...] = carry_ref[...]
 
 
-def adjoint_end(step, grad, keep_lanes, read_flat, decay):
+def adjoint_end(step, grad, keep_lanes, read_flat, decay, after=()):
     rows, inner = step.shape
     states, planes, _ = decay.shape
     chunk = CHUNK
@@ -215,13 +216,14 @@
         functools.partial(adjoint_end_kernel, states, chunk),
         out_shape=jax.ShapeDtypeStruct(decay.shape, jnp.float32),
         grid=(count,),
-        in_specs=[rowed, rowed, pl.BlockSpec((chunk, LANES), lambda i: (count - 1 - i, 0)), smem(), whole],
+        in_specs=[rowed, rowed, pl.BlockSpec((chunk, LANES), lambda i: (count - 1 - i, 0)), smem(), whole]
+        + [pl.BlockSpec(memory_space=pl.ANY)] * len(after),
         out_specs=whole,
         scratch_shapes=[pltpu.VMEM(decay.shape, jnp.float32)]
         + [pltpu.VMEM((chunk * 8, LANES), jnp.float32)] * 2,
         compiler_params=pltpu.CompilerParams(vmem_limit_bytes=32 << 20),
         name="adjoint_end",
-    )(step, grad, keep_lanes, read_flat, decay)
+    )(step, grad, keep_lanes, read_flat, decay, *after)
 
 
 def adjoint_full_kernel(
@@ -638,19 +640,27 @@
     )
 
 
+def anywhere():
+    return pl.BlockSpec(memory_space=pl.ANY)
+
+
 def vmem():
     return pl.BlockSpec(memory_space=pltpu.VMEM)
 
 
-def gather_rows_kernel(n_row, parts, x_ref, out_ref, send_y, recv_y, send_f, recv_f, own_sem):
+def gather_rows_kernel(n_row, parts, x_ref, *refs):
+    sibling, across = row_peers(n_row)
+    greet([sibling] + across)
+    finish_gather_rows(start_gather_rows(n_row, parts, x_ref, *refs[-6:]))
+
+
+def start_gather_rows(n_row, parts, x_ref, out_ref, send_y, recv_y, send_f, recv_f, own_sem):
     row, seq = lax.axis_index("row"), lax.axis_index("seq")
     y, core = row // 2, lax.rem(row, 2)
     n_y = n_row // 2
     rows = x_ref.shape[0]
     piece = rows // parts
-    sibling = (y * 2 + 1 - core, seq)
-    across = [(lax.rem(y + d, n_y) * 2 + core, seq) for d in range(1, n_y)]
-    greet([sibling] + across)
+    sibling, across = row_peers(n_row)
     pending = []
     for d in range(n_y - 1):
         for c in range(parts):
@@ -666,6 +676,15 @@
     own = send(x_ref, out_ref.at[span(row * rows, rows)], own_sem.at[0], own_sem.at[1], sibling)
     own.start()
     out_ref[span(row * rows, rows), :] = x_ref[...]
+    return (n_row, parts, out_ref, piece, rows, pending, own, send_f, recv_f)
+
+
+def finish_gather_rows(started):
+    n_row, parts, out_ref, piece, rows, pending, own, send_f, recv_f = started
+    row = lax.axis_index("row")
+    y, core = row // 2, lax.rem(row, 2)
+    n_y = n_row // 2
+    sibling = row_peers(n_row)[0]
     forwards = []
     for d in range(n_y - 1):
         origin = lax.rem(y + n_y - 1 - d, n_y) * 2 + core
@@ -682,7 +701,11 @@
         copy.wait()
 
 
-def gather_rows(block, collective=1):
+def gather_rows_scratch(n_y, parts):
+    return [pltpu.SemaphoreType.DMA((n_y - 1, parts))] * 4 + [pltpu.SemaphoreType.DMA((2,))]
+
+
+def gather_rows(block, after=(), collective=1):
     n_row = lax.axis_size("row")
     rows, width = block.shape
     parts = 4 if rows % 64 == 0 else 1
@@ -690,27 +713,39 @@
     return pl.pallas_call(
         functools.partial(gather_rows_kernel, n_row, parts),
         out_shape=jax.ShapeDtypeStruct((n_row * rows, width), block.dtype),
-        in_specs=[vmem()],
+        in_specs=[vmem()] + [anywhere()] * len(after),
         out_specs=vmem(),
-        scratch_shapes=[pltpu.SemaphoreType.DMA((n_y - 1, parts))] * 4
-        + [pltpu.SemaphoreType.DMA((2,))],
-        compiler_params=remote_params(collective, 40),
+        scratch_shapes=gather_rows_scratch(n_y, parts),
+        compiler_params=remote_params(collective + len(after), 40),
         name="gather_rows",
-    )(block)
-
-
-def reduce_rows_kernel(
+    )(block, *after)
+
+
+def row_peers(n_row):
+    row, seq = lax.axis_index("row"), lax.axis_index("seq")
+    y, core = row // 2, lax.rem(row, 2)
+    n_y = n_row // 2
+    sibling = (y * 2 + 1 - core, seq)
+    across = [(lax.rem(y + d, n_y) * 2 + core, seq) for d in range(1, n_y)]
+    return sibling, across
+
+
+def reduce_rows_kernel(n_row, parts, x_ref, out_ref, *scratch):
+    sibling, across = row_peers(n_row)
+    greet([sibling] + across)
+    reduce_rows_body(n_row, parts, x_ref, out_ref, *scratch)
+
+
+def reduce_rows_body(
     n_row, parts, x_ref, out_ref, near, stage, far, send_c, recv_c, send_y, recv_y
 ):
-    row, seq = lax.axis_index("row"), lax.axis_index("seq")
+    row = lax.axis_index("row")
+    sibling, across = row_peers(n_row)
     y, core = row // 2, lax.rem(row, 2)
     n_y = n_row // 2
     rows = out_ref.shape[0]
     piece = rows // parts
     other = 1 - core
-    sibling = (y * 2 + other, seq)
-    across = [(lax.rem(y + d, n_y) * 2 + core, seq) for d in range(1, n_y)]
-    greet([sibling] + across)
     order = [(d + 1) % n_y for d in range(n_y)]
     crossing = {}
     for d in order:
@@ -760,7 +795,19 @@
         copy.wait_send()
 
 
-def reduce_rows(partial, collective=2, dtype=jnp.float32):
+def reduce_rows_scratch(n_y, parts, buffer, dtype):
+    return (
+        [
+            pltpu.VMEM((n_y,) + buffer, dtype),
+            pltpu.VMEM((n_y - 1,) + buffer, dtype),
+            pltpu.VMEM((n_y - 1,) + buffer, dtype),
+        ]
+        + [pltpu.SemaphoreType.DMA((n_y, parts))] * 2
+        + [pltpu.SemaphoreType.DMA((n_y - 1, parts))] * 2
+    )
+
+
+def reduce_rows(partial, collective=14, dtype=jnp.float32):
     n_row = lax.axis_size("row")
     n_y = n_row // 2
     rows, width = partial.shape[0] // n_row, partial.shape[1]
@@ -771,13 +818,7 @@
         out_shape=jax.ShapeDtypeStruct(buffer, dtype),
         in_specs=[vmem()],
         out_specs=vmem(),
-        scratch_shapes=[
-            pltpu.VMEM((n_y,) + buffer, partial.dtype),
-            pltpu.VMEM((n_y - 1,) + buffer, partial.dtype),
-            pltpu.VMEM((n_y - 1,) + buffer, partial.dtype),
-        ]
-        + [pltpu.SemaphoreType.DMA((n_y, parts))] * 2
-        + [pltpu.SemaphoreType.DMA((n_y - 1, parts))] * 2,
+        scratch_shapes=reduce_rows_scratch(n_y, parts, buffer, partial.dtype),
         compiler_params=remote_params(collective, 40),
         name="reduce_rows",
     )(partial)
@@ -821,36 +862,79 @@
         copy.wait_send()
 
 
-def gather_seq_kernel(n_seq, parts, x_ref, out_ref, send_sem, recv_sem):
-    _, seq, place, after, before = ring_neighbours(n_seq)
+def gather_seq_kernel(
+    n_row, n_seq, parts, x_ref, up_ref, *refs
+):
+    out_ref, own_ref, send_sem, recv_sem, send_w, recv_w, local_sem = refs[-7:]
+    row, seq, place, after, before = ring_neighbours(n_seq)
     rows = x_ref.shape[0]
-    greet([after, before])
+    depth, both = up_ref.shape[1:]
+    ff_dim = both // 2
+    ff_row = ff_dim // n_row
+    others = [lax.rem(row + d, n_row) for d in range(1, n_row)]
+    greet([after, before] + [(other, seq) for other in others])
+
+    def slabs(dest):
+        odd = lax.rem(dest, 2)
+        for part in range(2):
+            column = part * ff_dim + dest * ff_row
+            slot = part * (1 - odd) + (1 - part) * odd
+            yield part, (
+                up_ref.at[1, :, pl.ds(pl.multiple_of(column, LANES), ff_row)],
+                own_ref.at[span(row * depth, depth), pl.ds(pl.multiple_of(slot * ff_row, LANES), ff_row)],
+            )
+
+    moved = []
+    for d, other in enumerate(others):
+        for part, (source, target) in slabs(other):
+            copy = send(source, target, send_w.at[d, part], recv_w.at[d, part], (other, seq))
+            copy.start()
+            moved.append(copy)
+    local = []
+    for part, (source, target) in slabs(row):
+        copy = pltpu.make_async_copy(source, target, local_sem.at[part])
+        copy.start()
+        local.append(copy)
     out_ref[span(seq * rows, rows), :] = x_ref[...]
     ring_gather(n_seq, parts, rows, out_ref, send_sem, recv_sem, place, after, before)
-
-
-def gather_seq(block, collective=3):
-    n_seq = lax.axis_size("seq")
+    for copy in moved + local:
+        copy.wait()
+
+
+def gather_seq(block, up_weight, after=(), collective=3):
+    n_row, n_seq = lax.axis_size("row"), lax.axis_size("seq")
     rows, width = block.shape
     parts = 2 if rows % 64 == 0 else 1
+    depth, both = up_weight.shape[1:]
     return pl.pallas_call(
-        functools.partial(gather_seq_kernel, n_seq, parts),
-        out_shape=jax.ShapeDtypeStruct((n_seq * rows, width), block.dtype),
-        in_specs=[vmem()],
-        out_specs=vmem(),
-        scratch_shapes=[pltpu.SemaphoreType.DMA((2, n_seq - 1, parts))] * 2,
+        functools.partial(gather_seq_kernel, n_row, n_seq, parts),
+        out_shape=(
+            jax.ShapeDtypeStruct((n_seq * rows, width), block.dtype),
+            jax.ShapeDtypeStruct((depth * n_row, both // n_row), up_weight.dtype),
+        ),
+        in_specs=[vmem(), anywhere()] + [anywhere()] * len(after),
+        out_specs=(vmem(), anywhere()),
+        scratch_shapes=[pltpu.SemaphoreType.DMA((2, n_seq - 1, parts))] * 2
+        + [pltpu.SemaphoreType.DMA((n_row - 1, 2))] * 2
+        + [pltpu.SemaphoreType.DMA((2,))],
         compiler_params=remote_params(collective, 48),
         name="gather_seq",
-    )(block)
-
-
-def reduce_seq_kernel(n_seq, parts, x_ref, out_ref, held, send_sem, recv_sem):
+    )(block, up_weight, *after)
+
+
+def reduce_seq_kernel(n_seq, parts, x_ref, *refs):
+    out_ref, held, send_sem, recv_sem = refs[-4:]
+    _, _, _, after, before = ring_neighbours(n_seq)
+    greet([after, before])
+    reduce_seq_body(n_seq, parts, x_ref, out_ref, held, send_sem, recv_sem)
+
+
+def reduce_seq_body(n_seq, parts, x_ref, out_ref, held, send_sem, recv_sem):
     n_x = n_seq // GROUPS
     _, seq, place, after, before = ring_neighbours(n_seq)
     rows = out_ref.shape[0]
     half = rows // 2
     piece = half // parts
-    greet([after, before])
     sent = {}
     for step in range(n_seq - 1):
         for c in range(parts):
@@ -890,7 +974,7 @@
         copy.wait_send()
 
 
-def reduce_seq(partial, collective=4, dtype=jnp.float32):
+def reduce_seq(partial, after=(), collective=4, dtype=jnp.float32):
     n_seq = lax.axis_size("seq")
     rows, width = partial.shape[0] // n_seq, partial.shape[1]
     if rows % 32:
@@ -899,22 +983,33 @@
     return pl.pallas_call(
         functools.partial(reduce_seq_kernel, n_seq, parts),
         out_shape=jax.ShapeDtypeStruct((rows, width), dtype),
-        in_specs=[vmem()],
+        in_specs=[vmem()] + [anywhere()] * len(after),
         out_specs=vmem(),
         scratch_shapes=[pltpu.VMEM((2, n_seq - 1, rows // 2, width), partial.dtype)]
         + [pltpu.SemaphoreType.DMA((2, n_seq - 1, parts))] * 2,
         compiler_params=remote_params(collective, 48),
         name="reduce_seq",
-    )(partial)
-
-
-def exchange_kernel(n_seq, forward, x_ref, decay_ref, out_ref, all_ref, send_sem, recv_sem):
-    _, seq, place, after, before = ring_neighbours(n_seq)
+    )(partial, *after)
+
+
+def exchange_kernel(n_row, n_seq, forward, x_ref, decay_ref, *refs):
+    if forward:
+        out_ref, all_ref, send_sem, recv_sem = refs[-4:]
+    else:
+        blocks_ref, low_ref = refs[:2]
+        out_ref, spread_ref, rows_ref, all_ref, send_sem, recv_sem, send_b, recv_b = refs[-13:-5]
+    row, seq, place, after, before = ring_neighbours(n_seq)
     rows = x_ref.shape[0]
     states, planes, _ = decay_ref.shape
-    greet([after, before])
+    if forward:
+        greet([after, before])
+    else:
+        sibling, across = row_peers(n_row)
+        greet([sibling] + across + [(row, lax.rem(seq + d, n_seq)) for d in range(1, n_seq)])
+        riding = start_gather_rows(n_row, 4, low_ref, rows_ref, *refs[-5:])
     all_ref[span(seq * rows, rows), :] = x_ref[...]
     ring_gather(n_seq, 1, rows, all_ref, send_sem, recv_sem, place, after, before)
+    swapped = [] if forward else start_swap(n_seq, blocks_ref, spread_ref, send_b, recv_b)
     out_ref[...] = jnp.zeros_like(out_ref)
 
     def take(turn, _):
@@ -930,10 +1025,14 @@
         return 0
 
     lax.fori_loop(0, n_seq, take, 0)
-
-
-def exchange_states(summed, end_state, decay, forward, collective):
-    n_seq = lax.axis_size("seq")
+    if not forward:
+        finish_gather_rows(riding)
+    for copy in swapped:
+        copy.wait()
+
+
+def exchange_states(summed, end_state, decay, collective, blocks=None, rider=None, after=()):
+    n_row, n_seq = lax.axis_size("row"), lax.axis_size("seq")
     states, planes, _ = decay.shape
     high = summed.astype(jnp.bfloat16)
     lower = (summed - high.astype(jnp.float32)).astype(jnp.bfloat16)
@@ -947,91 +1046,199 @@
         ],
         axis=0,
     )
+    ring = [pltpu.VMEM((n_seq * rows, LANES), jnp.bfloat16)] + [
+        pltpu.SemaphoreType.DMA((2, n_seq - 1, 1))
+    ] * 2
+    entering = jax.ShapeDtypeStruct(decay.shape, jnp.float32)
+    if blocks is None:
+        return pl.pallas_call(
+            functools.partial(exchange_kernel, n_row, n_seq, True),
+            out_shape=entering,
+            in_specs=[vmem(), vmem()] + [anywhere()] * len(after),
+            out_specs=vmem(),
+            scratch_shapes=ring,
+            compiler_params=remote_params(collective, 32),
+            name="exchange_states",
+        )(payload, decay, *after)
     return pl.pallas_call(
-        functools.partial(exchange_kernel, n_seq, forward),
-        out_shape=jax.ShapeDtypeStruct(decay.shape, jnp.float32),
-        in_specs=[vmem(), vmem()],
-        out_specs=vmem(),
-        scratch_shapes=[pltpu.VMEM((n_seq * rows, LANES), jnp.bfloat16)]
-        + [pltpu.SemaphoreType.DMA((2, n_seq - 1, 1))] * 2,
-        compiler_params=remote_params(collective, 32),
-        name="exchange_states",
-    )(payload, decay)
-
-
-def collect_heads_kernel(n_x, x_ref, out_ref, send_sem, recv_sem):
+        functools.partial(exchange_kernel, n_row, n_seq, False),
+        out_shape=(
+            entering,
+            jax.ShapeDtypeStruct(blocks.shape, blocks.dtype),
+            jax.ShapeDtypeStruct((n_row * rider.shape[0], rider.shape[1]), rider.dtype),
+        ),
+        in_specs=[vmem()] * 4 + [anywhere()] * len(after),
+        out_specs=(vmem(),) * 3,
+        scratch_shapes=ring
+        + [pltpu.SemaphoreType.DMA((n_seq - 1,))] * 2
+        + gather_rows_scratch(n_row // 2, 4),
+        compiler_params=remote_params(collective, 40),
+        name="exchange_states_back",
+    )(payload, decay, blocks, rider, *after)
+
+
+def start_row_swap(n_row, x_ref, out_ref, send_sem, recv_sem, local_sem):
+    row, seq = lax.axis_index("row"), lax.axis_index("seq")
+    rows, cols = x_ref.shape[0], out_ref.shape[1]
+    mine = out_ref.at[span(row * rows, rows)]
+    moved = []
+    for d in range(1, n_row):
+        other = lax.rem(row + d, n_row)
+        copy = send(
+            x_ref.at[:, pl.ds(pl.multiple_of(other * cols, LANES), cols)],
+            mine,
+            send_sem.at[d - 1],
+            recv_sem.at[d - 1],
+            (other, seq),
+        )
+        copy.start()
+        moved.append(copy)
+    own = pltpu.make_async_copy(
+        x_ref.at[:, pl.ds(pl.multiple_of(row * cols, LANES), cols)], mine, local_sem
+    )
+    own.start()
+    return moved + [own]
+
+
+def swap_heads_kernel(
+    n_row, n_x, collect, x_ref, rider_ref, *refs
+):
+    if collect:
+        out_ref, rode_ref, send_sem, recv_sem, send_r, recv_r, local_sem = refs
+    else:
+        part_ref, out_ref, rode_ref, sum_ref, send_sem, recv_sem, send_r, recv_r, local_sem, *scratch = refs
     row, seq = lax.axis_index("row"), lax.axis_index("seq")
     z, x = seq // n_x, lax.rem(seq, n_x)
-    rows, cols = out_ref.shape[0], x_ref.shape[1]
     peers = [lax.rem(z + d, GROUPS) for d in range(1, GROUPS)]
-    greet([(row, peer * n_x + x) for peer in peers])
-    mine = pl.ds(pl.multiple_of(z * cols, LANES), cols)
+    greet(
+        [(row, peer * n_x + x) for peer in peers]
+        + [(lax.rem(row + d, n_row), seq) for d in range(1, n_row)]
+    )
+
+    def block(ref, place, wide):
+        if wide:
+            cols = ref.shape[1] // GROUPS
+            return ref.at[:, pl.ds(pl.multiple_of(place * cols, LANES), cols)]
+        rows = ref.shape[0] // GROUPS
+        return ref.at[span(place * rows, rows)]
+
     sent = []
     for d, peer in enumerate(peers):
         copy = send(
-            x_ref.at[span(peer * rows, rows)],
-            out_ref.at[:, mine],
+            block(x_ref, peer, not collect),
+            block(out_ref, z, collect),
             send_sem.at[d],
             recv_sem.at[d],
             (row, peer * n_x + x),
         )
         copy.start()
         sent.append(copy)
-    out_ref[:, mine] = x_ref[span(z * rows, rows), :]
-    for copy in sent:
+    riding = start_row_swap(n_row, rider_ref, rode_ref, send_r, recv_r, local_sem)
+    block(out_ref, z, collect)[...] = block(x_ref, z, not collect)[...]
+    if not collect:
+        reduce_rows_body(n_row, 4, part_ref, sum_ref, *scratch)
+    for copy in sent + riding:
         copy.wait()
 
 
-def spread_heads_kernel(n_x, x_ref, out_ref, send_sem, recv_sem):
+def swap_heads(values, rider, collect, collective, partial=None):
+    n_row, n_x = lax.axis_size("row"), lax.axis_size("seq") // GROUPS
+    rows, cols = values.shape
+    shape = (rows // GROUPS, cols * GROUPS) if collect else (rows * GROUPS, cols // GROUPS)
+    narrow = rider.shape[1] // n_row % LANES
+    if narrow:
+        swapped = lax.all_to_all(rider, "row", split_axis=1, concat_axis=0, tiled=True)
+        rider = jnp.zeros((16, n_row * LANES), rider.dtype)
+    rode = (rider.shape[0] * n_row, rider.shape[1] // n_row)
+    sem = pltpu.SemaphoreType.DMA
+    operands = [values, rider]
+    outputs = [
+        jax.ShapeDtypeStruct(shape, values.dtype),
+        jax.ShapeDtypeStruct(rode, rider.dtype),
+    ]
+    scratch = [sem((GROUPS - 1,))] * 2 + [sem((n_row - 1,))] * 2 + [sem]
+    if not collect:
+        buffer = (partial.shape[0] // n_row, partial.shape[1])
+        operands.append(partial)
+        outputs.append(jax.ShapeDtypeStruct(buffer, jnp.float32))
+        scratch += reduce_rows_scratch(n_row // 2, 4, buffer, partial.dtype)
+    results = pl.pallas_call(
+        functools.partial(swap_heads_kernel, n_row, n_x, collect),
+        out_shape=tuple(outputs),
+        in_specs=[vmem()] * len(operands),
+        out_specs=(vmem(),) * len(outputs),
+        scratch_shapes=scratch,
+        compiler_params=remote_params(collective, 40),
+        name="collect_heads" if collect else "spread_heads",
+    )(*operands)
+    if narrow:
+        return (results[0], swapped) + tuple(results[2:])
+    return results
+
+
+def start_swap(n_seq, x_ref, out_ref, send_sem, recv_sem):
     row, seq = lax.axis_index("row"), lax.axis_index("seq")
-    z, x = seq // n_x, lax.rem(seq, n_x)
-    rows, cols = x_ref.shape[0], out_ref.shape[1]
-    peers = [lax.rem(z + d, GROUPS) for d in range(1, GROUPS)]
-    greet([(row, peer * n_x + x) for peer in peers])
-    mine = span(z * rows, rows)
+    place = ring_place(seq, n_seq // GROUPS)
     sent = []
-    for d, peer in enumerate(peers):
+    for d in range(1, n_seq):
+        peer = lax.rem(seq + d, n_seq)
         copy = send(
-            x_ref.at[:, pl.ds(pl.multiple_of(peer * cols, LANES), cols)],
-            out_ref.at[mine],
-            send_sem.at[d],
-            recv_sem.at[d],
-            (row, peer * n_x + x),
+            x_ref.at[peer], out_ref.at[place], send_sem.at[d - 1], recv_sem.at[d - 1], (row, peer)
         )
         copy.start()
         sent.append(copy)
-    out_ref[mine, :] = x_ref[:, pl.ds(pl.multiple_of(z * cols, LANES), cols)]
-    for copy in sent:
-        copy.wait()
-
-
-def swap_heads(values, collect, collective):
-    n_x = lax.axis_size("seq") // GROUPS
-    rows, cols = values.shape
-    shape = (rows // GROUPS, cols * GROUPS) if collect else (rows * GROUPS, cols // GROUPS)
-    return pl.pallas_call(
-        functools.partial(collect_heads_kernel if collect else spread_heads_kernel, n_x),
-        out_shape=jax.ShapeDtypeStruct(shape, values.dtype),
-        in_specs=[vmem()],
-        out_specs=vmem(),
-        scratch_shapes=[pltpu.SemaphoreType.DMA((GROUPS - 1,))] * 2,
-        compiler_params=remote_params(collective, 32),
-        name="collect_heads" if collect else "spread_heads",
-    )(values)
+    out_ref[place] = x_ref[seq]
+    return sent
 
 
 def swap_seq_kernel(n_seq, x_ref, out_ref, send_sem, recv_sem):
     row, seq = lax.axis_index("row"), lax.axis_index("seq")
-    peers = [lax.rem(seq + d, n_seq) for d in range(1, n_seq)]
-    greet([(row, peer) for peer in peers])
-    sent = []
-    for d, peer in enumerate(peers):
-        copy = send(x_ref.at[peer], out_ref.at[seq], send_sem.at[d], recv_sem.at[d], (row, peer))
-        copy.start()
-        sent.append(copy)
-    out_ref[seq] = x_ref[seq]
-    for copy in sent:
+    greet([(row, lax.rem(seq + d, n_seq)) for d in range(1, n_seq)])
+    for copy in start_swap(n_seq, x_ref, out_ref, send_sem, recv_sem):
         copy.wait()
+
+
+def finish_kernel(
+    n_row, n_seq, parts, anchors, blocks_ref, packed_ref, *refs
+):
+    spread_ref, out_ref, send_b, recv_b, rowed, held, send_s, recv_s, *scratch = refs[anchors:]
+    row, seq = lax.axis_index("row"), lax.axis_index("seq")
+    sibling, across = row_peers(n_row)
+    greet([sibling] + across + [(row, lax.rem(seq + d, n_seq)) for d in range(1, n_seq)])
+    swapped = start_swap(n_seq, blocks_ref, spread_ref, send_b, recv_b)
+    reduce_rows_body(n_row, parts, packed_ref, rowed, *scratch)
+    reduce_seq_body(n_seq, 1, rowed, out_ref, held, send_s, recv_s)
+    for copy in swapped:
+        copy.wait()
+
+
+def swap_and_reduce(blocks, packed, collective, after=()):
+    n_row, n_seq = lax.axis_size("row"), lax.axis_size("seq")
+    rows, width = packed.shape[0] // (n_row * n_seq), packed.shape[1]
+    if rows % 32:
+        summed = lax.psum_scatter(packed, ("row", "seq"), scatter_dimension=0, tiled=True)
+        return swap_seq(blocks, collective), summed.astype(jnp.float32)
+    buffer = (n_seq * rows, width)
+    parts = 4
+    sem = pltpu.SemaphoreType.DMA
+    return pl.pallas_call(
+        functools.partial(finish_kernel, n_row, n_seq, parts, len(after)),
+        out_shape=(
+            jax.ShapeDtypeStruct(blocks.shape, blocks.dtype),
+            jax.ShapeDtypeStruct((rows, width), jnp.float32),
+        ),
+        in_specs=[vmem()] * 2 + [anywhere()] * len(after),
+        out_specs=(vmem(), vmem()),
+        scratch_shapes=[sem((n_seq - 1,))] * 2
+        + [
+            pltpu.VMEM(buffer, packed.dtype),
+            pltpu.VMEM((2, n_seq - 1, rows // 2, width), packed.dtype),
+        ]
+        + [sem((2, n_seq - 1, 1))] * 2
+        + reduce_rows_scratch(n_row // 2, parts, buffer, packed.dtype),
+        compiler_params=remote_params(collective, 32),
+        name="swap_and_reduce",
+    )(blocks, packed, *after)
 
 
 def swap_seq(blocks, collective):
@@ -1110,36 +1317,67 @@
     return pl.pallas_call(
         functools.partial(gather_input_kernel, parts),
         out_shape=jax.ShapeDtypeStruct((n_row * shard.shape[0], shard.shape[1]), shard.dtype),
-        in_specs=[pl.BlockSpec(memory_space=pl.ANY)],
-        out_specs=pl.BlockSpec(memory_space=pl.ANY),
+        in_specs=[pl.BlockSpec(memory_space=pltpu.HBM)],
+        out_specs=pl.BlockSpec(memory_space=pltpu.HBM),
         scratch_shapes=[sem, sem((2,))] + [sem((parts,))] * 8,
         compiler_params=remote_params(collective, 16),
         name="gather_input",
     )(shard)
 
 
+def grad_blocks_kernel(up_rows, d_ref, x_ref, h_ref, u_ref, out_ref):
+    out_ref[:up_rows, :] = left_trans(d_ref[...], x_ref[...]).astype(out_ref.dtype)
+    out_ref[up_rows:, :] = left_trans(h_ref[...], u_ref[...]).astype(out_ref.dtype)
+
+
+def grad_blocks(d_gate_up, spread, hidden, upstream):
+    n_seq = lax.axis_size("seq")
+    n_x = n_seq // GROUPS
+    tokens, width = spread.shape
+    up_rows, down_rows = d_gate_up.shape[1] // n_seq, hidden.shape[1] // n_seq
+    whole = pl.BlockSpec((tokens, width), lambda k: (0, 0))
+    return pl.pallas_call(
+        functools.partial(grad_blocks_kernel, up_rows),
+        out_shape=jax.ShapeDtypeStruct((n_seq * (up_rows + down_rows), width), jnp.bfloat16),
+        grid=(n_seq,),
+        in_specs=[
+            pl.BlockSpec((tokens, up_rows), lambda k: (0, ring_member(k, n_x))),
+            whole,
+            pl.BlockSpec((tokens, down_rows), lambda k: (0, ring_member(k, n_x))),
+            whole,
+        ],
+        out_specs=pl.BlockSpec((up_rows + down_rows, width), lambda k: (k, 0)),
+        compiler_params=pltpu.CompilerParams(vmem_limit_bytes=40 << 20),
+        name="grad_blocks",
+    )(d_gate_up, spread, hidden, upstream)
+
+
+def cycle(depth, breadth):
+    order = [(z, 0) for z in range(depth)]
+    for turn in range(depth):
+        across = range(1, breadth) if turn % 2 == 0 else range(breadth - 1, 0, -1)
+        order += [(depth - 1 - turn, x) for x in across]
+    return order
+
+
+def seq_order():
+    n_x = lax.axis_size("seq") // GROUPS
+    return [z * n_x + x for z, x in cycle(GROUPS, n_x)]
+
+
+def plane_order():
+    n_x = lax.axis_size("seq") // GROUPS
+    order = []
+    for y, x in cycle(lax.axis_size("row") // 2, n_x):
+        cores = (0, 1) if len(order) // 2 % 2 == 0 else (1, 0)
+        order += [(2 * y + core, x) for core in cores]
+    return order
+
+
 def plane_groups():
     n_seq = lax.axis_size("seq")
     n_x = n_seq // GROUPS
-    n_row = lax.axis_size("row")
-    return [
-        [r * n_seq + z * n_x + x for r in range(n_row) for x in range(n_x)] for z in range(GROUPS)
-    ]
-
-
-def swap_rows(values):
-    n_row = lax.axis_size("row")
-    row = lax.axis_index("row")
-    rows, columns = values.shape
-    owned = columns // n_row
-    whole = jnp.zeros((n_row * rows, owned), values.dtype)
-    for turn in range(n_row):
-        other = row ^ turn
-        piece = lax.dynamic_slice(values, (0, other * owned), (rows, owned))
-        if turn:
-            piece = lax.ppermute(piece, "row", [(i, i ^ turn) for i in range(n_row)])
-        whole = lax.dynamic_update_slice(whole, piece, (other * rows, 0))
-    return whole
+    return [[r * n_seq + z * n_x + x for r, x in plane_order()] for z in range(GROUPS)]
 
 
 def reduce_background(parts):
@@ -1169,19 +1407,6 @@
     return left_trans(flat, gathered).astype(jnp.bfloat16)
 
 
-def swap_seq_async(blocks):
-    n_seq = lax.axis_size("seq")
-    seq = lax.axis_index("seq")
-    whole = jnp.zeros_like(blocks)
-    for turn in range(n_seq):
-        other = seq ^ turn
-        piece = lax.dynamic_index_in_dim(blocks, other, 0)
-        if turn:
-            piece = lax.ppermute(piece, "seq", [(i, i ^ turn) for i in range(n_seq)])
-        whole = lax.dynamic_update_slice(whole, piece, (other, 0, 0))
-    return whole
-
-
 def norm_apply(values, gain_row):
     factor = lax.rsqrt(jnp.mean(values * values, axis=-1, keepdims=True) + eps)
     return (values * factor * gain_row, factor)
@@ -1228,19 +1453,23 @@
     )
 
 
-def own_up_columns(up_local):
+def own_up_columns(up_local, number):
     n_row = lax.axis_size("row")
     row = lax.axis_index("row")
-    depth, both = up_local.shape
+    depth, both = up_local.shape[1:]
     ff_dim = both // 2
     ff_row = ff_dim // n_row
     width = depth * n_row
 
     def slab(dest):
         odd = dest % 2
-        first = lax.dynamic_slice(up_local, (0, odd * ff_dim + dest * ff_row), (depth, ff_row))
-        second = lax.dynamic_slice(up_local, (0, (1 - odd) * ff_dim + dest * ff_row), (depth, ff_row))
-        return jnp.concatenate([first, second], axis=1)
+        halves = [
+            lax.dynamic_slice(
+                up_local, (number, 0, half * ff_dim + dest * ff_row), (1, depth, ff_row)
+            )[0]
+            for half in (odd, 1 - odd)
+        ]
+        return jnp.concatenate(halves, axis=1)
 
     whole = jnp.zeros((width, 2 * ff_row), up_local.dtype)
     for turn in range(n_row):
@@ -1252,18 +1481,18 @@
     return whole
 
 
-def mlp_forward(values, gain_row, up_own, down_own):
+def mlp_forward(values, gain_row, up_own, down_own, after=()):
     odd = lax.axis_index("row") % 2 == 1
     ff_row = down_own.shape[0]
     normed, factor = norm_apply(values, gain_row)
-    spread = gather_rows(normed.astype(jnp.bfloat16))
+    spread = gather_rows(normed.astype(jnp.bfloat16), after)
     gate_up = product(spread, up_own)
     first, second = (gate_up[:, :ff_row], gate_up[:, ff_row:])
     gate_part = jnp.where(odd, second, first)
     up_part = jnp.where(odd, first, second)
     hidden = (jax.nn.silu(gate_part) * up_part).astype(jnp.bfloat16)
     partial = product(hidden, down_own).astype(jnp.bfloat16)
-    return (values + reduce_rows(partial), (factor, spread, gate_part, up_part, hidden))
+    return (partial, (factor, spread, gate_part, up_part, hidden))
 
 
 def place_up_grad(grad):
@@ -1281,10 +1510,9 @@
     return lax.ppermute(grad, ("row", "seq"), pairs)
 
 
-def mlp_backward(values, gain_row, up_own, down_own, kept, upstream, upstream_all):
+def mlp_backward(values, gain_row, up_own, down_own, kept, upstream, upstream_all, sums_before=()):
     factor, spread, gate_part, up_part, hidden = kept
     odd = lax.axis_index("row") % 2 == 1
-    g_down = left_trans(hidden, upstream_all)
     d_hidden = right_trans(upstream_all, down_own)
     gate_sig = jax.nn.sigmoid(gate_part)
     d_gate = d_hidden * up_part * gate_sig * (1.0 + gate_part * (1.0 - gate_sig))
@@ -1292,10 +1520,28 @@
     d_gate_up = jnp.concatenate(
         [jnp.where(odd, d_up, d_gate), jnp.where(odd, d_gate, d_up)], axis=1
     ).astype(jnp.bfloat16)
+    n_seq = lax.axis_size("seq")
+    up_rows = d_gate_up.shape[1] // n_seq
+    if up_rows % (2 * LANES):
+        merged = jnp.concatenate(
+            [
+                left_trans(d_gate_up, spread).reshape(n_seq, up_rows, -1)[jnp.array(seq_order())],
+                left_trans(hidden, upstream_all).reshape(n_seq, up_rows // 2, -1)[jnp.array(seq_order())],
+            ],
+            axis=1,
+        )
+        merged = merged.reshape(-1, merged.shape[2]).astype(jnp.bfloat16)
+    else:
+        merged = grad_blocks(d_gate_up, spread, hidden, upstream_all)
+    d_gate_up, merged = lax.optimization_barrier((d_gate_up, merged))
+    merged = lax.optimization_barrier((merged,) + sums_before)[0]
+    summed = lax.psum_scatter(
+        merged, "seq", scatter_dimension=0, tiled=True, axis_index_groups=[seq_order()]
+    )
+    summed = (summed[:up_rows], summed[up_rows:])
     d_normed = reduce_rows(right_trans(d_gate_up, up_own).astype(jnp.bfloat16))
-    g_up = left_trans(d_gate_up, spread)
     d_norm, g_gain = norm_back(values, factor, gain_row, d_normed)
-    return (upstream + d_norm, g_gain, g_up, g_down)
+    return (upstream + d_norm, g_gain, summed)
 
 
 def matchings(edges, size):
@@ -1332,14 +1578,13 @@
     unit = math.gcd(owned, group_cols)
     count = owned // unit
     edges, slots = [], []
-    for r in range(n_row):
+    for member, (r, x) in enumerate(plane_order()):
         for z in range(GROUPS):
-            for x in range(n_x):
-                for u in range(count):
-                    local = (r * n_x + x) * owned + u * unit
-                    column = (local // group_cols) * width + z * group_cols + local % group_cols
-                    edges.append((r * n_seq + z * n_x + x, column // owned))
-                    slots.append((u, column % owned // unit))
+            for u in range(count):
+                local = member * owned + u * unit
+                column = (local // group_cols) * width + z * group_cols + local % group_cols
+                edges.append((r * n_seq + z * n_x + x, column // owned))
+                slots.append((u, column % owned // unit))
     result = jnp.zeros_like(piece)
     for chosen in matchings(edges, size):
         send_slot = [0] * size
@@ -1355,18 +1600,6 @@
             result, moved, (jnp.array(recv_slot, jnp.int32)[me] * unit, 0)
         )
     return result
-
-
-def place_out_grad(piece):
-    n_row = lax.axis_size("row")
-    n_seq = lax.axis_size("seq")
-    n_x = n_seq // GROUPS
-    pairs = []
-    for r in range(n_row):
-        for z in range(GROUPS):
-            for x in range(n_x):
-                pairs.append((r * n_seq + z * n_x + x, z * n_row * n_x + r * n_x + x))
-    return lax.ppermute(piece, ("row", "seq"), pairs)
 
 
 def per_device(
@@ -1421,13 +1654,15 @@
     tap_masks = conv_masks(positions, lengths)
     whole_in = gather_input(input_weight, 10)
     up_local = lax.optimization_barrier((mlp_up_weight, whole_in))[0]
-    up_first = own_up_columns(up_local[0])
-    up_last = own_up_columns(up_local[1])
+    up_first = own_up_columns(up_local, 0)
     down_first, down_last = (mlp_down_weight[0], mlp_down_weight[1])
     normed_in, factor_in = norm_apply(source, gain_in)
     low_in = normed_in.astype(jnp.bfloat16)
-    gathered_in = lax.all_gather(low_in, "seq", axis=0, tiled=True)
-    gathered_grad = lax.all_gather(cotangent[0], "row", axis=0, tiled=True)
+    low_sent, grad_sent = lax.optimization_barrier((low_in, cotangent[0], whole_in))[:2]
+    gathered_in = lax.all_gather(
+        low_sent, "seq", axis=0, tiled=True, axis_index_groups=[seq_order()]
+    )
+    gathered_grad = lax.all_gather(grad_sent, "row", axis=0, tiled=True)
     mixed_in = product(low_in, whole_in)
     conv_input = mixed_in[:, :inner_dim]
     gate_input = mixed_in[:, inner_dim:]
@@ -1455,18 +1690,20 @@
     summed_steps = jnp.where(
         jnp.min(keep_flag) > 0, jnp.sum(step_size, axis=0), RESET
     ).reshape(-1, LANES)
-    start_hidden = exchange_states(summed_steps, local_end, decay_planes, True, 5)
+    start_hidden = exchange_states(
+        summed_steps, local_end, decay_planes, 5
+    )
     scanned, marks = scan_out(
         start_hidden, step_size, activated_low, keep_lanes, in_flat, read_flat, decay_planes
     )
     mamba_out = scanned + skip_row * activated
     gate_act = jax.nn.silu(gate_input)
     gated = (mamba_out * gate_act).astype(jnp.bfloat16)
-    gated_rows = swap_rows(gated)
     first_out = source + product(gated, output_weight)
-    second_out, kept_first = mlp_forward(first_out, gains_mlp[0], up_first, down_first)
+    second_partial, kept_first = mlp_forward(first_out, gains_mlp[0], up_first, down_first)
+    second_out = first_out + reduce_rows(second_partial)
     normed_attn, factor_attn = norm_apply(second_out, gain_attn)
-    context = gather_seq(normed_attn.astype(jnp.bfloat16))
+    context, up_last = gather_seq(normed_attn.astype(jnp.bfloat16), mlp_up_weight, (gathered_in,))
     length = context.shape[0]
     head_weight = jnp.concatenate(
         [
@@ -1489,13 +1726,13 @@
     attended, log_total = attend(
         x_array, lows, triple, first_key[:, None], n_x, head_count, rows_here
     )
-    attended_low = swap_heads(attended, True, 7)
-    attended_rows = swap_rows(attended_low)
+    attended_low, gated_rows = swap_heads(attended, gated, True, 7)
     third_out = second_out + product(attended_low, attn_output)
-    final_out, kept_last = mlp_forward(third_out, gains_mlp[1], up_last, down_last)
-    output = final_out.astype(jnp.bfloat16)
+    final_partial, kept_last = mlp_forward(
+        third_out, gains_mlp[1], up_last, down_last, (gathered_grad,)
+    )
     grad_low = cotangent[0]
-    d_third, g_gain_last, g_up_last, g_down_last = mlp_backward(
+    d_third, g_gain_last, summed_last = mlp_backward(
         third_out,
         gains_mlp[1],
         up_last,
@@ -1506,10 +1743,15 @@
     )
     d_third_low = d_third.astype(jnp.bfloat16)
     d_third_rows = lax.all_gather(d_third_low, "row", axis=0, tiled=True)
-    d_attended = swap_heads(right_trans(d_third_low, attn_output).astype(jnp.bfloat16), False, 8)
-    up_piece, down_piece = reduce_background([g_up_last, g_down_last])
-    g_up_last = place_up_grad(up_piece).astype(jnp.float32).T
-    g_down_last = down_piece.astype(jnp.float32)
+    d_attended, attended_rows, final_sum = swap_heads(
+        right_trans(d_third_low, attn_output).astype(jnp.bfloat16),
+        attended_low,
+        False,
+        8,
+        final_partial,
+    )
+    output = (third_out + final_sum).astype(jnp.bfloat16)
+    g_down_last = summed_last[1].astype(jnp.float32)
     d_query, d_keys, d_values = attend_back(
         x_array,
         lows,
@@ -1529,63 +1771,61 @@
         own_x, d_query.reshape(GROUPS, 1, rows_here, group_cols), jnp.bfloat16(0)
     ).reshape(length, group_cols)
     d_triple = jnp.concatenate([d_query_full, d_keys, d_values], axis=1)
-    d_attn_normed = reduce_seq(right_trans(d_triple, head_weight).astype(jnp.bfloat16))
-    g_attn_weight = (
-        place_attn_grad(
-            lax.psum_scatter(
-                left_trans(d_triple, context).astype(jnp.bfloat16),
-                ("row", "seq"),
-                scatter_dimension=0,
-                tiled=True,
-                axis_index_groups=plane_groups(),
-            ),
-            width,
-        )
-        .astype(jnp.float32)
-        .T
+    d_attn_normed = reduce_seq(
+        right_trans(d_triple, head_weight).astype(jnp.bfloat16), tuple(summed_last)
+    )
+    g_attn_weight = lax.psum_scatter(
+        left_trans(d_triple, context).astype(jnp.bfloat16),
+        ("row", "seq"),
+        scatter_dimension=0,
+        tiled=True,
+        axis_index_groups=plane_groups(),
     )
     d_attn_norm, g_attn_gain = norm_back(
         second_out, factor_attn, gain_attn, d_attn_normed
     )
     d_second = d_third + d_attn_norm
-    d_first, g_gain_first, g_up_first, g_down_first = mlp_backward(
+    d_first, g_gain_first, summed_first = mlp_backward(
         first_out,
         gains_mlp[0],
         up_first,
         down_first,
         kept_first,
         d_second,
-        gather_rows(d_second.astype(jnp.bfloat16)),
+        gather_rows(d_second.astype(jnp.bfloat16), (d_third_rows,)),
+        (g_attn_weight,),
     )
     d_first_low = d_first.astype(jnp.bfloat16)
-    d_first_rows = gather_rows(d_first_low)
-    up_piece, down_piece, output_piece, attn_piece = reduce_background(
-        [
-            g_up_first,
-            g_down_first,
-            left_trans(gated_rows, d_first_rows),
-            left_trans(attended_rows, d_third_rows),
-        ]
-    )
-    g_up_first = place_up_grad(up_piece).astype(jnp.float32).T
-    g_down_first = down_piece.astype(jnp.float32)
-    g_output_weight = output_piece.astype(jnp.float32)
-    g_attn_output = attn_piece.astype(jnp.float32)
+    g_down_first = summed_first[1].astype(jnp.float32)
     d_gated = right_trans(d_first_low, output_weight)
     d_scanned = d_gated * gate_act
     gate_sig = jax.nn.sigmoid(gate_input)
     d_gate = d_gated * mamba_out * gate_sig * (1.0 + gate_input * (1.0 - gate_sig))
     d_gate_low = d_gate.astype(jnp.bfloat16)
-    g_input_gate = input_term(swap_seq_async(owner_blocks(d_gate_low)), gathered_in)
     g_skip_scale = jnp.sum(d_scanned * activated, axis=0)
-    back_end = adjoint_end(step_size, d_scanned, keep_lanes, read_flat, decay_planes)
-    end_grad = exchange_states(summed_steps, back_end, decay_planes, False, 6)
+    back_end = adjoint_end(
+        step_size, d_scanned, keep_lanes, read_flat, decay_planes
+    )
+    end_grad, gate_spread, d_first_rows = exchange_states(
+        summed_steps, back_end, decay_planes, 6, owner_blocks(d_gate_low), d_first_low, tuple(summed_first)
+    )
+    sums = [
+        left_trans(gated_rows, d_first_rows).astype(jnp.bfloat16),
+        left_trans(attended_rows, d_third_rows).astype(jnp.bfloat16),
+    ]
+    sums = lax.optimization_barrier(tuple(sums) + tuple(summed_first))[:2]
+    output_piece, attn_piece = reduce_background(sums)
+    g_output_weight = output_piece.astype(jnp.float32)
+    g_attn_output = attn_piece.astype(jnp.float32)
+    late = lax.optimization_barrier((summed_last[0], summed_first[0], g_attn_weight, end_grad))
+    g_up_last, g_up_first = [place_up_grad(piece).astype(jnp.float32).T for piece in late[:2]]
+    g_attn_weight = place_attn_grad(late[2], width).astype(jnp.float32).T
     g_step, g_activated, in_lanes, read_lanes, g_decays = adjoint_full(
         end_grad, marks, step_size, activated_low, d_scanned, keep_lanes, in_flat, read_flat, decay_planes
     )
     g_input_map = jnp.sum(in_lanes.reshape(rows_here, state_dim, LANES), axis=2)
     g_read_map = jnp.sum(read_lanes.reshape(rows_here, state_dim, LANES), axis=2)
-    g_decay_log = (g_decays.reshape(state_dim, inner_dim) * decays).T
+    g_decay_log = g_decays.reshape(state_dim, inner_dim) * decays
     d_step_pre = g_step * jax.nn.sigmoid(step_pre)
     g_step_bias = jnp.sum(d_step_pre, axis=0)
     d_step_low = d_step_pre.astype(jnp.bfloat16)
@@ -1609,53 +1849,63 @@
     back_rows = from_behind(d_padded[: CONV - 1].astype(jnp.bfloat16), "seq", -1)
     d_conv_input = d_padded[CONV - 1 :] + jnp.pad(back_rows, ((rows_here - (CONV - 1), 0), (0, 0)))
     d_conv_low = d_conv_input.astype(jnp.bfloat16)
-    g_input_conv = input_term(swap_seq(owner_blocks(d_conv_low), 9), gathered_in)
     d_mixed = jnp.concatenate([d_conv_low, d_gate_low], axis=1)
     d_normed_in = right_trans(d_mixed, whole_in)
     d_source, g_norm_gain = norm_back(source, factor_in, gain_in, d_normed_in)
     tokens_grad = (d_first + d_source).astype(jnp.bfloat16)
 
     owners = n_row * n_seq
-    g_input_weight = (
-        reduce_rows(jnp.concatenate([g_input_conv, g_input_gate], axis=0), 13).T
-    )
     gains = jnp.stack([g_norm_gain, g_attn_gain, g_gain_first, g_gain_last], axis=0)
-    gain_cols = gains.size // inner_dim
-    columns = [
-        g_select_weight,
-        left_trans(d_step_low, step_low),
+    gain_rows = gains.size // inner_dim
+    lines = [
         g_decay_log,
-        g_conv_weight.T,
-        g_conv_bias[:, None],
-        g_step_bias[:, None],
-        g_skip_scale[:, None],
-        gains.reshape(4, owners, -1).transpose(1, 0, 2).reshape(inner_dim, gain_cols),
+        g_conv_weight,
+        g_conv_bias[None],
+        g_step_bias[None],
+        g_skip_scale[None],
+        gains.reshape(gain_rows, -1, owners, width // owners)
+        .transpose(0, 2, 1, 3)
+        .reshape(gain_rows, inner_dim),
     ]
-    used = sum(part.shape[1] for part in columns)
-    packed = jnp.concatenate(
-        [part.astype(jnp.bfloat16) for part in columns]
-        + [jnp.zeros((inner_dim, -used % LANES), jnp.bfloat16)],
-        axis=1,
-    )
-    summed = reduce_seq(reduce_rows(packed, 11, jnp.bfloat16), 12)
+    used = sum(part.shape[0] for part in lines)
+    columns = [g_select_weight, left_trans(d_step_low, step_low)]
+    spare = -(used + sum(part.shape[1] for part in columns)) % LANES
+    lines.append(jnp.zeros((spare, inner_dim), jnp.float32))
+    packed = jnp.concatenate(columns + [jnp.concatenate(lines, axis=0).T], axis=1)
+    conv_spread, summed = swap_and_reduce(
+        owner_blocks(d_conv_low), packed.astype(jnp.bfloat16), 11, (output_piece, attn_piece)
+    )
+    g_input_weight = reduce_rows(
+        jnp.concatenate(
+            [input_term(conv_spread, gathered_in), input_term(gate_spread, gathered_in)], axis=0
+        ),
+        13,
+    ).T
+    at = columns[0].shape[1]
+    small_select = summed[:, :at]
+    small_step = summed[:, at : at + rank_dim].T
+    tail = summed[:, at + rank_dim :]
+    small_lines = tail.T
     small = []
     at = 0
-    for part in columns:
-        small.append(summed[:, at : at + part.shape[1]])
-        at += part.shape[1]
-    gain_sums = small[7].reshape(4, -1)
+    for part in lines[:-1]:
+        small.append(small_lines[at : at + part.shape[0]])
+        at += part.shape[0]
+    gain_sums = (
+        small[5].reshape(gain_rows, -1, width // owners).reshape(4, width // owners)
+    )
     return (
         output[None],
         tokens_grad[None],
         gain_sums[0],
         g_input_weight,
-        small[3].T,
-        small[4][:, 0],
-        small[0],
-        small[1].T,
-        small[5][:, 0],
-        small[2],
-        small[6][:, 0],
+        small[1],
+        small[2][0],
+        small_select,
+        small_step,
+        small[3][0],
+        tail[:, :state_dim],
+        small[4][0],
         g_output_weight,
         gain_sums[1],
         g_attn_weight,

time: 1390 us -> 1190 us (0.86)
  Pallas kernels: 795 us -> 738 us
  waiting for transfers between devices: 58.9 us -> 19.6 us
  local copies, waits for them, and re-layouts: 156 us -> 123 us
  matrix products: 194 us -> 165 us
  starting transfers between devices: 52.2 us -> 30.2 us
  other arithmetic: 97.7 us -> 79.8 us
    pallas_call x6 -> x8, Pallas kernels: 208 us -> 286 us  [the longest x1 72 us: gather_seq(): pl.pallas_call(functools.partial(gather_seq_kernel, n_row, n_seq, parts),...]
    pallas_call x2 -> x1, Pallas kernels: 156 us -> 80.7 us  [reduce_seq(): pl.pallas_call(functools.partial(reduce_seq_kernel, n_seq, parts), out_sh...]
    pallas_call x6 -> x4, Pallas kernels: 122 us -> 81.9 us  [reduce_rows(): pl.pallas_call(functools.partial(reduce_rows_kernel, n_row, parts), out_s...]
    ppermute x2, waiting for transfers between devices: 27.5 us -> 0.01 us  [place_up_grad(): return lax.ppermute(grad, ('row', 'seq'), pairs)]
    dot_general x11 -> x7, matrix products: 58.3 us -> 32.6 us  [left_trans(): lax.dot_general(left_op, right_op, (((0,), (0,)), ((), ())), preferred_el...]
    ppermute x13 -> x0, waiting for transfers between devices: 24.5 us -> none  [the longest x6 24.5 us: swap_rows(): piece = lax.ppermute(piece, 'row', [(i, i ^ turn) for i in range(n_row)])]
    ppermute x13 -> x0, starting transfers between devices: 21.5 us -> none  [the longest x7 16.3 us: swap_seq_async(): piece = lax.ppermute(piece, 'seq', [(i, i ^ turn) for i in range(n_seq)])]
    reduce_scatter x0 -> x2, waiting for transfers between devices: none -> 19.4 us  [mlp_backward(): lax.psum_scatter(merged, 'seq', scatter_dimension=0, tiled=True, axis_ind...]
  transfers between devices with their start and end apart: 32 -> 17, of which waited for: 8 -> 1; matrix products, arithmetic and copies ran while one was open for 26% -> 23% of each run, Pallas kernels for 51% -> 43%
where the time goes in v3:
time: 1190 us; the launch traced here: 1180 us
  Pallas kernels  738 us (62%)
  matrix products  165 us (14%)
  local copies, waits for them, and re-layouts  123 us (10%)
  other arithmetic  79.8 us (7%)
  starting transfers between devices  30.2 us (3%)
  between operations  19.9 us (2%)
  waiting for transfers between devices  19.6 us (2%)
    dot_general x10, matrix products, right_trans(): lax.dot_general(left_op, right_op, (((1,), (1,)), ((), ())), preferred_el...  86.7 us
    pallas_call x4, Pallas kernels, reduce_rows(): pl.pallas_call(functools.partial(reduce_rows_kernel, n_row, parts), out_s...  81.9 us
    pallas_call x1, Pallas kernels, reduce_seq(): pl.pallas_call(functools.partial(reduce_seq_kernel, n_seq, parts), out_sh...  80.7 us
    pallas_call x1, Pallas kernels, gather_seq(): pl.pallas_call(functools.partial(gather_seq_kernel, n_row, n_seq, parts),...  72 us
    pallas_call x1, Pallas kernels, gather_input(): pl.pallas_call(functools.partial(gather_input_kernel, parts), out_shape=j...  67.9 us
    pallas_call x3, Pallas kernels, gather_rows(): pl.pallas_call(functools.partial(gather_rows_kernel, n_row, parts), out_s...  63.5 us
    unnamed x340, local copies, waits for them, and re-layouts  61.9 us
    pallas_call x1, Pallas kernels, swap_and_reduce(): pl.pallas_call(functools.partial(finish_kernel, n_row, n_seq, parts, len(...  58.3 us
  transfers between devices with their start and end apart: 17, of which 1 were waited for; matrix products, arithmetic and copies ran while one was open for 23% of the time, Pallas kernels for 43%

profile of v3, /device:TPU:6, one launch (start us, length us, event | category | flops | bytes accessed | tf_op | source)
XLA Modules:
  0.0 1175.8 jit_solution(13498438810967487270)
XLA Ops:
  9.7 67.9 %gather_input.1 = bf16[1536,6144]{1,0:T(8,128)(2,1)S(1)} custom-call(bf16[384,6144]{1,0:T(8,128)(2,1)S(1)} %copy-done.29), custom_call_target="tpu_custom_call" | custom-call | tf_op jit(solution)/shard_map/gather_input/pallas_call | solution.py:1317
  149.0 13.7 %scan_end.1 = f32[16,24,128]{2,1,0:T(8,128)S(1)} custom-call(f32[256,3072]{1,0:T(8,128)S(1)} %copy-done.4, bf16[256,3072]{1,0:T(8,128)(2,1)S(1)} %get-tuple-element.243.refs_1_.refs_2_.act_ref, f32[256,128]{1,0:T(8,128)S(1)} %broadcast_in_dim.56.refs_2_.refs_3_.keep_ref, f32[4096]{0:T(1024)S(1)} %reshape.337.refs_3_.refs_4_.in_ref, f32[16,24,128]{2,1,0:T(8,128)S(1)} %bitcast.168), custom_call_target="tpu_custom_call" | custom-call | tf_op jit(solution)/shard_map/scan_end/pallas_call | solution.py:136
  162.9 26.0 %exchange_states.1.refs_0_ = f32[16,24,128]{2,1,0:T(8,128)S(1)} custom-call(bf16[448,128]{1,0:T(8,128)(2,1)S(1)} %fusion.42.x_ref, f32[16,24,128]{2,1,0:T(8,128)S(1)} %bitcast.169), custom_call_target="tpu_custom_call" | custom-call | tf_op jit(solution)/shard_map/exchange_states/pallas_call | solution.py:1054
  192.6 19.5 %scan_out.1 = (f32[256,3072]{1,0:T(8,128)S(1)}, f32[8,16,24,128]{3,2,1,0:T(8,128)S(1)}) custom-call(f32[16,24,128]{2,1,0:T(8,128)S(1)} %exchange_states.1.refs_0_, f32[256,3072]{1,0:T(8,128)S(1)} %copy-done.5, bf16[256,3072]{1,0:T(8,128)(2,1)S(1)} %get-tuple-element.243.refs_1_.refs_2_.act_ref, f32[256,128]{1,0:T(8,128)S(1)} %broadcast_in_dim.56.refs_2_.refs_3_.keep_ref, ...), custom_call_target="tpu_custom_call" | custom-call | tf_op jit(solution)/shard_map/scan_out/pallas_call | solution.py:155
  223.0 21.1 %gather_rows.3.x_ref = bf16[1024,1536]{1,0:T(8,128)(2,1)S(1)} custom-call(bf16[256,1536]{1,0:T(8,128)(2,1)S(1)} %multiply_convert_fusion.7.x_ref), custom_call_target="tpu_custom_call" | custom-call | tf_op jit(solution)/shard_map/gather_rows/pallas_call | solution.py:713
  272.9 21.5 %reduce_rows.4 = f32[256,1536]{1,0:T(8,128)S(1)} custom-call(bf16[1024,1536]{1,0:T(8,128)(2,1)S(1)} %convolution_convert_fusion.5.x_ref), custom_call_target="tpu_custom_call" | custom-call | tf_op jit(solution)/shard_map/reduce_rows/pallas_call | solution.py:816
  298.2 72.0 %gather_seq.1 = (bf16[2048,1536]{1,0:T(8,128)(2,1)}, bf16[1536,2048]{1,0:T(8,128)(2,1)}) custom-call(bf16[256,1536]{1,0:T(8,128)(2,1)S(1)} %copy-done.33, bf16[2,384,8192]{2,1,0:T(8,128)(2,1)} %up_ref.1, bf16[2048,1536]{1,0:T(8,128)(2,1)} %all-gather.4.cloned.1.call-done.refs_0_), custom_call_target="tpu_custom_call" | custom-call | tf_op jit(solution)/shard_map/gather_seq/pallas_call | solution.py:909
  382.8 20.5 %attend.1 = (bf16[1024,384]{1,0:T(8,128)(2,1)S(1)}, f32[3,1024,1]{2,1,0:T(8,128)S(1)}) custom-call(s32[1]{0:T(128)} %bitcast.20.x_ref, s32[4]{0:T(128)S(1)} %get-tuple-element.290.low_ref, bf16[2048,1152]{1,0:T(8,128)(2,1)S(1)} %project_heads.1.q_ref.k_ref.v_ref, bf16[2048,1152]{1,0:T(8,128)(2,1)S(1)} %project_heads.1.q_ref.k_ref.v_ref, ...), custom_call_target="tpu_custom_call" | custom-call | flops 1610612736 | bytes 3145728 | tf_op jit(solution)/shard_map/attend/pallas_call | solution.py:470
  403.3 19.7 %collect_heads.1 = (bf16[256,1536]{1,0:T(8,128)(2,1)S(1)}, bf16[1024,768]{1,0:T(8,128)(2,1)S(1)}) custom-call(bf16[1024,384]{1,0:T(8,128)(2,1)S(1)} %get-tuple-element.59.x_ref.out_ref, bf16[256,3072]{1,0:T(8,128)(2,1)S(1)} %copy-done.26), custom_call_target="tpu_custom_call" | custom-call | tf_op jit(solution)/shard_map/collect_heads/pallas_call | solution.py:1165
  427.9 22.0 %gather_rows.4.x_ref = bf16[1024,1536]{1,0:T(8,128)(2,1)S(1)} custom-call(bf16[256,1536]{1,0:T(8,128)(2,1)S(1)} %multiply_convert_fusion.5.x_ref, bf16[1024,1536]{1,0:T(8,128)(2,1)S(1)} %copy-done.13), custom_call_target="tpu_custom_call" | custom-call | tf_op jit(solution)/shard_map/gather_rows/pallas_call | solution.py:713
  475.5 13.8 %grad_blocks.2 = bf16[3072,1536]{1,0:T(8,128)(2,1)} custom-call(bf16[1024,2048]{1,0:T(8,128)(2,1)S(1)} %pad_maximum_fusion.1.d_ref, bf16[1024,1536]{1,0:T(8,128)(2,1)S(1)} %gather_rows.4.x_ref, bf16[1024,1024]{1,0:T(8,128)(2,1)S(1)} %get-tuple-element.233.h_ref, bf16[1024,1536]{1,0:T(8,128)(2,1)S(1)} %copy-done.14), custom_call_target="tpu_custom_call" | custom-call | tf_op jit(solution)/shard_map/grad_blocks/pallas_call | solution.py:1339
  501.5 21.8 %reduce_rows.5 = f32[256,1536]{1,0:T(8,128)S(1)} custom-call(bf16[1024,1536]{1,0:T(8,128)(2,1)S(1)} %convolution_convert_fusion.3.x_ref), custom_call_target="tpu_custom_call" | custom-call | tf_op jit(solution)/shard_map/reduce_rows/pallas_call | solution.py:816
  535.4 29.4 %spread_heads.1 = (bf16[1024,384]{1,0:T(8,128)(2,1)S(1)}, bf16[1024,384]{1,0:T(8,128)(2,1)S(1)}, f32[256,1536]{1,0:T(8,128)S(1)}) custom-call(bf16[256,1536]{1,0:T(8,128)(2,1)S(1)} %convolution_convert_fusion.12.x_ref, bf16[256,1536]{1,0:T(8,128)(2,1)S(1)} %copy-done.50, bf16[1024,1536]{1,0:T(8,128)(2,1)S(1)} %convolution_convert_fusion.4.refs_0_), custom_call_target="tpu_custom_call" | custom-call | tf_op jit(solution)/shard_map/spread_heads/pallas_call | solution.py:1165
  566.9 29.5 %attend_back.1 = (bf16[1024,384]{1,0:T(8,128)(2,1)S(1)}, bf16[2048,384]{1,0:T(8,128)(2,1)S(1)}, bf16[2048,384]{1,0:T(8,128)(2,1)S(1)}) custom-call(s32[1]{0:T(128)} %bitcast.20.x_ref, s32[4]{0:T(128)S(1)} %get-tuple-element.290.low_ref, bf16[2048,1152]{1,0:T(8,128)(2,1)S(1)} %bitcast.167, bf16[2048,1152]{1,0:T(8,128)(2,1)S(1)} %bitcast.167, ...), custom_call_target="tpu_custom_call" | custom-call | flops 4026531840 | bytes 6291456 | tf_op jit(solution)/shard_map/attend_back/pallas_call | solution.py:559
  626.3 80.7 %reduce_seq.1 = f32[256,1536]{1,0:T(8,128)S(1)} custom-call(bf16[2048,1536]{1,0:T(8,128)(2,1)} %convolution_convert_fusion.1.x_ref, bf16[256,1536]{1,0:T(8,128)(2,1)S(1)} %slice.203.refs_0_, bf16[128,1536]{1,0:T(8,128)(2,1)S(1)} %get-tuple-element.267.refs_1_), custom_call_target="tpu_custom_call" | custom-call | tf_op jit(solution)/shard_map/reduce_seq/pallas_call | solution.py:983
  714.5 20.5 %gather_rows.5.u_ref = bf16[1024,1536]{1,0:T(8,128)(2,1)S(1)} custom-call(bf16[256,1536]{1,0:T(8,128)(2,1)S(1)} %copy-done.41, bf16[1024,1536]{1,0:T(8,128)(2,1)S(1)} %copy-done.36), custom_call_target="tpu_custom_call" | custom-call | tf_op jit(solution)/shard_map/gather_rows/pallas_call | solution.py:713
  747.0 13.8 %grad_blocks.3 = bf16[3072,1536]{1,0:T(8,128)(2,1)} custom-call(bf16[1024,2048]{1,0:T(8,128)(2,1)S(1)} %pad_maximum_fusion.2.d_ref, bf16[1024,1536]{1,0:T(8,128)(2,1)S(1)} %copy-done.16, bf16[1024,1024]{1,0:T(8,128)(2,1)S(1)} %copy-done.22, bf16[1024,1536]{1,0:T(8,128)(2,1)S(1)} %gather_rows.5.u_ref), custom_call_target="tpu_custom_call" | custom-call | tf_op jit(solution)/shard_map/grad_blocks/pallas_call | solution.py:1339
  780.8 21.5 %reduce_rows.6 = f32[256,1536]{1,0:T(8,128)S(1)} custom-call(bf16[1024,1536]{1,0:T(8,128)(2,1)S(1)} %convolution_convert_fusion.2.x_ref), custom_call_target="tpu_custom_call" | custom-call | tf_op jit(solution)/shard_map/reduce_rows/pallas_call | solution.py:816
  827.4 13.8 %adjoint_end.1 = f32[16,24,128]{2,1,0:T(8,128)S(1)} custom-call(f32[256,3072]{1,0:T(8,128)S(1)} %copy-done.6, f32[256,3072]{1,0:T(8,128)S(1)} %copy-done.12, f32[256,128]{1,0:T(8,128)S(1)} %broadcast_in_dim.56.refs_2_.refs_3_.keep_ref, f32[4096]{0:T(1024)S(1)} %reshape.340.refs_5_.read_ref, f32[16,24,128]{2,1,0:T(8,128)S(1)} %bitcast.171), custom_call_target="tpu_custom_call" | custom-call | tf_op jit(solution)/shard_map/adjoint_end/pallas_call | solution.py:215
  842.6 19.4 %reduce-scatter.9.cloned.1.call-done = bf16[384,1536]{1,0:T(8,128)(2,1)} async-done(((bf16[3072,1536]{1,0:T(8,128)(2,1)}), bf16[384,1536]{1,0:T(8,128)(2,1)}) %reduce-scatter.9.cloned.1.call-update) | async-done | bytes 1179664 | tf_op jit(solution)/shard_map/reduce_scatter | solution.py:1538
  868.0 52.5 %exchange_states_back.1 = (f32[16,24,128]{2,1,0:T(8,128)S(1)}, bf16[8,256,384]{2,1,0:T(8,128)(2,1)S(1)}, bf16[1024,1536]{1,0:T(8,128)(2,1)S(1)}) custom-call(bf16[448,128]{1,0:T(8,128)(2,1)S(1)} %copy-done.51, f32[16,24,128]{2,1,0:T(8,128)S(1)} %bitcast.172, bf16[8,256,384]{2,1,0:T(8,128)(2,1)S(1)} %copy-done.28, bf16[256,1536]{1,0:T(8,128)(2,1)S(1)} %copy-done.40, ...), custom_call_target="tpu_custom_call" | custom-call | tf_op jit(solution)/shard_map/exchange_states_back/pallas_call | solution.py:1063
  949.4 48.9 %adjoint_full.1 = (f32[256,3072]{1,0:T(8,128)}, f32[256,3072]{1,0:T(8,128)}, f32[4096,128]{1,0:T(8,128)S(1)}, f32[4096,128]{1,0:T(8,128)}, f32[16,24,128]{2,1,0:T(8,128)S(1)}) custom-call(f32[16,24,128]{2,1,0:T(8,128)S(1)} %copy-done.59, f32[8,16,24,128]{3,2,1,0:T(8,128)S(1)} %copy-done.44, f32[256,3072]{1,0:T(8,128)} %get-tuple-element.261.refs_0_.refs_1_.step_ref, ...), custom_call_target="tpu_custom_call" | custom-call | tf_op jit(solution)/shard_map/adjoint_full/pallas_call | solution.py:349
  1081.3 58.3 %swap_and_reduce.1 = (bf16[8,256,384]{2,1,0:T(8,128)(2,1)S(1)}, f32[96,256]{1,0:T(8,128)S(1)}) custom-call(bf16[8,256,384]{2,1,0:T(8,128)(2,1)S(1)} %copy-done.27, bf16[3072,256]{1,0:T(8,128)(2,1)S(1)} %pad_maximum_fusion.12.packed_ref, bf16[96,1536]{1,0:T(8,128)(2,1)S(1)} %get-tuple-element.274.refs_0_, bf16[48,1536]{1,0:T(8,128)(2,1)S(1)} %get-tuple-element.269.refs_1_), custom_call_target="tpu_custom_call" | custom-call | tf_op jit(solution)/shard_map/swap_and_reduce/pallas_call | solution.py:1224
  1147.0 17.1 %reduce_rows.7 = f32[192,1536]{1,0:T(8,128)S(1)} custom-call(bf16[768,1536]{1,0:T(8,128)(2,1)S(1)} %pad_maximum_fusion.6.x_ref), custom_call_target="tpu_custom_call" | custom-call | tf_op jit(solution)/shard_map/reduce_rows/pallas_call | solution.py:816
  (565 shorter events, 410.9 us)
Async XLA Ops:
  7.2 134.0 %copy-start = (bf16[3072,128]{1,0:T(8,128)(2,1)S(1)}, bf16[3072,128]{1,0:T(8,128)(2,1)}, u32[]{:S(2)}) copy-start(bf16[3072,128]{1,0:T(8,128)(2,1)} %param.30) | copy-start | bytes 2359300
  7.2 289.7 %all-gather.4.cloned.1.call-start = ((), (), s32[]{:S(2)}) async-start(), calls=%async_computation.4 | async-start | bytes 7077888 | tf_op jit(solution)/shard_map/all_gather | solution.py:1662
  86.2 339.7 %all-gather.6.cloned.1.call-start = ((), (), s32[]{:S(2)}) async-start(), calls=%async_computation.5 | async-start | bytes 3932160 | tf_op jit(solution)/shard_map/all_gather | solution.py:1665
  91.5 152.6 %collective-permute-start.1 = (bf16[384,2048]{1,0:T(8,128)(2,1)}, bf16[384,2048]{1,0:T(8,128)(2,1)}, u32[]{:S(2)}, u32[]{:S(2)}) collective-permute-start(bf16[384,2048]{1,0:T(8,128)(2,1)} %pad_maximum_fusion.9), channel_id=1, source_target_pairs={{0,8},{8,0},{16,24},{24,16},{1,9},{9,1},{17,25},{25,17},{2,10},{10... | collective-permute-start | bytes 4718600 | tf_op jit(solution)/shard_map/ppermute | solution.py:1479
  93.1 154.9 %collective-permute-start.2 = (bf16[384,2048]{1,0:T(8,128)(2,1)}, bf16[384,2048]{1,0:T(8,128)(2,1)}, u32[]{:S(2)}, u32[]{:S(2)}) collective-permute-start(bf16[384,2048]{1,0:T(8,128)(2,1)} %pad_maximum_fusion.10), channel_id=1, source_target_pairs={{0,16},{8,24},{16,0},{24,8},{1,17},{9,25},{17,1},{25,9},{2,18},{10... | collective-permute-start | bytes 4718600 | tf_op jit(solution)/shard_map/ppermute | solution.py:1479
  95.9 154.9 %collective-permute-start.3 = (bf16[384,2048]{1,0:T(8,128)(2,1)}, bf16[384,2048]{1,0:T(8,128)(2,1)}, u32[]{:S(2)}, u32[]{:S(2)}) collective-permute-start(bf16[384,2048]{1,0:T(8,128)(2,1)} %pad_maximum_fusion.11), channel_id=1, source_target_pairs={{0,24},{8,16},{16,8},{24,0},{1,25},{9,17},{17,9},{25,1},{2,26},{10... | collective-permute-start | bytes 4718600 | tf_op jit(solution)/shard_map/ppermute | solution.py:1479
  104.7 26.8 %collective-permute-start = (bf16[3,3072]{1,0:T(4,128)(2,1)S(1)}, bf16[3,3072]{1,0:T(4,128)(2,1)S(1)}, u32[]{:S(2)}, u32[]{:S(2)}) collective-permute-start(bf16[3,3072]{1,0:T(4,128)(2,1)S(1)} %slice.311), channel_id=1, source_target_pairs={{0,1},{1,2},{2,3},{3,4},{4,5},{5,6},{6,7},{8,9},{9,10},{10,11},{11... | collective-permute-start | bytes 55304 | tf_op jit(solution)/shard_map/ppermute | solution.py:27
  109.0 514.0 %reduce-scatter.5.cloned.1.call-start = ((), (), s32[]{:S(2)}) async-start(), calls=%async_computation.6 | async-start | bytes 10616832 | tf_op jit(solution)/shard_map/reduce_scatter | solution.py:1538
  126.4 96.4 %copy-start.111 = (f32[1536]{0:T(1024)}, f32[1536]{0:T(1024)S(1)}, u32[]{:S(2)}) copy-start(f32[1536]{0:T(1024)S(1)} %get-tuple-element.218) | copy-start | bytes 18436
  130.5 81.7 %copy-start.120 = (f32[3072]{0:T(1024)}, f32[3072]{0:T(1024)S(1)}, u32[]{:S(2)}) copy-start(f32[3072]{0:T(1024)S(1)} %convert_element_type.264) | copy-start | bytes 36868
  192.6 630.9 %copy-start.54 = (f32[4096]{0:T(1024)}, f32[4096]{0:T(1024)S(1)}, u32[]{:S(2)}) copy-start(f32[4096]{0:T(1024)S(1)} %reshape.340.refs_5_.read_ref) | copy-start | bytes 49156
  298.2 124.9 %slice-start.6 = ((s8[4718592]{0:T(1024)(128)(4,1)}), s8[524288]{0:T(1024)(128)(4,1)S(1)}, s32[]{:S(2)}) async-start(s8[4718592]{0:T(1024)(128)(4,1)} %bitcast.208), calls=%async_computation.17 | async-start | bytes 1048576
  491.3 220.2 %all-gather.8.cloned.1.call-start = ((), (), s32[]{:S(2)}) async-start(), calls=%async_computation.7 | async-start | bytes 3932160 | tf_op jit(solution)/shard_map/all_gather | solution.py:1745
  525.1 237.6 %reduce-scatter.7.cloned.1.call-start = ((), (), s32[]{:S(2)}) async-start(), calls=%async_computation.8 | async-start | bytes 3981312 | tf_op jit(solution)/shard_map/reduce_scatter | solution.py:1777
  609.6 252.4 %reduce-scatter.9.cloned.1.call-start = ((), (), s32[]{:S(2)}) async-start(), calls=%async_computation.9 | async-start | bytes 10616832 | tf_op jit(solution)/shard_map/reduce_scatter | solution.py:1538
  624.2 82.8 %copy-start.37 = (bf16[256,1536]{1,0:T(8,128)(2,1)}, bf16[256,1536]{1,0:T(8,128)(2,1)S(1)}, u32[]{:S(2)}) copy-start(bf16[256,1536]{1,0:T(8,128)(2,1)S(1)} %slice.203.refs_0_) | copy-start | bytes 2359300
  626.3 81.3 %copy-start.85 = (bf16[1,256,1536]{2,1,0:T(8,128)(2,1)S(1)}, bf16[1,256,1536]{2,1,0:T(8,128)(2,1)}, u32[]{:S(2)}) copy-start(bf16[1,256,1536]{2,1,0:T(8,128)(2,1)} %param.43) | copy-start | bytes 2359300
  762.8 313.6 %reduce-scatter.11.cloned.1.call-start = ((), (), s32[]{:S(2)}) async-start(), calls=%async_computation.10 | async-start | bytes 3981312 | tf_op jit(solution)/shard_map/reduce_scatter | solution.py:1388
  920.6 148.9 %collective-permute-start.8 = (bf16[256,1536]{1,0:T(8,128)(2,1)}, bf16[256,1536]{1,0:T(8,128)(2,1)}, u32[]{:S(2)}, u32[]{:S(2)}) collective-permute-start(bf16[256,1536]{1,0:T(8,128)(2,1)} %slice.205.refs_2_), channel_id=1, source_target_pairs={{0,0},{1,1},{2,2},{3,3},{4,16},{5,17},{6,18},{7,19},{8,20},{9,21},... | collective-permute-start | bytes 2359304 | tf_op jit(solution)/shard_map/ppermute | solution.py:1510
  922.6 147.0 %collective-permute-start.9 = (bf16[256,1536]{1,0:T(8,128)(2,1)S(1)}, bf16[256,1536]{1,0:T(8,128)(2,1)}, u32[]{:S(2)}, u32[]{:S(2)}) collective-permute-start(bf16[256,1536]{1,0:T(8,128)(2,1)S(1)} %copy-done.38), channel_id=1, source_target_pairs={{0,0},{1,1},{2,2},{3,3},{4,16},{5,17},{6,18},{7,19},{8,20},{9,21},... | collective-permute-start | bytes 2359304 | tf_op jit(solution)/shard_map/ppermute | solution.py:1510
  932.1 134.5 %collective-permute-start.5 = (bf16[48,1536]{1,0:T(8,128)(2,1)}, bf16[48,1536]{1,0:T(8,128)(2,1)}, u32[]{:S(2)}, u32[]{:S(2)}) collective-permute-start(bf16[48,1536]{1,0:T(8,128)(2,1)} %get-tuple-element.272), channel_id=1, source_target_pairs={{0,0},{2,3},{4,6},{6,8},{8,1},{10,4},{12,7},{14,9},{24,2},{26,5},{... | collective-permute-start | bytes 442376 | tf_op jit(solution)/shard_map/ppermute | solution.py:1598
  934.0 133.6 %collective-permute-start.6 = (bf16[48,1536]{1,0:T(8,128)(2,1)}, bf16[48,1536]{1,0:T(8,128)(2,1)}, u32[]{:S(2)}, u32[]{:S(2)}) collective-permute-start(bf16[48,1536]{1,0:T(8,128)(2,1)} %get-tuple-element.271), channel_id=1, source_target_pairs={{0,0},{2,3},{4,5},{6,8},{8,1},{10,4},{12,6},{14,9},{24,2},{26,13},... | collective-permute-start | bytes 442376 | tf_op jit(solution)/shard_map/ppermute | solution.py:1598
  1024.2 12.6 %collective-permute-start.4 = (bf16[3,3072]{1,0:T(4,128)(2,1)}, bf16[3,3072]{1,0:T(4,128)(2,1)S(1)}, u32[]{:S(2)}, u32[]{:S(2)}) collective-permute-start(bf16[3,3072]{1,0:T(4,128)(2,1)} %slice.310), channel_id=1, source_target_pairs={{1,0},{2,1},{3,2},{4,3},{5,4},{6,5},{7,6},{9,8},{10,9},{11,10},{12... | collective-permute-start | bytes 55304 | tf_op jit(solution)/shard_map/ppermute | solution.py:27
  1036.9 31.6 %collective-permute-start.7 = (bf16[48,1536]{1,0:T(8,128)(2,1)}, bf16[48,1536]{1,0:T(8,128)(2,1)S(1)}, u32[]{:S(2)}, u32[]{:S(2)}) collective-permute-start(bf16[48,1536]{1,0:T(8,128)(2,1)} %get-tuple-element.270), channel_id=1, source_target_pairs={{0,0},{2,2},{4,5},{6,8},{8,1},{10,3},{12,6},{14,9},{24,10},{26,4},... | collective-permute-start | bytes 442376 | tf_op jit(solution)/shard_map/ppermute | solution.py:1598
  (159 other events, 2347.1 us)
Sparse Core Ops, SparseCore 0:
  86.4 68.8 all-gather.3
  156.8 28.1 all-gather.5
  491.4 111.6 reduce-scatter.4
  605.1 30.8 all-gather.7
  638.2 59.2 reduce-scatter.6
  762.9 99.0 reduce-scatter.8
  946.4 94.6 reduce-scatter.10

commit v4 on v3

--- a/solution.py
+++ b/solution.py
@@ -227,11 +227,13 @@
 
 
 def adjoint_full_kernel(
-    states, chunk,
-    end_ref, marks_ref, step_ref, act_ref, grad_ref, keep_ref, in_ref, read_ref, decay_ref,
+    states, chunk, anchors,
+    end_ref, marks_ref, step_ref, act_ref, grad_ref, keep_ref, in_ref, read_ref, decay_ref, *refs
+):
+    (
     d_step_ref, d_act_ref, d_in_ref, d_read_ref, d_decay_ref,
     carry_ref, step_t, rate_t, act_t, grad_t, d_step_t, d_act_t, factor_t, held_t, in_t, read_t,
-):
+    ) = refs[anchors:]
     index = pl.program_id(0)
     last = pl.num_programs(0) - 1
     groups = step_ref.shape[1] // (8 * LANES)
@@ -337,7 +339,7 @@
     lax.fori_loop(0, chunk * states // 8, shrink, 0, unroll=4)
 
 
-def adjoint_full(end_grad, marks, step, act, grad, keep_lanes, in_flat, read_flat, decay):
+def adjoint_full(end_grad, marks, step, act, grad, keep_lanes, in_flat, read_flat, decay, after=()):
     rows, inner = step.shape
     states, planes, _ = decay.shape
     chunk = CHUNK
@@ -347,7 +349,7 @@
     maps = pl.BlockSpec((chunk * states, LANES), lambda i: (count - 1 - i, 0))
     big = pltpu.VMEM((chunk * states * 8, LANES), jnp.float32)
     return pl.pallas_call(
-        functools.partial(adjoint_full_kernel, states, chunk),
+        functools.partial(adjoint_full_kernel, states, chunk, len(after)),
         out_shape=(
             jax.ShapeDtypeStruct((rows, inner), jnp.float32),
             jax.ShapeDtypeStruct((rows, inner), jnp.float32),
@@ -362,14 +364,15 @@
             rowed, rowed, rowed,
             pl.BlockSpec((chunk, LANES), lambda i: (count - 1 - i, 0)),
             smem(), smem(), whole,
-        ],
+        ]
+        + [pl.BlockSpec(memory_space=pl.ANY)] * len(after),
         out_specs=(rowed, rowed, maps, maps, whole),
         scratch_shapes=[pltpu.VMEM(decay.shape, jnp.float32)]
         + [pltpu.VMEM((chunk * 8, LANES), jnp.float32)] * 6
         + [big] * 4,
         compiler_params=pltpu.CompilerParams(vmem_limit_bytes=48 << 20),
         name="adjoint_full",
-    )(end_grad, marks, step, act, grad, keep_lanes, in_flat, read_flat, decay)
+    )(end_grad, marks, step, act, grad, keep_lanes, in_flat, read_flat, decay, *after)
 
 
 KEYS = 512
@@ -648,12 +651,6 @@
     return pl.BlockSpec(memory_space=pltpu.VMEM)
 
 
-def gather_rows_kernel(n_row, parts, x_ref, *refs):
-    sibling, across = row_peers(n_row)
-    greet([sibling] + across)
-    finish_gather_rows(start_gather_rows(n_row, parts, x_ref, *refs[-6:]))
-
-
 def start_gather_rows(n_row, parts, x_ref, out_ref, send_y, recv_y, send_f, recv_f, own_sem):
     row, seq = lax.axis_index("row"), lax.axis_index("seq")
     y, core = row // 2, lax.rem(row, 2)
@@ -705,20 +702,64 @@
     return [pltpu.SemaphoreType.DMA((n_y - 1, parts))] * 4 + [pltpu.SemaphoreType.DMA((2,))]
 
 
-def gather_rows(block, after=(), collective=1):
-    n_row = lax.axis_size("row")
-    rows, width = block.shape
-    parts = 4 if rows % 64 == 0 else 1
-    n_y = n_row // 2
-    return pl.pallas_call(
-        functools.partial(gather_rows_kernel, n_row, parts),
-        out_shape=jax.ShapeDtypeStruct((n_row * rows, width), block.dtype),
-        in_specs=[vmem()] + [anywhere()] * len(after),
-        out_specs=vmem(),
-        scratch_shapes=gather_rows_scratch(n_y, parts),
-        compiler_params=remote_params(collective + len(after), 40),
-        name="gather_rows",
-    )(block, *after)
+def owner_of(row, seq, n_row, n_seq):
+    half = n_seq // 2
+    late, odd = seq // half, lax.rem(row, 2)
+    moved = late + odd - 2 * late * odd
+    owner_seq = (1 - moved) * seq + moved * (odd * half + lax.rem(seq, half))
+    return moved * (n_row // 2) + row // 2, owner_seq
+
+
+def holder_of(row, seq, n_row, n_seq):
+    half = n_seq // 2
+    raised, late = row // (n_row // 2), seq // half
+    holder_seq = (1 - raised) * seq + raised * ((1 - late) * half + lax.rem(seq, half))
+    return 2 * (row - raised * (n_row // 2)) + late, holder_seq
+
+
+def greet_riders(peers, n_row, n_seq):
+    row, seq = lax.axis_index("row"), lax.axis_index("seq")
+    target, source = owner_of(row, seq, n_row, n_seq), holder_of(row, seq, n_row, n_seq)
+    staying = jnp.logical_and(target[0] == row, target[1] == seq)
+    barrier = pltpu.get_barrier_semaphore()
+    for peer in peers:
+        pl.semaphore_signal(barrier, inc=1, device_id=peer, device_id_type=MESH)
+
+    @pl.when(jnp.logical_not(staying))
+    def _():
+        pl.semaphore_signal(barrier, inc=1, device_id=source, device_id_type=MESH)
+
+    pl.semaphore_wait(barrier, len(peers) + 1 - staying.astype(jnp.int32))
+
+
+def start_ride(n_row, n_seq, ride_ref, rode_ref, ride_sem):
+    row, seq = lax.axis_index("row"), lax.axis_index("seq")
+    target = owner_of(row, seq, n_row, n_seq)
+    staying = jnp.logical_and(target[0] == row, target[1] == seq)
+    ride = send(ride_ref, rode_ref, ride_sem.at[0], ride_sem.at[1], target)
+    keep = pltpu.make_async_copy(ride_ref, rode_ref, ride_sem.at[2])
+
+    @pl.when(jnp.logical_not(staying))
+    def _():
+        ride.start()
+
+    @pl.when(staying)
+    def _():
+        keep.start()
+
+    return staying, ride, keep
+
+
+def finish_ride(started):
+    staying, ride, keep = started
+
+    @pl.when(jnp.logical_not(staying))
+    def _():
+        ride.wait()
+
+    @pl.when(staying)
+    def _():
+        keep.wait()
 
 
 def row_peers(n_row):
@@ -730,10 +771,12 @@
     return sibling, across
 
 
-def reduce_rows_kernel(n_row, parts, x_ref, out_ref, *scratch):
+def reduce_rows_kernel(n_row, n_seq, parts, x_ref, ride_ref, out_ref, rode_ref, ride_sem, *scratch):
     sibling, across = row_peers(n_row)
-    greet([sibling] + across)
+    greet_riders([sibling] + across, n_row, n_seq)
+    ridden = start_ride(n_row, n_seq, ride_ref, rode_ref, ride_sem)
     reduce_rows_body(n_row, parts, x_ref, out_ref, *scratch)
+    finish_ride(ridden)
 
 
 def reduce_rows_body(
@@ -807,21 +850,24 @@
     )
 
 
-def reduce_rows(partial, collective=14, dtype=jnp.float32):
-    n_row = lax.axis_size("row")
-    n_y = n_row // 2
+def reduce_rows(partial, ride, collective):
+    n_row, n_seq = lax.axis_size("row"), lax.axis_size("seq")
     rows, width = partial.shape[0] // n_row, partial.shape[1]
     parts = 4 if rows % 64 == 0 else 2 if rows % 32 == 0 else 1
     buffer = (rows, width)
     return pl.pallas_call(
-        functools.partial(reduce_rows_kernel, n_row, parts),
-        out_shape=jax.ShapeDtypeStruct(buffer, dtype),
-        in_specs=[vmem()],
-        out_specs=vmem(),
-        scratch_shapes=reduce_rows_scratch(n_y, parts, buffer, partial.dtype),
+        functools.partial(reduce_rows_kernel, n_row, n_seq, parts),
+        out_shape=(
+            jax.ShapeDtypeStruct(buffer, jnp.float32),
+            jax.ShapeDtypeStruct(ride.shape, ride.dtype),
+        ),
+        in_specs=[vmem(), anywhere()],
+        out_specs=(vmem(), anywhere()),
+        scratch_shapes=[pltpu.SemaphoreType.DMA((3,))]
+        + reduce_rows_scratch(n_row // 2, parts, buffer, partial.dtype),
         compiler_params=remote_params(collective, 40),
         name="reduce_rows",
-    )(partial)
+    )(partial, ride)
 
 
 def ring_neighbours(n_seq):
@@ -901,7 +947,7 @@
         copy.wait()
 
 
-def gather_seq(block, up_weight, after=(), collective=3):
+def gather_seq(block, up_weight, after=(), collective=15):
     n_row, n_seq = lax.axis_size("row"), lax.axis_size("seq")
     rows, width = block.shape
     parts = 2 if rows % 64 == 0 else 1
@@ -1202,12 +1248,27 @@
     n_row, n_seq, parts, anchors, blocks_ref, packed_ref, *refs
 ):
     spread_ref, out_ref, send_b, recv_b, rowed, held, send_s, recv_s, *scratch = refs[anchors:]
+    rows = out_ref.shape[0]
     row, seq = lax.axis_index("row"), lax.axis_index("seq")
     sibling, across = row_peers(n_row)
     greet([sibling] + across + [(row, lax.rem(seq + d, n_seq)) for d in range(1, n_seq)])
     swapped = start_swap(n_seq, blocks_ref, spread_ref, send_b, recv_b)
     reduce_rows_body(n_row, parts, packed_ref, rowed, *scratch)
-    reduce_seq_body(n_seq, 1, rowed, out_ref, held, send_s, recv_s)
+    spread = []
+    for d in range(1, n_seq):
+        peer = lax.rem(seq + d, n_seq)
+        copy = send(
+            rowed.at[span(peer * rows, rows)], held.at[d - 1], send_s.at[d - 1], recv_s.at[d - 1], (row, peer)
+        )
+        copy.start()
+        spread.append(copy)
+    total = rowed[span(seq * rows, rows), :].astype(jnp.float32)
+    for d, copy in enumerate(spread):
+        copy.wait_recv()
+        total = total + held[d].astype(jnp.float32)
+    out_ref[...] = total
+    for copy in spread:
+        copy.wait_send()
     for copy in swapped:
         copy.wait()
 
@@ -1215,7 +1276,7 @@
 def swap_and_reduce(blocks, packed, collective, after=()):
     n_row, n_seq = lax.axis_size("row"), lax.axis_size("seq")
     rows, width = packed.shape[0] // (n_row * n_seq), packed.shape[1]
-    if rows % 32:
+    if rows % 16:
         summed = lax.psum_scatter(packed, ("row", "seq"), scatter_dimension=0, tiled=True)
         return swap_seq(blocks, collective), summed.astype(jnp.float32)
     buffer = (n_seq * rows, width)
@@ -1232,9 +1293,9 @@
         scratch_shapes=[sem((n_seq - 1,))] * 2
         + [
             pltpu.VMEM(buffer, packed.dtype),
-            pltpu.VMEM((2, n_seq - 1, rows // 2, width), packed.dtype),
+            pltpu.VMEM((n_seq - 1, rows, width), packed.dtype),
         ]
-        + [sem((2, n_seq - 1, 1))] * 2
+        + [sem((n_seq - 1,))] * 2
         + reduce_rows_scratch(n_row // 2, parts, buffer, packed.dtype),
         compiler_params=remote_params(collective, 32),
         name="swap_and_reduce",
@@ -1325,31 +1386,305 @@
     )(shard)
 
 
-def grad_blocks_kernel(up_rows, d_ref, x_ref, h_ref, u_ref, out_ref):
+def grad_blocks_kernel(up_rows, down_rows, d_ref, x_ref, h_ref, u_ref, *refs):
+    out_ref = refs[-1]
+    both = up_rows + down_rows
     out_ref[:up_rows, :] = left_trans(d_ref[...], x_ref[...]).astype(out_ref.dtype)
-    out_ref[up_rows:, :] = left_trans(h_ref[...], u_ref[...]).astype(out_ref.dtype)
-
-
-def grad_blocks(d_gate_up, spread, hidden, upstream):
+    out_ref[up_rows:both, :] = left_trans(h_ref[...], u_ref[...]).astype(out_ref.dtype)
+    if len(refs) > 1:
+        out_ref[both:, :] = refs[0][0]
+
+
+def grad_blocks(d_gate_up, spread, hidden, upstream, extra=()):
     n_seq = lax.axis_size("seq")
     n_x = n_seq // GROUPS
     tokens, width = spread.shape
     up_rows, down_rows = d_gate_up.shape[1] // n_seq, hidden.shape[1] // n_seq
+    rows = up_rows + down_rows + sum(part.shape[1] for part in extra)
     whole = pl.BlockSpec((tokens, width), lambda k: (0, 0))
     return pl.pallas_call(
-        functools.partial(grad_blocks_kernel, up_rows),
-        out_shape=jax.ShapeDtypeStruct((n_seq * (up_rows + down_rows), width), jnp.bfloat16),
+        functools.partial(grad_blocks_kernel, up_rows, down_rows),
+        out_shape=jax.ShapeDtypeStruct((n_seq * rows, width), jnp.bfloat16),
         grid=(n_seq,),
         in_specs=[
             pl.BlockSpec((tokens, up_rows), lambda k: (0, ring_member(k, n_x))),
             whole,
             pl.BlockSpec((tokens, down_rows), lambda k: (0, ring_member(k, n_x))),
             whole,
+        ]
+        + [
+            pl.BlockSpec((1,) + part.shape[1:], lambda k: (ring_member(k, n_x), 0, 0))
+            for part in extra
         ],
-        out_specs=pl.BlockSpec((up_rows + down_rows, width), lambda k: (k, 0)),
-        compiler_params=pltpu.CompilerParams(vmem_limit_bytes=40 << 20),
+        out_specs=pl.BlockSpec((rows, width), lambda k: (k, 0)),
+        compiler_params=pltpu.CompilerParams(vmem_limit_bytes=44 << 20),
         name="grad_blocks",
-    )(d_gate_up, spread, hidden, upstream)
+    )(d_gate_up, spread, hidden, upstream, *extra)
+
+
+UNITS = 256
+COLUMNS = 512
+
+
+def mlp_kernel(mode, n_row, n_seq, parts, anchors, *refs):
+    forward, both = mode == "forward", mode == "both"
+    refs = list(refs)
+
+    def take(count):
+        taken = refs[:count]
+        del refs[:count]
+        return taken
+
+    block_ref, up_ref, down_ref = take(3)
+    if both:
+        (back_ref,) = take(1)
+    elif not forward:
+        gate_ref, raise_ref, ride_ref = take(3)
+    take(anchors)
+    if forward:
+        all_ref, sum_ref, hidden_ref, gate_ref, raise_ref = take(5)
+    elif both:
+        all_ref, sum_ref, hidden_ref, slope_ref, out_ref = take(5)
+    else:
+        all_ref, sum_ref, slope_ref, rode_ref = take(4)
+        back_ref = all_ref
+    up, down, local_sem, part, near, stage, far, values_t, back_t, unit_t = take(10)
+    send_c, recv_c, send_t, recv_t = take(4)
+    gather_scratch = take(5)
+    send_y, recv_y, send_f, recv_f, _ = gather_scratch
+    riding = not forward and not both
+    if riding:
+        (ride_sem,) = take(1)
+
+    row, seq = lax.axis_index("row"), lax.axis_index("seq")
+    y, core = row // 2, lax.rem(row, 2)
+    n_y = n_row // 2
+    rows = block_ref.shape[0]
+    piece = rows // parts
+    width = block_ref.shape[1]
+    units = down.shape[0]
+    sibling, across = row_peers(n_row)
+    beside = y * 2 + 1 - core
+    if riding:
+        greet_riders([sibling] + across, n_row, n_seq)
+    else:
+        greet([sibling] + across)
+    if riding:
+        ridden = start_ride(n_row, n_seq, ride_ref, rode_ref, ride_sem)
+    loads = [
+        pltpu.make_async_copy(up_ref, up, local_sem.at[0]),
+        pltpu.make_async_copy(down_ref, down, local_sem.at[1]),
+    ]
+    for load in loads:
+        load.start()
+    started = start_gather_rows(n_row, parts, block_ref, all_ref, *gather_scratch)
+    pending, own = started[5], started[6]
+    for load in loads:
+        load.wait()
+
+    def work(offsets, size):
+        spans = [span(offset, size) for offset in offsets]
+        many = len(offsets) * size
+        used = pl.ds(0, many)
+
+        def joined(ref, cols):
+            return jnp.concatenate([ref[here, cols] for here in spans], axis=0)
+
+        def divided(ref, cols, value):
+            for i, here in enumerate(spans):
+                ref[here, cols] = value[i * size : (i + 1) * size]
+
+        for i, here in enumerate(spans):
+            values_t[pl.ds(i * size, size), :] = all_ref[here, :]
+            if both:
+                back_t[pl.ds(i * size, size), :] = back_ref[here, :]
+        back = back_t if both else values_t
+
+        def unit(j, _):
+            at = pl.multiple_of(j * UNITS, UNITS)
+            low = pl.ds(at, UNITS)
+            gate_cols = pl.ds(pl.multiple_of(core * units + at, UNITS), UNITS)
+            up_cols = pl.ds(pl.multiple_of((1 - core) * units + at, UNITS), UNITS)
+            if forward or both:
+                gate = product(values_t[used, :], up[:, gate_cols])
+                raised = product(values_t[used, :], up[:, up_cols])
+            else:
+                gate, raised = joined(gate_ref, low), joined(raise_ref, low)
+            share = 1.0 / (1.0 + jnp.exp(-gate))
+            active = gate * share
+            if forward or both:
+                hidden = (active * raised).astype(hidden_ref.dtype)
+                divided(hidden_ref, low, hidden)
+            if forward:
+                unit_t[used, low] = hidden
+                divided(gate_ref, low, gate)
+                divided(raise_ref, low, raised)
+            else:
+                d_hidden = right_trans(back[used, :], down[low, :])
+                d_gate = d_hidden * raised * share * (1.0 + gate * (1.0 - share))
+                d_gate = d_gate.astype(slope_ref.dtype)
+                d_raised = (d_hidden * active).astype(slope_ref.dtype)
+                unit_t[used, gate_cols] = d_gate
+                unit_t[used, up_cols] = d_raised
+                divided(slope_ref, gate_cols, d_gate)
+                divided(slope_ref, up_cols, d_raised)
+            return 0
+
+        lax.fori_loop(0, units // UNITS, unit, 0)
+
+        def column(j, _):
+            cols = pl.ds(pl.multiple_of(j * COLUMNS, COLUMNS), COLUMNS)
+            if forward:
+                total = product(unit_t[used, :], down[:, cols])
+            else:
+                total = right_trans(unit_t[used, :], up[cols, :])
+            divided(part, cols, total.astype(part.dtype))
+            return 0
+
+        lax.fori_loop(0, width // COLUMNS, column, 0)
+
+    def to_sibling(d, block, c):
+        return send(
+            part.at[span(block * rows + c * piece, piece)],
+            near.at[d, span(c * piece, piece)],
+            send_c.at[d, c],
+            recv_c.at[d, c],
+            sibling,
+        )
+
+    def to_far(d, c):
+        where = span(c * piece, piece)
+        return send(
+            stage.at[d - 1, where],
+            far.at[d - 1, where],
+            send_t.at[d - 1, c],
+            recv_t.at[d - 1, c],
+            across[d - 1],
+        )
+
+    def forwarded(d, block, c):
+        where = all_ref.at[span(block * rows + c * piece, piece)]
+        return send(where, where, send_f.at[d, c], recv_f.at[d, c], sibling)
+
+    def arriving(d, c):
+        return send(
+            block_ref.at[span(c * piece, piece)],
+            all_ref.at[span(row * rows + c * piece, piece)],
+            send_y.at[d, c],
+            recv_y.at[d, c],
+            across[d],
+        )
+
+    own.wait_recv()
+    work([row * rows, beside * rows], rows)
+    for c in range(parts):
+        to_sibling(0, beside, c).start()
+    for d in range(n_y - 1):
+        shift = n_y - 1 - d
+        there = lax.rem(y + shift, n_y) * 2
+
+        def far_step(c, _, d=d, shift=shift, there=there):
+            arriving(d, c).wait_recv()
+            forwarded(d, there + core, c).start()
+            forwarded(d, there + core, c).wait_recv()
+            work([(there + core) * rows + c * piece, (there + 1 - core) * rows + c * piece], piece)
+            to_sibling(shift, there + 1 - core, c).start()
+            to_sibling(shift, there + 1 - core, c).wait_recv()
+            where = span(c * piece, piece)
+            total = part[span((there + core) * rows + c * piece, piece), :].astype(
+                jnp.float32
+            ) + near[shift, where, :].astype(jnp.float32)
+            stage[shift - 1, where, :] = total.astype(stage.dtype)
+            to_far(shift, c).start()
+            return 0
+
+        lax.fori_loop(0, parts, far_step, 0)
+
+    if both:
+
+        def result(i, _):
+            here = span(i * rows, rows)
+
+            def column(j, _):
+                cols = pl.ds(pl.multiple_of(j * COLUMNS, COLUMNS), COLUMNS)
+                out_ref[here, cols] = product(hidden_ref[here, :], down[:, cols]).astype(
+                    out_ref.dtype
+                )
+                return 0
+
+            lax.fori_loop(0, width // COLUMNS, column, 0)
+            return 0
+
+        lax.fori_loop(0, n_row, result, 0)
+
+    def last(c, _):
+        where = span(c * piece, piece)
+        to_sibling(0, beside, c).wait()
+        total = part[span(row * rows + c * piece, piece), :].astype(jnp.float32) + near[
+            0, where, :
+        ].astype(jnp.float32)
+        for d in range(n_y - 1):
+            to_far(d + 1, c).wait()
+            total = total + far[d, where, :].astype(jnp.float32)
+        sum_ref[where, :] = total
+        for d in range(n_y - 1):
+            shift = n_y - 1 - d
+            there = lax.rem(y + shift, n_y) * 2
+            to_sibling(shift, there + 1 - core, c).wait_send()
+            forwarded(d, there + core, c).wait_send()
+            arriving(d, c).wait_send()
+        return 0
+
+    lax.fori_loop(0, parts, last, 0)
+    own.wait_send()
+    if riding:
+        finish_ride(ridden)
+
+
+def mlp_fused(mode, block, up_own, down_own, extra, after, collective, ride=()):
+    n_row, n_seq = lax.axis_size("row"), lax.axis_size("seq")
+    n_y = n_row // 2
+    rows, width = block.shape
+    units = down_own.shape[0]
+    parts = 2
+    total = n_row * rows
+    low, high = jnp.bfloat16, jnp.float32
+    shapes = [((total, width), low), ((rows, width), high)]
+    if mode == "forward":
+        shapes += [((total, units), low), ((total, units), high), ((total, units), high)]
+    elif mode == "both":
+        shapes += [((total, units), low), ((total, 2 * units), low), ((total, width), low)]
+    else:
+        shapes += [((total, 2 * units), low)]
+    shapes += [(rider.shape, rider.dtype) for rider in ride]
+    sem = pltpu.SemaphoreType.DMA
+    buffer = (rows, width)
+    return pl.pallas_call(
+        functools.partial(mlp_kernel, mode, n_row, n_seq, parts, len(after)),
+        out_shape=tuple(jax.ShapeDtypeStruct(*shape) for shape in shapes),
+        in_specs=[vmem(), anywhere(), anywhere()]
+        + [vmem()] * len(extra)
+        + [anywhere()] * (len(ride) + len(after)),
+        out_specs=(vmem(),) * (len(shapes) - len(ride)) + (anywhere(),) * len(ride),
+        scratch_shapes=[
+            pltpu.VMEM(up_own.shape, low),
+            pltpu.VMEM(down_own.shape, low),
+            sem((2,)),
+            pltpu.VMEM((total, width), low),
+            pltpu.VMEM((n_y,) + buffer, low),
+            pltpu.VMEM((n_y - 1,) + buffer, low),
+            pltpu.VMEM((n_y - 1,) + buffer, low),
+            pltpu.VMEM((2 * rows, width), low),
+            pltpu.VMEM((2 * rows, width) if mode == "both" else (16, LANES), low),
+            pltpu.VMEM((2 * rows, units if mode == "forward" else 2 * units), low),
+        ]
+        + [sem((n_y, parts))] * 2
+        + [sem((n_y - 1, parts))] * 2
+        + gather_rows_scratch(n_y, parts)
+        + [sem((3,))] * len(ride),
+        compiler_params=remote_params(collective, 56),
+        name="mlp_" + mode,
+    )(block, up_own, down_own, *extra, *ride, *after)
 
 
 def cycle(depth, breadth):
@@ -1378,20 +1713,6 @@
     n_seq = lax.axis_size("seq")
     n_x = n_seq // GROUPS
     return [[r * n_seq + z * n_x + x for r, x in plane_order()] for z in range(GROUPS)]
-
-
-def reduce_background(parts):
-    n_seq = lax.axis_size("seq")
-    shaped = [part.astype(jnp.bfloat16).reshape(n_seq, -1, part.shape[1]) for part in parts]
-    merged = jnp.concatenate(shaped, axis=1)
-    merged = merged.reshape(-1, merged.shape[2])
-    summed = lax.psum_scatter(merged, "seq", scatter_dimension=0, tiled=True)
-    pieces = []
-    at = 0
-    for part in shaped:
-        pieces.append(summed[at : at + part.shape[1]])
-        at += part.shape[1]
-    return pieces
 
 
 def owner_blocks(half):
@@ -1481,67 +1802,26 @@
     return whole
 
 
-def mlp_forward(values, gain_row, up_own, down_own, after=()):
-    odd = lax.axis_index("row") % 2 == 1
-    ff_row = down_own.shape[0]
-    normed, factor = norm_apply(values, gain_row)
-    spread = gather_rows(normed.astype(jnp.bfloat16), after)
-    gate_up = product(spread, up_own)
-    first, second = (gate_up[:, :ff_row], gate_up[:, ff_row:])
-    gate_part = jnp.where(odd, second, first)
-    up_part = jnp.where(odd, first, second)
-    hidden = (jax.nn.silu(gate_part) * up_part).astype(jnp.bfloat16)
-    partial = product(hidden, down_own).astype(jnp.bfloat16)
-    return (partial, (factor, spread, gate_part, up_part, hidden))
-
-
-def place_up_grad(grad):
-    n_row = lax.axis_size("row")
+def mlp_gradients(spread, hidden, d_gate_up, upstream_all, extra=(), before=()):
     n_seq = lax.axis_size("seq")
-    half = n_seq // 2
-    pairs = []
-    for r in range(n_row):
-        for s in range(n_seq):
-            if s // half == r % 2:
-                owner = (r // 2, s)
-            else:
-                owner = (n_row // 2 + r // 2, (r % 2) * half + s % half)
-            pairs.append((r * n_seq + s, owner[0] * n_seq + owner[1]))
-    return lax.ppermute(grad, ("row", "seq"), pairs)
-
-
-def mlp_backward(values, gain_row, up_own, down_own, kept, upstream, upstream_all, sums_before=()):
-    factor, spread, gate_part, up_part, hidden = kept
-    odd = lax.axis_index("row") % 2 == 1
-    d_hidden = right_trans(upstream_all, down_own)
-    gate_sig = jax.nn.sigmoid(gate_part)
-    d_gate = d_hidden * up_part * gate_sig * (1.0 + gate_part * (1.0 - gate_sig))
-    d_up = d_hidden * gate_part * gate_sig
-    d_gate_up = jnp.concatenate(
-        [jnp.where(odd, d_up, d_gate), jnp.where(odd, d_gate, d_up)], axis=1
-    ).astype(jnp.bfloat16)
-    n_seq = lax.axis_size("seq")
+    width = spread.shape[1]
     up_rows = d_gate_up.shape[1] // n_seq
-    if up_rows % (2 * LANES):
-        merged = jnp.concatenate(
-            [
-                left_trans(d_gate_up, spread).reshape(n_seq, up_rows, -1)[jnp.array(seq_order())],
-                left_trans(hidden, upstream_all).reshape(n_seq, up_rows // 2, -1)[jnp.array(seq_order())],
-            ],
-            axis=1,
-        )
-        merged = merged.reshape(-1, merged.shape[2]).astype(jnp.bfloat16)
+    if extra:
+        extra = [part.astype(jnp.bfloat16).reshape(n_seq, -1, width) for part in extra]
+        extra = [jnp.concatenate(extra, axis=1)]
+    if up_rows % (2 * LANES) or (extra and extra[0].shape[1] % 16):
+        parts = [left_trans(d_gate_up, spread), left_trans(hidden, upstream_all)]
+        parts = [part.astype(jnp.bfloat16).reshape(n_seq, -1, width) for part in parts]
+        merged = jnp.concatenate(parts + list(extra), axis=1)[jnp.array(seq_order())]
+        merged = merged.reshape(-1, width)
     else:
-        merged = grad_blocks(d_gate_up, spread, hidden, upstream_all)
-    d_gate_up, merged = lax.optimization_barrier((d_gate_up, merged))
-    merged = lax.optimization_barrier((merged,) + sums_before)[0]
+        merged = grad_blocks(d_gate_up, spread, hidden, upstream_all, extra)
+    merged = lax.optimization_barrier((merged,) + before)[0]
     summed = lax.psum_scatter(
         merged, "seq", scatter_dimension=0, tiled=True, axis_index_groups=[seq_order()]
     )
-    summed = (summed[:up_rows], summed[up_rows:])
-    d_normed = reduce_rows(right_trans(d_gate_up, up_own).astype(jnp.bfloat16))
-    d_norm, g_gain = norm_back(values, factor, gain_row, d_normed)
-    return (upstream + d_norm, g_gain, summed)
+    down_end = up_rows + up_rows // 2
+    return (merged, summed[:up_rows], summed[up_rows:down_end], summed[down_end:])
 
 
 def matchings(edges, size):
@@ -1700,8 +1980,11 @@
     gate_act = jax.nn.silu(gate_input)
     gated = (mamba_out * gate_act).astype(jnp.bfloat16)
     first_out = source + product(gated, output_weight)
-    second_partial, kept_first = mlp_forward(first_out, gains_mlp[0], up_first, down_first)
-    second_out = first_out + reduce_rows(second_partial)
+    normed_first, factor_first = norm_apply(first_out, gains_mlp[0])
+    spread_first, second_sum, hidden_first, gate_first, raise_first = mlp_fused(
+        "forward", normed_first.astype(jnp.bfloat16), up_first, down_first, (), (), 1
+    )
+    second_out = first_out + second_sum
     normed_attn, factor_attn = norm_apply(second_out, gain_attn)
     context, up_last = gather_seq(normed_attn.astype(jnp.bfloat16), mlp_up_weight, (gathered_in,))
     length = context.shape[0]
@@ -1728,19 +2011,13 @@
     )
     attended_low, gated_rows = swap_heads(attended, gated, True, 7)
     third_out = second_out + product(attended_low, attn_output)
-    final_partial, kept_last = mlp_forward(
-        third_out, gains_mlp[1], up_last, down_last, (gathered_grad,)
-    )
-    grad_low = cotangent[0]
-    d_third, g_gain_last, summed_last = mlp_backward(
-        third_out,
-        gains_mlp[1],
-        up_last,
-        down_last,
-        kept_last,
-        grad_low.astype(jnp.float32),
-        gathered_grad,
-    )
+    normed_last, factor_last = norm_apply(third_out, gains_mlp[1])
+    spread_last, d_normed_last, hidden_last, slope_last, final_partial = mlp_fused(
+        "both", normed_last.astype(jnp.bfloat16), up_last, down_last, (gathered_grad,), (), 2
+    )
+    summed_last = mlp_gradients(spread_last, hidden_last, slope_last, gathered_grad)[1:3]
+    d_norm_last, g_gain_last = norm_back(third_out, factor_last, gains_mlp[1], d_normed_last)
+    d_third = cotangent[0].astype(jnp.float32) + d_norm_last
     d_third_low = d_third.astype(jnp.bfloat16)
     d_third_rows = lax.all_gather(d_third_low, "row", axis=0, tiled=True)
     d_attended, attended_rows, final_sum = swap_heads(
@@ -1774,8 +2051,10 @@
     d_attn_normed = reduce_seq(
         right_trans(d_triple, head_weight).astype(jnp.bfloat16), tuple(summed_last)
     )
+    g_attn_local = left_trans(d_triple, context).astype(jnp.bfloat16)
+    g_attn_local = lax.optimization_barrier((g_attn_local, d_attn_normed))[0]
     g_attn_weight = lax.psum_scatter(
-        left_trans(d_triple, context).astype(jnp.bfloat16),
+        g_attn_local,
         ("row", "seq"),
         scatter_dimension=0,
         tiled=True,
@@ -1785,18 +2064,19 @@
         second_out, factor_attn, gain_attn, d_attn_normed
     )
     d_second = d_third + d_attn_norm
-    d_first, g_gain_first, summed_first = mlp_backward(
-        first_out,
-        gains_mlp[0],
+    second_rows, d_normed_first, slope_first, up_placed = mlp_fused(
+        "backward",
+        d_second.astype(jnp.bfloat16),
         up_first,
         down_first,
-        kept_first,
-        d_second,
-        gather_rows(d_second.astype(jnp.bfloat16), (d_third_rows,)),
-        (g_attn_weight,),
-    )
+        (gate_first, raise_first),
+        (d_third_rows,),
+        3,
+        (summed_last[0],),
+    )
+    d_norm_first, g_gain_first = norm_back(first_out, factor_first, gains_mlp[0], d_normed_first)
+    d_first = d_second + d_norm_first
     d_first_low = d_first.astype(jnp.bfloat16)
-    g_down_first = summed_first[1].astype(jnp.float32)
     d_gated = right_trans(d_first_low, output_weight)
     d_scanned = d_gated * gate_act
     gate_sig = jax.nn.sigmoid(gate_input)
@@ -1807,22 +2087,36 @@
         step_size, d_scanned, keep_lanes, read_flat, decay_planes
     )
     end_grad, gate_spread, d_first_rows = exchange_states(
-        summed_steps, back_end, decay_planes, 6, owner_blocks(d_gate_low), d_first_low, tuple(summed_first)
-    )
-    sums = [
-        left_trans(gated_rows, d_first_rows).astype(jnp.bfloat16),
-        left_trans(attended_rows, d_third_rows).astype(jnp.bfloat16),
-    ]
-    sums = lax.optimization_barrier(tuple(sums) + tuple(summed_first))[:2]
-    output_piece, attn_piece = reduce_background(sums)
-    g_output_weight = output_piece.astype(jnp.float32)
-    g_attn_output = attn_piece.astype(jnp.float32)
-    late = lax.optimization_barrier((summed_last[0], summed_first[0], g_attn_weight, end_grad))
-    g_up_last, g_up_first = [place_up_grad(piece).astype(jnp.float32).T for piece in late[:2]]
-    g_attn_weight = place_attn_grad(late[2], width).astype(jnp.float32).T
+        summed_steps, back_end, decay_planes, 6, owner_blocks(d_gate_low), d_first_low
+    )
+    merged_first, up_first_sum, g_down_first, tail_sum = mlp_gradients(
+        spread_first,
+        hidden_first,
+        slope_first,
+        second_rows,
+        (left_trans(gated_rows, d_first_rows), left_trans(attended_rows, d_third_rows)),
+        (g_attn_weight, end_grad),
+    )
     g_step, g_activated, in_lanes, read_lanes, g_decays = adjoint_full(
-        end_grad, marks, step_size, activated_low, d_scanned, keep_lanes, in_flat, read_flat, decay_planes
-    )
+        end_grad,
+        marks,
+        step_size,
+        activated_low,
+        d_scanned,
+        keep_lanes,
+        in_flat,
+        read_flat,
+        decay_planes,
+        (merged_first,),
+    )
+    g_up_last = up_placed.astype(jnp.float32).T
+    g_attn_weight = lax.optimization_barrier((g_attn_weight, end_grad))[0]
+    attn_placed = place_attn_grad(g_attn_weight, width)
+    g_attn_weight = attn_placed.astype(jnp.float32).T
+    g_down_first = g_down_first.astype(jnp.float32)
+    output_rows = inner_dim // (n_row * n_seq)
+    g_output_weight = tail_sum[:output_rows].astype(jnp.float32)
+    g_attn_output = tail_sum[output_rows:].astype(jnp.float32)
     g_input_map = jnp.sum(in_lanes.reshape(rows_here, state_dim, LANES), axis=2)
     g_read_map = jnp.sum(read_lanes.reshape(rows_here, state_dim, LANES), axis=2)
     g_decay_log = g_decays.reshape(state_dim, inner_dim) * decays
@@ -1873,14 +2167,17 @@
     lines.append(jnp.zeros((spare, inner_dim), jnp.float32))
     packed = jnp.concatenate(columns + [jnp.concatenate(lines, axis=0).T], axis=1)
     conv_spread, summed = swap_and_reduce(
-        owner_blocks(d_conv_low), packed.astype(jnp.bfloat16), 11, (output_piece, attn_piece)
-    )
-    g_input_weight = reduce_rows(
+        owner_blocks(d_conv_low), packed.astype(jnp.bfloat16), 11, (attn_placed,)
+    )
+    g_input_weight, first_placed = reduce_rows(
         jnp.concatenate(
             [input_term(conv_spread, gathered_in), input_term(gate_spread, gathered_in)], axis=0
         ),
+        up_first_sum,
         13,
-    ).T
+    )
+    g_input_weight = g_input_weight.T
+    g_up_first = first_placed.astype(jnp.float32).T
     at = columns[0].shape[1]
     small_select = summed[:, :at]
     small_step = summed[:, at : at + rank_dim].T

time: 1190 us -> 1140 us (0.958)
  matrix products: 165 us -> 100 us
  Pallas kernels: 738 us -> 769 us
    pallas_call x10 -> x7, Pallas kernels: 222 us -> 275 us  [the longest x3 171 us: mlp_fused(): pl.pallas_call(functools.partial(mlp_kernel, mode, n_row, n_seq, parts, l...]
    dot_general x10 -> x6, matrix products: 86.7 us -> 48.6 us  [right_trans(): lax.dot_general(left_op, right_op, (((1,), (1,)), ((), ())), preferred_el...]
    dot_general x9 -> x5, matrix products: 45.4 us -> 17.8 us  [product(): return jnp.dot(left_op, right_op, preferred_element_type=jnp.float32)]
    unnamed x340 -> x304, local copies, waits for them, and re-layouts: 61.9 us -> 53.6 us
  transfers between devices with their start and end apart: 17 -> 14, of which waited for: 1 -> 2; matrix products, arithmetic and copies ran while one was open for 23% -> 21% of each run, Pallas kernels for 43% -> 54%
where the time goes in v4:
time: 1140 us; the launch traced here: 1130 us
  Pallas kernels  769 us (67%)
  local copies, waits for them, and re-layouts  122 us (11%)
  matrix products  100 us (9%)
  other arithmetic  77.3 us (7%)
  starting transfers between devices  25 us (2%)
  between operations  19.6 us (2%)
  waiting for transfers between devices  14.7 us (1%)
    pallas_call x3, Pallas kernels, mlp_fused(): pl.pallas_call(functools.partial(mlp_kernel, mode, n_row, n_seq, parts, l...  171 us
    pallas_call x1, Pallas kernels, gather_seq(): pl.pallas_call(functools.partial(gather_seq_kernel, n_row, n_seq, parts),...  72 us
    pallas_call x1, Pallas kernels, reduce_seq(): pl.pallas_call(functools.partial(reduce_seq_kernel, n_seq, parts), out_sh...  69.1 us
    pallas_call x1, Pallas kernels, gather_input(): pl.pallas_call(functools.partial(gather_input_kernel, parts), out_shape=j...  67.9 us
    unnamed x304, local copies, waits for them, and re-layouts  53.6 us
    pallas_call x1, Pallas kernels, exchange_states(): pl.pallas_call(functools.partial(exchange_kernel, n_row, n_seq, False), o...  53 us
    pallas_call x2, Pallas kernels, swap_heads(): pl.pallas_call(functools.partial(swap_heads_kernel, n_row, n_x, collect),...  49.7 us
    pallas_call x1, Pallas kernels, adjoint_full(): pl.pallas_call(functools.partial(adjoint_full_kernel, states, chunk, len(...  48.8 us
  transfers between devices with their start and end apart: 14, of which 2 were waited for; matrix products, arithmetic and copies ran while one was open for 21% of the time, Pallas kernels for 54%

profile of v4, /device:TPU:6, one launch (start us, length us, event | category | flops | bytes accessed | tf_op | source)
XLA Modules:
  0.0 1127.9 jit_solution(5518482430608211420)
XLA Ops:
  9.7 67.9 %gather_input.1 = bf16[1536,6144]{1,0:T(8,128)(2,1)S(1)} custom-call(bf16[384,6144]{1,0:T(8,128)(2,1)S(1)} %copy-done.22), custom_call_target="tpu_custom_call" | custom-call | tf_op jit(solution)/shard_map/gather_input/pallas_call | solution.py:1378
  155.0 13.7 %scan_end.1 = f32[16,24,128]{2,1,0:T(8,128)S(1)} custom-call(f32[256,3072]{1,0:T(8,128)S(1)} %copy-done.3, bf16[256,3072]{1,0:T(8,128)(2,1)S(1)} %get-tuple-element.253.refs_1_.refs_2_.act_ref, f32[256,128]{1,0:T(8,128)S(1)} %broadcast_in_dim.56.refs_2_.refs_3_.keep_ref, f32[4096]{0:T(1024)S(1)} %reshape.334.refs_3_.refs_4_.in_ref, f32[16,24,128]{2,1,0:T(8,128)S(1)} %bitcast.143), custom_call_target="tpu_custom_call" | custom-call | tf_op jit(solution)/shard_map/scan_end/pallas_call | solution.py:136
  168.8 25.9 %exchange_states.1.refs_0_ = f32[16,24,128]{2,1,0:T(8,128)S(1)} custom-call(bf16[448,128]{1,0:T(8,128)(2,1)S(1)} %fusion.32.x_ref, f32[16,24,128]{2,1,0:T(8,128)S(1)} %bitcast.144), custom_call_target="tpu_custom_call" | custom-call | tf_op jit(solution)/shard_map/exchange_states/pallas_call | solution.py:1100
  198.4 19.5 %scan_out.1 = (f32[256,3072]{1,0:T(8,128)S(1)}, f32[8,16,24,128]{3,2,1,0:T(8,128)S(1)}) custom-call(f32[16,24,128]{2,1,0:T(8,128)S(1)} %exchange_states.1.refs_0_, f32[256,3072]{1,0:T(8,128)S(1)} %copy-done.4, bf16[256,3072]{1,0:T(8,128)(2,1)S(1)} %get-tuple-element.253.refs_1_.refs_2_.act_ref, f32[256,128]{1,0:T(8,128)S(1)} %broadcast_in_dim.56.refs_2_.refs_3_.keep_ref, ...), custom_call_target="tpu_custom_call" | custom-call | tf_op jit(solution)/shard_map/scan_out/pallas_call | solution.py:155
  238.1 54.3 %mlp_forward.1 = (bf16[1024,1536]{1,0:T(8,128)(2,1)}, f32[256,1536]{1,0:T(8,128)}, bf16[1024,1024]{1,0:T(8,128)(2,1)}, f32[1024,1024]{1,0:T(8,128)}, f32[1024,1024]{1,0:T(8,128)}) custom-call(bf16[256,1536]{1,0:T(8,128)(2,1)} %multiply_convert_fusion.5.refs_0_, bf16[1536,2048]{1,0:T(8,128)(2,1)} %constant_dynamic-update-slice_fusion.1.refs_1_, ...), custom_call_target="tpu_custom_call" | custom-call | tf_op jit(solution)/shard_map/mlp_forward/pallas_call | solution.py:1662
  297.5 72.0 %gather_seq.1 = (bf16[2048,1536]{1,0:T(8,128)(2,1)}, bf16[1536,2048]{1,0:T(8,128)(2,1)}) custom-call(bf16[256,1536]{1,0:T(8,128)(2,1)S(1)} %copy-done.28, bf16[2,384,8192]{2,1,0:T(8,128)(2,1)} %up_ref.1, bf16[2048,1536]{1,0:T(8,128)(2,1)} %all-gather.4.cloned.1.call-done.refs_0_), custom_call_target="tpu_custom_call" | custom-call | tf_op jit(solution)/shard_map/gather_seq/pallas_call | solution.py:955
  369.6 12.5 %project_heads.1.q_ref.k_ref.v_ref = bf16[2048,1152]{1,0:T(8,128)(2,1)S(1)} custom-call(bf16[2048,1536]{1,0:T(8,128)(2,1)} %get-tuple-element.68.ctx_ref, bf16[1536,1152]{1,0:T(8,128)(2,1)S(1)} %copy-done.25, f32[2048,128]{1,0:T(8,128)S(1)} %copy-done.13, f32[2048,128]{1,0:T(8,128)S(1)} %copy-done.15), custom_call_target="tpu_custom_call" | custom-call | flops 7247757312 | bytes 9830400 | tf_op jit(solution)/shard_map/project_heads/pallas_call | solution.py:402
  382.1 20.4 %attend.1 = (bf16[1024,384]{1,0:T(8,128)(2,1)S(1)}, f32[3,1024,1]{2,1,0:T(8,128)S(1)}) custom-call(s32[1]{0:T(128)} %bitcast.20.x_ref, s32[4]{0:T(128)S(1)} %get-tuple-element.296.low_ref, bf16[2048,1152]{1,0:T(8,128)(2,1)S(1)} %project_heads.1.q_ref.k_ref.v_ref, bf16[2048,1152]{1,0:T(8,128)(2,1)S(1)} %project_heads.1.q_ref.k_ref.v_ref, ...), custom_call_target="tpu_custom_call" | custom-call | flops 1610612736 | bytes 3145728 | tf_op jit(solution)/shard_map/attend/pallas_call | solution.py:473
  402.6 20.0 %collect_heads.1 = (bf16[256,1536]{1,0:T(8,128)(2,1)S(1)}, bf16[1024,768]{1,0:T(8,128)(2,1)S(1)}) custom-call(bf16[1024,384]{1,0:T(8,128)(2,1)S(1)} %get-tuple-element.69.x_ref.out_ref, bf16[256,3072]{1,0:T(8,128)(2,1)S(1)} %copy-done.19), custom_call_target="tpu_custom_call" | custom-call | tf_op jit(solution)/shard_map/collect_heads/pallas_call | solution.py:1211
  426.5 52.3 %mlp_both.1 = (bf16[1024,1536]{1,0:T(8,128)(2,1)}, f32[256,1536]{1,0:T(8,128)}, bf16[1024,1024]{1,0:T(8,128)(2,1)}, bf16[1024,2048]{1,0:T(8,128)(2,1)}, bf16[1024,1536]{1,0:T(8,128)(2,1)}) custom-call(bf16[256,1536]{1,0:T(8,128)(2,1)} %multiply_convert_fusion.3.refs_0_, bf16[1536,2048]{1,0:T(8,128)(2,1)} %get-tuple-element.71.refs_1_, ...), custom_call_target="tpu_custom_call" | custom-call | tf_op jit(solution)/shard_map/mlp_both/pallas_call | solution.py:1662
  482.3 14.1 %grad_blocks.2 = bf16[3072,1536]{1,0:T(8,128)(2,1)} custom-call(bf16[1024,2048]{1,0:T(8,128)(2,1)} %get-tuple-element.81.d_ref, bf16[1024,1536]{1,0:T(8,128)(2,1)S(1)} %copy-done.34, bf16[1024,1024]{1,0:T(8,128)(2,1)S(1)} %copy-done.37, bf16[1024,1536]{1,0:T(8,128)(2,1)S(1)} %copy-done.10), custom_call_target="tpu_custom_call" | custom-call | tf_op jit(solution)/shard_map/grad_blocks/pallas_call | solution.py:1405
  507.5 29.7 %spread_heads.1 = (bf16[1024,384]{1,0:T(8,128)(2,1)S(1)}, bf16[1024,384]{1,0:T(8,128)(2,1)S(1)}, f32[256,1536]{1,0:T(8,128)S(1)}) custom-call(bf16[256,1536]{1,0:T(8,128)(2,1)S(1)} %convolution_convert_fusion.8.x_ref, bf16[256,1536]{1,0:T(8,128)(2,1)S(1)} %copy-done.47, bf16[1024,1536]{1,0:T(8,128)(2,1)S(1)} %copy-done.33), custom_call_target="tpu_custom_call" | custom-call | tf_op jit(solution)/shard_map/spread_heads/pallas_call | solution.py:1211
  541.5 29.5 %attend_back.1 = (bf16[1024,384]{1,0:T(8,128)(2,1)S(1)}, bf16[2048,384]{1,0:T(8,128)(2,1)S(1)}, bf16[2048,384]{1,0:T(8,128)(2,1)S(1)}) custom-call(s32[1]{0:T(128)} %bitcast.20.x_ref, s32[4]{0:T(128)S(1)} %get-tuple-element.296.low_ref, bf16[2048,1152]{1,0:T(8,128)(2,1)S(1)} %copy-done.2, bf16[2048,1152]{1,0:T(8,128)(2,1)S(1)} %copy-done.2, ...), custom_call_target="tpu_custom_call" | custom-call | flops 4026531840 | bytes 6291456 | tf_op jit(solution)/shard_map/attend_back/pallas_call | solution.py:562
  593.0 14.5 %reduce-scatter.4.cloned.1.call-done = bf16[384,1536]{1,0:T(8,128)(2,1)} async-done(((bf16[3072,1536]{1,0:T(8,128)(2,1)}), bf16[384,1536]{1,0:T(8,128)(2,1)}) %reduce-scatter.4.cloned.1.call-update) | async-done | bytes 1179664 | tf_op jit(solution)/shard_map/reduce_scatter | solution.py:1820
  610.7 69.1 %reduce_seq.1 = f32[256,1536]{1,0:T(8,128)S(1)} custom-call(bf16[2048,1536]{1,0:T(8,128)(2,1)} %convolution_convert_fusion.1.x_ref, bf16[256,1536]{1,0:T(8,128)(2,1)S(1)} %slice.186.refs_0_.refs_5_, bf16[128,1536]{1,0:T(8,128)(2,1)S(1)} %get-tuple-element.277.refs_1_), custom_call_target="tpu_custom_call" | custom-call | tf_op jit(solution)/shard_map/reduce_seq/pallas_call | solution.py:1029
  690.3 64.0 %mlp_backward.1 = (bf16[1024,1536]{1,0:T(8,128)(2,1)}, f32[256,1536]{1,0:T(8,128)}, bf16[1024,2048]{1,0:T(8,128)(2,1)}, bf16[256,1536]{1,0:T(8,128)(2,1)}) custom-call(bf16[256,1536]{1,0:T(8,128)(2,1)} %get-tuple-element.247.refs_0_, bf16[1536,2048]{1,0:T(8,128)(2,1)} %constant_dynamic-update-slice_fusion.1.refs_1_, ...), custom_call_target="tpu_custom_call" | custom-call | tf_op jit(solution)/shard_map/mlp_backward/pallas_call | solution.py:1662
  758.8 12.3 %fusion.3 = (bf16[3072]{0:T(1024)(128)(2,1)S(1)}, f32[256,3072]{1,0:T(8,128)}, bf16[256,3072]{1,0:T(8,128)(2,1)}) fusion(bf16[256,3072]{1,0:T(8,128)(2,1)S(1)} %get-tuple-element.253.refs_1_.refs_2_.act_ref, f32[256,6144]{1,0:T(8,128)} %copy-done.71, f32[256,3072]{1,0:T(8,128)S(1)} %copy-done.30, f32[3072]{0:T(1024)S(1)} %copy-done.105, ...), kind=kOutput, calls=%fused_computation.19 | convolution fusion | flops 2429285376 | bytes 22824960 | tf_op jit(solution)/shard_map/dot_general | solution.py:41
  782.8 13.8 %adjoint_end.1 = f32[16,24,128]{2,1,0:T(8,128)S(1)} custom-call(f32[256,3072]{1,0:T(8,128)S(1)} %copy-done.5, f32[256,3072]{1,0:T(8,128)S(1)} %copy-done.11, f32[256,128]{1,0:T(8,128)S(1)} %broadcast_in_dim.56.refs_2_.refs_3_.keep_ref, f32[4096]{0:T(1024)S(1)} %reshape.337.refs_5_.read_ref, f32[16,24,128]{2,1,0:T(8,128)S(1)} %bitcast.146), custom_call_target="tpu_custom_call" | custom-call | tf_op jit(solution)/shard_map/adjoint_end/pallas_call | solution.py:215
  796.7 53.0 %exchange_states_back.1 = (f32[16,24,128]{2,1,0:T(8,128)S(1)}, bf16[8,256,384]{2,1,0:T(8,128)(2,1)S(1)}, bf16[1024,1536]{1,0:T(8,128)(2,1)S(1)}) custom-call(bf16[448,128]{1,0:T(8,128)(2,1)S(1)} %fusion.33.x_ref, f32[16,24,128]{2,1,0:T(8,128)S(1)} %bitcast.147, bf16[8,256,384]{2,1,0:T(8,128)(2,1)S(1)} %copy-done.21, ...), custom_call_target="tpu_custom_call" | custom-call | tf_op jit(solution)/shard_map/exchange_states_back/pallas_call | solution.py:1109
  858.0 15.2 %grad_blocks.3.refs_0_ = bf16[4224,1536]{1,0:T(8,128)(2,1)} custom-call(bf16[1024,2048]{1,0:T(8,128)(2,1)} %get-tuple-element.89.d_ref, bf16[1024,1536]{1,0:T(8,128)(2,1)S(1)} %copy-done.31, bf16[1024,1024]{1,0:T(8,128)(2,1)S(1)} %copy-done.35, bf16[1024,1536]{1,0:T(8,128)(2,1)S(1)} %copy-done.32, bf16[8,144,1536]{2,1,0:T(8,128)(2,1)} %pad_maximum_fusion.2.refs_0_), custom_call_target="tpu_custom_call" | custom-call | tf_op jit(solution)/shard_map/grad_blocks/pallas_call | solution.py:1405
  903.2 48.8 %adjoint_full.1 = (f32[256,3072]{1,0:T(8,128)}, f32[256,3072]{1,0:T(8,128)}, f32[4096,128]{1,0:T(8,128)S(1)}, f32[4096,128]{1,0:T(8,128)}, f32[16,24,128]{2,1,0:T(8,128)S(1)}) custom-call(f32[16,24,128]{2,1,0:T(8,128)S(1)} %copy-done.49, f32[8,16,24,128]{3,2,1,0:T(8,128)S(1)} %copy-done.39, f32[256,3072]{1,0:T(8,128)} %get-tuple-element.273.refs_0_.refs_1_.step_ref, ...), custom_call_target="tpu_custom_call" | custom-call | tf_op jit(solution)/shard_map/adjoint_full/pallas_call | solution.py:351
  989.5 11.3 %fusion.22 = (bf16[1536]{0:T(1024)(128)(2,1)S(1)}, f32[256]{0:T(256)}, f32[256,1536]{1,0:T(8,128)}) fusion(bf16[1,256,1536]{2,1,0:T(8,128)(2,1)S(1)} %copy-done.69, f32[256]{0:T(256)S(1)} %copy-done.125, f32[1536]{0:T(1024)S(1)} %copy-done.103, bf16[1536,6144]{1,0:T(8,128)(2,1)} %copy-done.6, bf16[256,3072]{1,0:T(8,128)(2,1)S(1)} %copy-done.87, ...), kind=kOutput, calls=%fused_computation.66 | convolution fusion | flops 4840880128 | bytes 24390656 | tf_op jit(solution)/shard_map/dot_general | solution.py:41
  1020.9 47.7 %swap_and_reduce.1 = (bf16[8,256,384]{2,1,0:T(8,128)(2,1)S(1)}, f32[96,256]{1,0:T(8,128)S(1)}) custom-call(bf16[8,256,384]{2,1,0:T(8,128)(2,1)S(1)} %copy-done.20, bf16[3072,256]{1,0:T(8,128)(2,1)S(1)} %pad_maximum_fusion.10.packed_ref, bf16[144,1536]{1,0:T(8,128)(2,1)S(1)} %constant_dynamic-update-slice_fusion.refs_0_), custom_call_target="tpu_custom_call" | custom-call | tf_op jit(solution)/shard_map/swap_and_reduce/pallas_call | solution.py:1285
  1084.2 26.0 %reduce_rows.1 = (f32[192,1536]{1,0:T(8,128)S(1)}, bf16[256,1536]{1,0:T(8,128)(2,1)S(1)}) custom-call(bf16[768,1536]{1,0:T(8,128)(2,1)S(1)} %pad_maximum_fusion.4.x_ref, bf16[256,1536]{1,0:T(8,128)(2,1)S(1)} %slice.191.ride_ref), custom_call_target="tpu_custom_call" | custom-call | tf_op jit(solution)/shard_map/reduce_rows/pallas_call | solution.py:858
  (503 shorter events, 300.7 us)
Async XLA Ops:
  7.2 140.1 %copy-start = (bf16[3072,128]{1,0:T(8,128)(2,1)S(1)}, bf16[3072,128]{1,0:T(8,128)(2,1)}, u32[]{:S(2)}) copy-start(bf16[3072,128]{1,0:T(8,128)(2,1)} %param.30) | copy-start | bytes 2359300
  7.2 289.2 %all-gather.4.cloned.1.call-start = ((), (), s32[]{:S(2)}) async-start(), calls=%async_computation.3 | async-start | bytes 7077888 | tf_op jit(solution)/shard_map/all_gather | solution.py:1942
  9.7 74.3 %copy-start.131 = (bf16[1536]{0:T(1024)(128)(2,1)S(1)}, bf16[1536]{0:T(1024)(128)(2,1)}, u32[]{:S(2)}) copy-start(bf16[1536]{0:T(1024)(128)(2,1)} %param.26) | copy-start | bytes 9220
  9.7 74.3 %copy-start.67 = (bf16[1,256,1536]{2,1,0:T(8,128)(2,1)S(1)}, bf16[1,256,1536]{2,1,0:T(8,128)(2,1)}, u32[]{:S(2)}) copy-start(bf16[1,256,1536]{2,1,0:T(8,128)(2,1)} %param.25) | copy-start | bytes 2359300
  86.3 340.2 %all-gather.6.cloned.1.call-start = ((), (), s32[]{:S(2)}) async-start(), calls=%async_computation.4 | async-start | bytes 3932160 | tf_op jit(solution)/shard_map/all_gather | solution.py:1945
  91.6 138.3 %collective-permute-start.1 = (bf16[384,2048]{1,0:T(8,128)(2,1)}, bf16[384,2048]{1,0:T(8,128)(2,1)}, u32[]{:S(2)}, u32[]{:S(2)}) collective-permute-start(bf16[384,2048]{1,0:T(8,128)(2,1)} %pad_maximum_fusion.7), channel_id=1, source_target_pairs={{0,8},{8,0},{16,24},{24,16},{1,9},{9,1},{17,25},{25,17},{2,10},{10... | collective-permute-start | bytes 4718600 | tf_op jit(solution)/shard_map/ppermute | solution.py:1800
  93.2 139.4 %collective-permute-start.2 = (bf16[384,2048]{1,0:T(8,128)(2,1)}, bf16[384,2048]{1,0:T(8,128)(2,1)}, u32[]{:S(2)}, u32[]{:S(2)}) collective-permute-start(bf16[384,2048]{1,0:T(8,128)(2,1)} %pad_maximum_fusion.8), channel_id=1, source_target_pairs={{0,16},{8,24},{16,0},{24,8},{1,17},{9,25},{17,1},{25,9},{2,18},{10... | collective-permute-start | bytes 4718600 | tf_op jit(solution)/shard_map/ppermute | solution.py:1800
  96.0 139.4 %collective-permute-start.3 = (bf16[384,2048]{1,0:T(8,128)(2,1)}, bf16[384,2048]{1,0:T(8,128)(2,1)}, u32[]{:S(2)}, u32[]{:S(2)}) collective-permute-start(bf16[384,2048]{1,0:T(8,128)(2,1)} %pad_maximum_fusion.9), channel_id=1, source_target_pairs={{0,24},{8,16},{16,8},{24,0},{1,25},{9,17},{17,9},{25,1},{2,26},{10... | collective-permute-start | bytes 4718600 | tf_op jit(solution)/shard_map/ppermute | solution.py:1800
  104.7 32.9 %collective-permute-start = (bf16[3,3072]{1,0:T(4,128)(2,1)S(1)}, bf16[3,3072]{1,0:T(4,128)(2,1)S(1)}, u32[]{:S(2)}, u32[]{:S(2)}) collective-permute-start(bf16[3,3072]{1,0:T(4,128)(2,1)S(1)} %slice.256), channel_id=1, source_target_pairs={{0,1},{1,2},{2,3},{3,4},{4,5},{5,6},{6,7},{8,9},{9,10},{10,11},{11... | collective-permute-start | bytes 55304 | tf_op jit(solution)/shard_map/ppermute | solution.py:27
  109.0 498.4 %reduce-scatter.4.cloned.1.call-start = ((), (), s32[]{:S(2)}) async-start(), calls=%async_computation.5 | async-start | bytes 10616832 | tf_op jit(solution)/shard_map/reduce_scatter | solution.py:1820
  136.6 81.4 %copy-start.104 = (f32[3072]{0:T(1024)}, f32[3072]{0:T(1024)S(1)}, u32[]{:S(2)}) copy-start(f32[3072]{0:T(1024)S(1)} %convert_element_type.244) | copy-start | bytes 36868
  294.2 75.3 %copy-start.120 = (f32[256]{0:T(256)}, f32[256]{0:T(256)S(1)}, u32[]{:S(2)}) copy-start(f32[256]{0:T(256)S(1)} %add_rsqrt_fusion.1) | copy-start | bytes 3076
  297.5 72.0 %copy-start.13 = (f32[2048,128]{1,0:T(8,128)S(1)}, f32[2048,128]{1,0:T(8,128)}, u32[]{:S(2)}) copy-start(f32[2048,128]{1,0:T(8,128)} %get-tuple-element.304.cos_ref.cos_all) | copy-start | bytes 3145732
  297.5 72.0 %copy-start.15 = (f32[2048,128]{1,0:T(8,128)S(1)}, f32[2048,128]{1,0:T(8,128)}, u32[]{:S(2)}) copy-start(f32[2048,128]{1,0:T(8,128)} %get-tuple-element.305.sin_ref.sin_all) | copy-start | bytes 3145732
  297.5 72.0 %copy-start.25 = (bf16[1536,1152]{1,0:T(8,128)(2,1)S(1)}, bf16[1536,1152]{1,0:T(8,128)(2,1)}, u32[]{:S(2)}) copy-start(bf16[1536,1152]{1,0:T(8,128)(2,1)} %pad_maximum_fusion.1.weight_ref) | copy-start | bytes 10616836
  297.5 125.2 %slice-start = ((s8[4718592]{0:T(1024)(128)(4,1)}), s8[524288]{0:T(1024)(128)(4,1)S(1)}, s32[]{:S(2)}) async-start(s8[4718592]{0:T(1024)(128)(4,1)} %bitcast.180), calls=%async_computation.9 | async-start | bytes 1048576
  496.4 185.0 %all-gather.8.cloned.1.call-start = ((), (), s32[]{:S(2)}) async-start(), calls=%async_computation.6 | async-start | bytes 3932160 | tf_op jit(solution)/shard_map/all_gather | solution.py:2022
  502.1 371.1 %reduce-scatter.6.cloned.1.call-start = ((), (), s32[]{:S(2)}) async-start(), calls=%async_computation.7 | async-start | bytes 3981312 | tf_op jit(solution)/shard_map/reduce_scatter | solution.py:2056
  608.6 71.2 %copy-start.17 = (bf16[256,1536]{1,0:T(8,128)(2,1)}, bf16[256,1536]{1,0:T(8,128)(2,1)S(1)}, u32[]{:S(2)}) copy-start(bf16[256,1536]{1,0:T(8,128)(2,1)S(1)} %slice.186.refs_0_.refs_5_) | copy-start | bytes 2359300
  681.1 401.8 %reduce-scatter.8.cloned.1.call-start = ((), (), s32[]{:S(2)}) async-start(), calls=%async_computation.8 | async-start | bytes 14598144 | tf_op jit(solution)/shard_map/reduce_scatter | solution.py:1820
  887.3 129.3 %collective-permute-start.5 = (bf16[48,1536]{1,0:T(8,128)(2,1)}, bf16[48,1536]{1,0:T(8,128)(2,1)}, u32[]{:S(2)}, u32[]{:S(2)}) collective-permute-start(bf16[48,1536]{1,0:T(8,128)(2,1)} %get-tuple-element.280), channel_id=1, source_target_pairs={{0,0},{2,3},{4,6},{6,8},{8,1},{10,4},{12,7},{14,9},{24,2},{26,5},{... | collective-permute-start | bytes 442376 | tf_op jit(solution)/shard_map/ppermute | solution.py:1878
  891.7 125.9 %collective-permute-start.6 = (bf16[48,1536]{1,0:T(8,128)(2,1)}, bf16[48,1536]{1,0:T(8,128)(2,1)}, u32[]{:S(2)}, u32[]{:S(2)}) collective-permute-start(bf16[48,1536]{1,0:T(8,128)(2,1)} %get-tuple-element.279), channel_id=1, source_target_pairs={{0,0},{2,3},{4,5},{6,8},{8,1},{10,4},{12,6},{14,9},{24,2},{26,13},... | collective-permute-start | bytes 442376 | tf_op jit(solution)/shard_map/ppermute | solution.py:1878
  901.2 117.3 %collective-permute-start.7 = (bf16[48,1536]{1,0:T(8,128)(2,1)}, bf16[48,1536]{1,0:T(8,128)(2,1)}, u32[]{:S(2)}, u32[]{:S(2)}) collective-permute-start(bf16[48,1536]{1,0:T(8,128)(2,1)} %get-tuple-element.278), channel_id=1, source_target_pairs={{0,0},{2,2},{4,5},{6,8},{8,1},{10,3},{12,6},{14,9},{24,10},{26,4},... | collective-permute-start | bytes 442376 | tf_op jit(solution)/shard_map/ppermute | solution.py:1878
  979.7 7.3 collective-permute-start.4
  (138 other events, 1506.5 us)
Sparse Core Ops, SparseCore 0:
  86.4 68.8 all-gather.3
  156.9 28.1 all-gather.5
  496.5 110.9 reduce-scatter.3
  609.4 30.8 all-gather.7
  681.2 46.3 reduce-scatter.5
  873.4 145.1 reduce-scatter.7

commit v5 on v4

--- a/solution.py
+++ b/solution.py
@@ -380,42 +380,6 @@
 
 def turn_half(values):
     return pltpu.roll(values, HEAD_DIM // 2, 1)
-
-
-def project_kernel(rotated, ctx_ref, weight_ref, cos_ref, sin_ref, out_ref):
-    cosine, sine = cos_ref[...], sin_ref[...]
-    ctx = ctx_ref[...]
-    step = 3 * HEAD_DIM
-    for start in range(0, weight_ref.shape[1], step):
-        triple = product(ctx, weight_ref[:, start : start + step])
-        for head in range(0, step, HEAD_DIM):
-            part = triple[:, head : head + HEAD_DIM]
-            if start + head < rotated:
-                part = part * cosine + turn_half(part) * sine
-            out_ref[:, start + head : start + head + HEAD_DIM] = part.astype(jnp.bfloat16)
-
-
-def project_heads(ctx, weight, cosine, sine, rotated):
-    length, width = ctx.shape
-    columns = weight.shape[1]
-    rows = min(256, length)
-    return pl.pallas_call(
-        functools.partial(project_kernel, rotated),
-        out_shape=jax.ShapeDtypeStruct((length, columns), jnp.bfloat16),
-        grid=(length // rows,),
-        in_specs=[
-            pl.BlockSpec((rows, width), lambda i: (i, 0)),
-            pl.BlockSpec((width, columns), lambda i: (0, 0)),
-            pl.BlockSpec((rows, HEAD_DIM), lambda i: (i, 0)),
-            pl.BlockSpec((rows, HEAD_DIM), lambda i: (i, 0)),
-        ],
-        out_specs=pl.BlockSpec((rows, columns), lambda i: (i, 0)),
-        compiler_params=pltpu.CompilerParams(vmem_limit_bytes=40 << 20),
-        cost_estimate=pl.CostEstimate(
-            flops=2 * length * width * columns, bytes_accessed=2 * (length * width + width * columns), transcendentals=0
-        ),
-        name="project_heads",
-    )(ctx, weight, cosine, sine)
 
 
 def mask_keys(scores_shape, chunk, first_key, q_pos):
@@ -870,6 +834,23 @@
     )(partial, ride)
 
 
+def load_heads(weight_ref, weight, weight_sem, n_x):
+    width = weight_ref.shape[0]
+    cols = weight.shape[1] // 3
+    z = lax.axis_index("seq") // n_x
+    loads = []
+    for part in range(3):
+        column = pl.ds(pl.multiple_of(part * width + z * cols, LANES), cols)
+        load = pltpu.make_async_copy(
+            weight_ref.at[:, column],
+            weight.at[:, pl.ds(part * cols, cols)],
+            weight_sem.at[part],
+        )
+        load.start()
+        loads.append(load)
+    return loads
+
+
 def ring_neighbours(n_seq):
     n_x = n_seq // GROUPS
     row, seq = lax.axis_index("row"), lax.axis_index("seq")
@@ -879,19 +860,25 @@
     return row, seq, place, after, before
 
 
-def ring_gather(n_seq, parts, rows, out_ref, send_sem, recv_sem, place, after, before):
+def ring_gather(
+    n_seq, parts, rows, out_ref, send_sem, recv_sem, place, after, before, work=None
+):
     n_x = n_seq // GROUPS
     half = rows // 2
     piece = half // parts
     sent = {}
+
+    def start_of(step, way):
+        shift = n_seq - step if way == 0 else step
+        member = ring_member(lax.rem(place + shift, n_seq), n_x)
+        return member * rows + way * half
+
     for step in range(n_seq - 1):
         for c in range(parts):
             for way in range(2):
                 if step:
                     sent[step - 1, c, way].wait_recv()
-                shift = n_seq - step if way == 0 else step
-                member = ring_member(lax.rem(place + shift, n_seq), n_x)
-                where = out_ref.at[span(member * rows + way * half + c * piece, piece)]
+                where = out_ref.at[span(start_of(step, way) + c * piece, piece)]
                 copy = send(
                     where,
                     where,
@@ -901,17 +888,25 @@
                 )
                 copy.start()
                 sent[step, c, way] = copy
-    for c in range(parts):
-        for way in range(2):
+        if work is not None:
+            for way in range(2):
+                work(start_of(step, way), half)
+    for way in range(2):
+        for c in range(parts):
             sent[n_seq - 2, c, way].wait_recv()
+        if work is not None:
+            work(start_of(n_seq - 1, way), half)
     for copy in sent.values():
         copy.wait_send()
 
 
 def gather_seq_kernel(
-    n_row, n_seq, parts, x_ref, up_ref, *refs
+    n_row, n_seq, parts, rotated, x_ref, up_ref, weight_ref, cos_ref, sin_ref, *refs
 ):
-    out_ref, own_ref, send_sem, recv_sem, send_w, recv_w, local_sem = refs[-7:]
+    (
+        out_ref, triple_ref, own_ref, send_sem, recv_sem, send_w, recv_w, local_sem, weight, weight_sem,
+    ) = refs[-10:]
+    loads = load_heads(weight_ref, weight, weight_sem, n_seq // GROUPS)
     row, seq, place, after, before = ring_neighbours(n_seq)
     rows = x_ref.shape[0]
     depth, both = up_ref.shape[1:]
@@ -941,63 +936,93 @@
         copy = pltpu.make_async_copy(source, target, local_sem.at[part])
         copy.start()
         local.append(copy)
+    def project(start, size):
+        here = span(start, size)
+        cosine, sine = cos_ref[here, :], sin_ref[here, :]
+        step = 3 * HEAD_DIM
+        for left in range(0, weight.shape[1], step):
+            triple = product(out_ref[here, :], weight[:, left : left + step])
+            for head in range(0, step, HEAD_DIM):
+                value = triple[:, head : head + HEAD_DIM]
+                if left + head < rotated:
+                    value = value * cosine + turn_half(value) * sine
+                triple_ref[here, left + head : left + head + HEAD_DIM] = value.astype(
+                    triple_ref.dtype
+                )
+
     out_ref[span(seq * rows, rows), :] = x_ref[...]
-    ring_gather(n_seq, parts, rows, out_ref, send_sem, recv_sem, place, after, before)
+    for load in loads:
+        load.wait()
+    ring_gather(n_seq, parts, rows, out_ref, send_sem, recv_sem, place, after, before, project)
     for copy in moved + local:
         copy.wait()
 
 
-def gather_seq(block, up_weight, after=(), collective=15):
+def gather_seq(block, up_weight, weight, cosine, sine, rotated, after=(), collective=15):
     n_row, n_seq = lax.axis_size("row"), lax.axis_size("seq")
     rows, width = block.shape
     parts = 2 if rows % 64 == 0 else 1
     depth, both = up_weight.shape[1:]
     return pl.pallas_call(
-        functools.partial(gather_seq_kernel, n_row, n_seq, parts),
+        functools.partial(gather_seq_kernel, n_row, n_seq, parts, rotated),
         out_shape=(
             jax.ShapeDtypeStruct((n_seq * rows, width), block.dtype),
+            jax.ShapeDtypeStruct((n_seq * rows, weight.shape[1] // GROUPS), block.dtype),
             jax.ShapeDtypeStruct((depth * n_row, both // n_row), up_weight.dtype),
         ),
-        in_specs=[vmem(), anywhere()] + [anywhere()] * len(after),
-        out_specs=(vmem(), anywhere()),
+        in_specs=[vmem()] + [anywhere()] * 2 + [vmem()] * 2 + [anywhere()] * len(after),
+        out_specs=(vmem(), vmem(), anywhere()),
         scratch_shapes=[pltpu.SemaphoreType.DMA((2, n_seq - 1, parts))] * 2
         + [pltpu.SemaphoreType.DMA((n_row - 1, 2))] * 2
-        + [pltpu.SemaphoreType.DMA((2,))],
+        + [pltpu.SemaphoreType.DMA((2,))]
+        + [
+            pltpu.VMEM((width, weight.shape[1] // GROUPS), weight.dtype),
+            pltpu.SemaphoreType.DMA((3,)),
+        ],
         compiler_params=remote_params(collective, 48),
         name="gather_seq",
-    )(block, up_weight, *after)
-
-
-def reduce_seq_kernel(n_seq, parts, x_ref, *refs):
-    out_ref, held, send_sem, recv_sem = refs[-4:]
-    _, _, _, after, before = ring_neighbours(n_seq)
-    greet([after, before])
-    reduce_seq_body(n_seq, parts, x_ref, out_ref, held, send_sem, recv_sem)
-
-
-def reduce_seq_body(n_seq, parts, x_ref, out_ref, held, send_sem, recv_sem):
+    )(block, up_weight, weight, cosine, sine, *after)
+
+
+def reduce_seq_kernel(n_row, n_seq, parts, x_ref, weight_ref, rider_ref, *refs):
+    out_ref, rode_ref, held, made, send_sem, recv_sem, weight, weight_sem, *scratch = refs
     n_x = n_seq // GROUPS
+    loads = load_heads(weight_ref, weight, weight_sem, n_x)
     _, seq, place, after, before = ring_neighbours(n_seq)
-    rows = out_ref.shape[0]
+    rows, width = out_ref.shape
     half = rows // 2
     piece = half // parts
+    sibling, across = row_peers(n_row)
+    greet([after, before, sibling] + across)
+    riding = start_gather_rows(n_row, 4, rider_ref, rode_ref, *scratch)
+    for load in loads:
+        load.wait()
+
+    def make(step, way):
+        shift = 2 * n_seq - 1 - step if way == 0 else 1 + step
+        member = ring_member(lax.rem(place + shift, n_seq), n_x)
+        here = span(member * rows + way * half, half)
+        for left in range(0, width, COLUMNS):
+            made[way, step % 2, :, left : left + COLUMNS] = right_trans(
+                x_ref[here, :], weight[left : left + COLUMNS, :]
+            ).astype(made.dtype)
+
     sent = {}
     for step in range(n_seq - 1):
-        for c in range(parts):
-            for way in range(2):
-                shift = 2 * n_seq - 1 - step if way == 0 else 1 + step
-                member = ring_member(lax.rem(place + shift, n_seq), n_x)
-                own = span(member * rows + way * half + c * piece, piece)
+        for way in range(2):
+            if step == 0:
+                make(step, way)
+            for c in range(parts):
                 where = pl.ds(c * piece, piece)
                 if step:
                     sent[step - 1, c, way].wait_recv()
                     held[way, step - 1, where, :] = (
                         held[way, step - 1, where, :].astype(jnp.float32)
-                        + x_ref[own, :].astype(jnp.float32)
+                        + made[way, step % 2, where, :].astype(jnp.float32)
                     ).astype(held.dtype)
                     source = held.at[way, step - 1, where]
                 else:
-                    source = x_ref.at[own]
+                    source = made.at[way, 0, where]
                 copy = send(
                     source,
                     held.at[way, step, where],
@@ -1007,35 +1032,49 @@
                 )
                 copy.start()
                 sent[step, c, way] = copy
-    for c in range(parts):
         for way in range(2):
+            if step == 1:
+                for c in range(parts):
+                    sent[0, c, way].wait_send()
+            make(step + 1, way)
+    for way in range(2):
+        for c in range(parts):
             sent[n_seq - 2, c, way].wait_recv()
             where = pl.ds(c * piece, piece)
-            start = way * half + c * piece
-            out_ref[pl.ds(start, piece), :] = (
-                held[way, n_seq - 2, where, :].astype(jnp.float32)
-                + x_ref[span(seq * rows + start, piece), :].astype(jnp.float32)
-            ).astype(out_ref.dtype)
-    for copy in sent.values():
-        copy.wait_send()
-
-
-def reduce_seq(partial, after=(), collective=4, dtype=jnp.float32):
-    n_seq = lax.axis_size("seq")
-    rows, width = partial.shape[0] // n_seq, partial.shape[1]
-    if rows % 32:
-        return lax.psum_scatter(partial, "seq", scatter_dimension=0, tiled=True).astype(dtype)
-    parts = 2 if rows % 64 == 0 else 1
+            out_ref[pl.ds(way * half + c * piece, piece), :] = held[
+                way, n_seq - 2, where, :
+            ].astype(jnp.float32) + made[way, (n_seq - 1) % 2, where, :].astype(jnp.float32)
+    for (step, _, _), copy in sent.items():
+        if step:
+            copy.wait_send()
+    finish_gather_rows(riding)
+
+
+def reduce_seq(values, weight, rider, collective=4):
+    n_row, n_seq = lax.axis_size("row"), lax.axis_size("seq")
+    rows, width = values.shape[0] // n_seq, weight.shape[0]
+    parts = 2
     return pl.pallas_call(
-        functools.partial(reduce_seq_kernel, n_seq, parts),
-        out_shape=jax.ShapeDtypeStruct((rows, width), dtype),
-        in_specs=[vmem()] + [anywhere()] * len(after),
-        out_specs=vmem(),
-        scratch_shapes=[pltpu.VMEM((2, n_seq - 1, rows // 2, width), partial.dtype)]
-        + [pltpu.SemaphoreType.DMA((2, n_seq - 1, parts))] * 2,
+        functools.partial(reduce_seq_kernel, n_row, n_seq, parts),
+        out_shape=(
+            jax.ShapeDtypeStruct((rows, width), jnp.float32),
+            jax.ShapeDtypeStruct((n_row * rider.shape[0], rider.shape[1]), rider.dtype),
+        ),
+        in_specs=[vmem(), anywhere(), vmem()],
+        out_specs=(vmem(), vmem()),
+        scratch_shapes=[
+            pltpu.VMEM((2, n_seq - 1, rows // 2, width), values.dtype),
+            pltpu.VMEM((2, 2, rows // 2, width), values.dtype),
+        ]
+        + [pltpu.SemaphoreType.DMA((2, n_seq - 1, parts))] * 2
+        + [
+            pltpu.VMEM((width, values.shape[1]), weight.dtype),
+            pltpu.SemaphoreType.DMA((3,)),
+        ]
+        + gather_rows_scratch(n_row // 2, 4),
         compiler_params=remote_params(collective, 48),
         name="reduce_seq",
-    )(partial, *after)
+    )(values, weight, rider)
 
 
 def exchange_kernel(n_row, n_seq, forward, x_ref, decay_ref, *refs):
@@ -1426,7 +1465,7 @@
 COLUMNS = 512
 
 
-def mlp_kernel(mode, n_row, n_seq, parts, anchors, *refs):
+def mlp_kernel(mode, number, n_row, parts, pieces, *refs):
     forward, both = mode == "forward", mode == "both"
     refs = list(refs)
 
@@ -1435,26 +1474,31 @@
         del refs[:count]
         return taken
 
-    block_ref, up_ref, down_ref = take(3)
+    block_ref, down_ref = take(2)
+    up_refs = take(pieces)
     if both:
         (back_ref,) = take(1)
     elif not forward:
-        gate_ref, raise_ref, ride_ref = take(3)
-    take(anchors)
-    if forward:
-        all_ref, sum_ref, hidden_ref, gate_ref, raise_ref = take(5)
-    elif both:
-        all_ref, sum_ref, hidden_ref, slope_ref, out_ref = take(5)
-    else:
-        all_ref, sum_ref, slope_ref, rode_ref = take(4)
+        gate_in, raise_in = take(2)
+    all_ref, sum_ref = take(2)
+    results = take(3 if forward or both else 1)
+    if not forward and not both:
         back_ref = all_ref
     up, down, local_sem, part, near, stage, far, values_t, back_t, unit_t = take(10)
     send_c, recv_c, send_t, recv_t = take(4)
     gather_scratch = take(5)
     send_y, recv_y, send_f, recv_f, _ = gather_scratch
-    riding = not forward and not both
-    if riding:
-        (ride_sem,) = take(1)
+    (store_sem,) = take(1)
+    if forward:
+        hidden_ref, gate_ref, raise_ref = held = take(3)
+    elif both:
+        hidden_ref, slope_ref, out_ref = held = take(3)
+    else:
+        slope_ref, gate_ref, raise_ref = take(3)
+        held = [slope_ref]
+    stores = [
+        pltpu.make_async_copy(held[i], results[i], store_sem.at[i]) for i in range(len(held))
+    ]
 
     row, seq = lax.axis_index("row"), lax.axis_index("seq")
     y, core = row // 2, lax.rem(row, 2)
@@ -1465,16 +1509,16 @@
     units = down.shape[0]
     sibling, across = row_peers(n_row)
     beside = y * 2 + 1 - core
-    if riding:
-        greet_riders([sibling] + across, n_row, n_seq)
-    else:
-        greet([sibling] + across)
-    if riding:
-        ridden = start_ride(n_row, n_seq, ride_ref, rode_ref, ride_sem)
-    loads = [
-        pltpu.make_async_copy(up_ref, up, local_sem.at[0]),
-        pltpu.make_async_copy(down_ref, down, local_sem.at[1]),
-    ]
+    greet([sibling] + across)
+    loads = [pltpu.make_async_copy(down_ref.at[number], down, local_sem.at[1])]
+    depth = width // pieces
+    for turn in range(pieces):
+        origin = lax.rem(row + turn, n_row) if pieces > 1 else 0
+        where = up.at[span(origin * depth, depth)]
+        loads.append(pltpu.make_async_copy(up_refs[turn], where, local_sem.at[4 + turn]))
+    if not forward and not both:
+        loads.append(pltpu.make_async_copy(gate_in, gate_ref, local_sem.at[2]))
+        loads.append(pltpu.make_async_copy(raise_in, raise_ref, local_sem.at[3]))
     for load in loads:
         load.start()
     started = start_gather_rows(n_row, parts, block_ref, all_ref, *gather_scratch)
@@ -1600,6 +1644,8 @@
 
         lax.fori_loop(0, parts, far_step, 0)
 
+    for store in stores[: 2 if both else 3]:
+        store.start()
     if both:
 
         def result(i, _):
@@ -1616,6 +1662,7 @@
             return 0
 
         lax.fori_loop(0, n_row, result, 0)
+        stores[2].start()
 
     def last(c, _):
         where = span(c * piece, piece)
@@ -1637,15 +1684,15 @@
 
     lax.fori_loop(0, parts, last, 0)
     own.wait_send()
-    if riding:
-        finish_ride(ridden)
-
-
-def mlp_fused(mode, block, up_own, down_own, extra, after, collective, ride=()):
-    n_row, n_seq = lax.axis_size("row"), lax.axis_size("seq")
+    for store in stores:
+        store.wait()
+
+
+def mlp_fused(mode, number, block, ups, downs, extra, collective):
+    n_row = lax.axis_size("row")
     n_y = n_row // 2
     rows, width = block.shape
-    units = down_own.shape[0]
+    units = downs.shape[1]
     parts = 2
     total = n_row * rows
     low, high = jnp.bfloat16, jnp.float32
@@ -1656,20 +1703,22 @@
         shapes += [((total, units), low), ((total, 2 * units), low), ((total, width), low)]
     else:
         shapes += [((total, 2 * units), low)]
-    shapes += [(rider.shape, rider.dtype) for rider in ride]
+    kept = shapes[2:] + [(part.shape, part.dtype) for part in extra if mode == "backward"]
     sem = pltpu.SemaphoreType.DMA
     buffer = (rows, width)
     return pl.pallas_call(
-        functools.partial(mlp_kernel, mode, n_row, n_seq, parts, len(after)),
+        functools.partial(
+            mlp_kernel, mode, number, n_row, parts, len(ups)
+        ),
         out_shape=tuple(jax.ShapeDtypeStruct(*shape) for shape in shapes),
-        in_specs=[vmem(), anywhere(), anywhere()]
-        + [vmem()] * len(extra)
-        + [anywhere()] * (len(ride) + len(after)),
-        out_specs=(vmem(),) * (len(shapes) - len(ride)) + (anywhere(),) * len(ride),
+        in_specs=[vmem(), anywhere()]
+        + [anywhere()] * len(ups)
+        + [vmem() if mode == "both" else anywhere()] * len(extra),
+        out_specs=(vmem(),) * 2 + (anywhere(),) * (len(shapes) - 2),
         scratch_shapes=[
-            pltpu.VMEM(up_own.shape, low),
-            pltpu.VMEM(down_own.shape, low),
-            sem((2,)),
+            pltpu.VMEM((width, 2 * units), low),
+            pltpu.VMEM((units, width), low),
+            sem((4 + len(ups),)),
             pltpu.VMEM((total, width), low),
             pltpu.VMEM((n_y,) + buffer, low),
             pltpu.VMEM((n_y - 1,) + buffer, low),
@@ -1681,10 +1730,62 @@
         + [sem((n_y, parts))] * 2
         + [sem((n_y - 1, parts))] * 2
         + gather_rows_scratch(n_y, parts)
-        + [sem((3,))] * len(ride),
+        + [sem((3,))]
+        + [pltpu.VMEM(*shape) for shape in kept],
         compiler_params=remote_params(collective, 56),
         name="mlp_" + mode,
-    )(block, up_own, down_own, *extra, *ride, *after)
+    )(block, downs, *ups, *extra)
+
+
+def owner_kernel(a_ref, b_ref, out_ref):
+    first, second = a_ref[...], b_ref[...]
+    half = first.shape[1] // 2
+    out_ref[0] = jnp.concatenate([first[:, :half], second[:, :half]], axis=1)
+    out_ref[1] = jnp.concatenate([first[:, half:], second[:, half:]], axis=1)
+
+
+def conv_kernel(x_ref, top_ref, taps_ref, bias_ref, masks_ref, pre_ref, act_ref):
+    values, top = x_ref[...], top_ref[...]
+    edge = lax.broadcasted_iota(jnp.int32, top.shape, 0)
+    total = bias_ref[...] + jnp.zeros_like(values)
+    for tap in range(CONV):
+        shift = CONV - 1 - tap
+        moved = values
+        if shift:
+            moved = pltpu.roll(values, shift, 0)
+            head = jnp.where(edge < shift, pltpu.roll(top, shift, 0), moved[:8])
+            moved = jnp.concatenate([head, moved[8:]], axis=0)
+        total = total + taps_ref[tap : tap + 1, :] * moved * masks_ref[:, tap : tap + 1]
+    pre_ref[...] = total
+    act_ref[...] = (total / (1.0 + jnp.exp(-total))).astype(act_ref.dtype)
+
+
+def conv_forward(mixed, halo, taps, bias, masks):
+    rows = mixed.shape[0]
+    inner = taps.shape[1]
+    cols = 512
+    top = jnp.concatenate([jnp.zeros((8 - halo.shape[0], inner), halo.dtype), halo], axis=0)
+    return pl.pallas_call(
+        conv_kernel,
+        out_shape=(
+            jax.ShapeDtypeStruct((rows, inner), jnp.float32),
+            jax.ShapeDtypeStruct((rows, inner), jnp.bfloat16),
+        ),
+        grid=(inner // cols,),
+        in_specs=[
+            pl.BlockSpec((rows, cols), lambda j: (0, j)),
+            pl.BlockSpec((8, cols), lambda j: (0, j)),
+            pl.BlockSpec((CONV, cols), lambda j: (0, j)),
+            pl.BlockSpec((1, cols), lambda j: (0, j)),
+            pl.BlockSpec((rows, CONV), lambda j: (0, 0)),
+        ],
+        out_specs=(
+            pl.BlockSpec((rows, cols), lambda j: (0, j)),
+            pl.BlockSpec((rows, cols), lambda j: (0, j)),
+        ),
+        compiler_params=pltpu.CompilerParams(vmem_limit_bytes=24 << 20),
+        name="conv_forward",
+    )(mixed, top, taps, bias[None], masks.T)
 
 
 def cycle(depth, breadth):
@@ -1719,6 +1820,19 @@
     n_row, n_seq = lax.axis_size("row"), lax.axis_size("seq")
     rows, columns = half.shape
     owned = columns // (n_row // 2 * n_seq)
+    if n_row == 4 and owned % LANES == LANES // 2:
+        pairs = n_seq // 2
+        return pl.pallas_call(
+            owner_kernel,
+            out_shape=jax.ShapeDtypeStruct((n_seq, rows, 2 * owned), half.dtype),
+            grid=(pairs,),
+            in_specs=[
+                pl.BlockSpec((rows, 2 * owned), lambda i: (0, i)),
+                pl.BlockSpec((rows, 2 * owned), lambda i: (0, pairs + i)),
+            ],
+            out_specs=pl.BlockSpec((2, rows, 2 * owned), lambda i: (i, 0, 0)),
+            name="owner_blocks",
+        )(half, half)
     shaped = half.reshape(rows, n_row // 2, n_seq, owned).transpose(2, 0, 1, 3)
     return shaped.reshape(n_seq, rows, n_row // 2 * owned)
 
@@ -1780,7 +1894,6 @@
     depth, both = up_local.shape[1:]
     ff_dim = both // 2
     ff_row = ff_dim // n_row
-    width = depth * n_row
 
     def slab(dest):
         odd = dest % 2
@@ -1792,14 +1905,34 @@
         ]
         return jnp.concatenate(halves, axis=1)
 
-    whole = jnp.zeros((width, 2 * ff_row), up_local.dtype)
-    for turn in range(n_row):
-        other = row ^ turn
-        piece = slab(other)
-        if turn:
-            piece = lax.ppermute(piece, "row", [(i, i ^ turn) for i in range(n_row)])
-        whole = lax.dynamic_update_slice(whole, piece, (other * depth, 0))
-    return whole
+    pieces = [slab(row)]
+    for turn in range(1, n_row):
+        pieces.append(
+            lax.ppermute(
+                slab((row + n_row - turn) % n_row),
+                "row",
+                [(i, (i - turn) % n_row) for i in range(n_row)],
+            )
+        )
+    return pieces
+
+
+def place_up_grad(grad):
+    n_row = lax.axis_size("row")
+    n_seq = lax.axis_size("seq")
+    holders = [(r, s) for r in range(n_row) for s in range(n_seq)]
+    pairs = []
+    for r, s in holders:
+        owner = owner_of_python(r, s, n_row, n_seq)
+        pairs.append((r * n_seq + s, owner[0] * n_seq + owner[1]))
+    return lax.ppermute(grad, ("row", "seq"), pairs)
+
+
+def owner_of_python(r, s, n_row, n_seq):
+    half = n_seq // 2
+    if s // half == r % 2:
+        return (r // 2, s)
+    return (n_row // 2 + r // 2, (r % 2) * half + s % half)
 
 
 def mlp_gradients(spread, hidden, d_gate_up, upstream_all, extra=(), before=()):
@@ -1935,7 +2068,6 @@
     whole_in = gather_input(input_weight, 10)
     up_local = lax.optimization_barrier((mlp_up_weight, whole_in))[0]
     up_first = own_up_columns(up_local, 0)
-    down_first, down_last = (mlp_down_weight[0], mlp_down_weight[1])
     normed_in, factor_in = norm_apply(source, gain_in)
     low_in = normed_in.astype(jnp.bfloat16)
     low_sent, grad_sent = lax.optimization_barrier((low_in, cotangent[0], whole_in))[:2]
@@ -1950,15 +2082,9 @@
         conv_input[rows_here - (CONV - 1) :].astype(jnp.bfloat16), "seq", 1
     ).astype(jnp.float32)
     padded = jnp.concatenate([halo_rows, conv_input], axis=0)
-    conv_pre = conv_bias.astype(jnp.float32)
-    for tap_index in range(CONV):
-        conv_pre = (
-            conv_pre
-            + conv_taps[tap_index]
-            * padded[tap_index : tap_index + rows_here]
-            * tap_masks[tap_index][:, None]
-        )
-    activated_low = jax.nn.silu(conv_pre).astype(jnp.bfloat16)
+    conv_pre, activated_low = conv_forward(
+        mixed_in, halo_rows, conv_taps, conv_bias.astype(jnp.float32), tap_masks
+    )
     activated = activated_low.astype(jnp.float32)
     picked = product(activated_low, select_weight)
     step_low = picked[:, :rank_dim].astype(jnp.bfloat16)
@@ -1982,21 +2108,11 @@
     first_out = source + product(gated, output_weight)
     normed_first, factor_first = norm_apply(first_out, gains_mlp[0])
     spread_first, second_sum, hidden_first, gate_first, raise_first = mlp_fused(
-        "forward", normed_first.astype(jnp.bfloat16), up_first, down_first, (), (), 1
+        "forward", 0, normed_first.astype(jnp.bfloat16), up_first, mlp_down_weight, (), 1
     )
     second_out = first_out + second_sum
     normed_attn, factor_attn = norm_apply(second_out, gain_attn)
-    context, up_last = gather_seq(normed_attn.astype(jnp.bfloat16), mlp_up_weight, (gathered_in,))
-    length = context.shape[0]
-    head_weight = jnp.concatenate(
-        [
-            lax.dynamic_slice(
-                attn_weight, (0, part * width + z_index * group_cols), (width, group_cols)
-            )
-            for part in range(3)
-        ],
-        axis=1,
-    )
+    length = rows_here * n_seq
     cosine, sine_tab = rotary_tables(jnp.arange(length, dtype=jnp.int32))
     block_starts = (jnp.arange(GROUPS, dtype=jnp.int32) * n_x + x_index) * rows_here
     query_pos = (
@@ -2005,7 +2121,15 @@
     first_key = first_allowed(query_pos, lengths)
     lows = jnp.min(first_key.reshape(GROUPS, rows_here), axis=1)
     x_array = x_index.reshape(1).astype(jnp.int32)
-    triple = project_heads(context, head_weight, cosine, sine_tab, 2 * group_cols)
+    context, triple, up_last = gather_seq(
+        normed_attn.astype(jnp.bfloat16),
+        mlp_up_weight,
+        attn_weight,
+        cosine,
+        sine_tab,
+        2 * group_cols,
+        (gathered_in,),
+    )
     attended, log_total = attend(
         x_array, lows, triple, first_key[:, None], n_x, head_count, rows_here
     )
@@ -2013,13 +2137,11 @@
     third_out = second_out + product(attended_low, attn_output)
     normed_last, factor_last = norm_apply(third_out, gains_mlp[1])
     spread_last, d_normed_last, hidden_last, slope_last, final_partial = mlp_fused(
-        "both", normed_last.astype(jnp.bfloat16), up_last, down_last, (gathered_grad,), (), 2
-    )
-    summed_last = mlp_gradients(spread_last, hidden_last, slope_last, gathered_grad)[1:3]
+        "both", 1, normed_last.astype(jnp.bfloat16), [up_last], mlp_down_weight, (gathered_grad,), 2
+    )
     d_norm_last, g_gain_last = norm_back(third_out, factor_last, gains_mlp[1], d_normed_last)
     d_third = cotangent[0].astype(jnp.float32) + d_norm_last
     d_third_low = d_third.astype(jnp.bfloat16)
-    d_third_rows = lax.all_gather(d_third_low, "row", axis=0, tiled=True)
     d_attended, attended_rows, final_sum = swap_heads(
         right_trans(d_third_low, attn_output).astype(jnp.bfloat16),
         attended_low,
@@ -2028,7 +2150,6 @@
         final_partial,
     )
     output = (third_out + final_sum).astype(jnp.bfloat16)
-    g_down_last = summed_last[1].astype(jnp.float32)
     d_query, d_keys, d_values = attend_back(
         x_array,
         lows,
@@ -2048,9 +2169,11 @@
         own_x, d_query.reshape(GROUPS, 1, rows_here, group_cols), jnp.bfloat16(0)
     ).reshape(length, group_cols)
     d_triple = jnp.concatenate([d_query_full, d_keys, d_values], axis=1)
-    d_attn_normed = reduce_seq(
-        right_trans(d_triple, head_weight).astype(jnp.bfloat16), tuple(summed_last)
-    )
+    d_attn_normed, d_third_rows = reduce_seq(d_triple, attn_weight, d_third_low)
+    summed_last = mlp_gradients(
+        spread_last, hidden_last, slope_last, gathered_grad, (), (d_attn_normed,)
+    )[1:3]
+    g_down_last = summed_last[1].astype(jnp.float32)
     g_attn_local = left_trans(d_triple, context).astype(jnp.bfloat16)
     g_attn_local = lax.optimization_barrier((g_attn_local, d_attn_normed))[0]
     g_attn_weight = lax.psum_scatter(
@@ -2064,15 +2187,14 @@
         second_out, factor_attn, gain_attn, d_attn_normed
     )
     d_second = d_third + d_attn_norm
-    second_rows, d_normed_first, slope_first, up_placed = mlp_fused(
+    second_rows, d_normed_first, slope_first = mlp_fused(
         "backward",
+        0,
         d_second.astype(jnp.bfloat16),
         up_first,
-        down_first,
+        mlp_down_weight,
         (gate_first, raise_first),
-        (d_third_rows,),
         3,
-        (summed_last[0],),
     )
     d_norm_first, g_gain_first = norm_back(first_out, factor_first, gains_mlp[0], d_normed_first)
     d_first = d_second + d_norm_first
@@ -2109,9 +2231,10 @@
         decay_planes,
         (merged_first,),
     )
+    g_attn_weight, up_late = lax.optimization_barrier((g_attn_weight, summed_last[0], end_grad))[:2]
+    attn_placed = place_attn_grad(g_attn_weight, width)
+    up_placed = place_up_grad(up_late)
     g_up_last = up_placed.astype(jnp.float32).T
-    g_attn_weight = lax.optimization_barrier((g_attn_weight, end_grad))[0]
-    attn_placed = place_attn_grad(g_attn_weight, width)
     g_attn_weight = attn_placed.astype(jnp.float32).T
     g_down_first = g_down_first.astype(jnp.float32)
     output_rows = inner_dim // (n_row * n_seq)
@@ -2131,6 +2254,16 @@
     pre_sig = jax.nn.sigmoid(conv_pre)
     d_conv_pre = d_activated * pre_sig * (1.0 + conv_pre * (1.0 - pre_sig))
     g_conv_bias = jnp.sum(d_conv_pre, axis=0)
+    edge = CONV - 1
+    d_edge = jnp.zeros((edge, inner_dim), jnp.float32)
+    for tap_index in range(edge):
+        kept_rows = (
+            d_conv_pre[: edge - tap_index]
+            * tap_masks[tap_index][: edge - tap_index, None]
+            * conv_taps[tap_index]
+        )
+        d_edge = d_edge + jnp.pad(kept_rows, ((tap_index, 0), (0, 0)))
+    back_rows = from_behind(d_edge.astype(jnp.bfloat16), "seq", -1)
     tap_grads = []
     d_padded = jnp.zeros((rows_here + CONV - 1, inner_dim), jnp.float32)
     for tap_index in range(CONV):
@@ -2140,7 +2273,6 @@
             masked * conv_taps[tap_index], ((tap_index, CONV - 1 - tap_index), (0, 0))
         )
     g_conv_weight = jnp.stack(tap_grads, axis=0)
-    back_rows = from_behind(d_padded[: CONV - 1].astype(jnp.bfloat16), "seq", -1)
     d_conv_input = d_padded[CONV - 1 :] + jnp.pad(back_rows, ((rows_here - (CONV - 1), 0), (0, 0)))
     d_conv_low = d_conv_input.astype(jnp.bfloat16)
     d_mixed = jnp.concatenate([d_conv_low, d_gate_low], axis=1)
@@ -2167,7 +2299,7 @@
     lines.append(jnp.zeros((spare, inner_dim), jnp.float32))
     packed = jnp.concatenate(columns + [jnp.concatenate(lines, axis=0).T], axis=1)
     conv_spread, summed = swap_and_reduce(
-        owner_blocks(d_conv_low), packed.astype(jnp.bfloat16), 11, (attn_placed,)
+        owner_blocks(d_conv_low), packed.astype(jnp.bfloat16), 11, (attn_placed, up_placed)
     )
     g_input_weight, first_placed = reduce_rows(
         jnp.concatenate(

time: 1140 us -> 1090 us (0.956)
  local copies, waits for them, and re-layouts: 122 us -> 86 us
  Pallas kernels: 769 us -> 744 us
    pallas_call x6 -> x8, Pallas kernels: 324 us -> 291 us  [the longest x3 136 us: mlp_fused(): pl.pallas_call(functools.partial(mlp_kernel, mode, number, n_row, parts,...]
    reduce_scatter x2, waiting for transfers between devices: 14.5 us -> 0.02 us  [mlp_gradients(): lax.psum_scatter(merged, 'seq', scatter_dimension=0, tiled=True, axis_ind...]
    ppermute x3, waiting for transfers between devices: 0.01 us -> 12.7 us  [place_attn_grad(): moved = lax.ppermute(taken, ('row', 'seq'), [edges[e] for e in chosen])]
    unnamed x304 -> x290, local copies, waits for them, and re-layouts: 53.6 us -> 59.8 us
    dot_general x6 -> x5, matrix products: 48.6 us -> 42.7 us  [right_trans(): lax.dot_general(left_op, right_op, (((1,), (1,)), ((), ())), preferred_el...]
  transfers between devices with their start and end apart: 14 -> 14, of which waited for: 2 -> 3; matrix products, arithmetic and copies ran while one was open for 21% -> 17% of each run, Pallas kernels for 54% -> 44%
where the time goes in v5:
time: 1090 us; the launch traced here: 1080 us
  Pallas kernels  744 us (68%)
  matrix products  101 us (9%)
  local copies, waits for them, and re-layouts  86 us (8%)
  other arithmetic  80.4 us (7%)
  starting transfers between devices  25 us (2%)
  waiting for transfers between devices  21.6 us (2%)
  between operations  18.9 us (2%)
    pallas_call x3, Pallas kernels, mlp_fused(): pl.pallas_call(functools.partial(mlp_kernel, mode, number, n_row, parts,...  136 us
    pallas_call x1, Pallas kernels, gather_seq(): pl.pallas_call(functools.partial(gather_seq_kernel, n_row, n_seq, parts,...  74.7 us
    pallas_call x1, Pallas kernels, reduce_seq(): pl.pallas_call(functools.partial(reduce_seq_kernel, n_row, n_seq, parts),...  68.8 us
    pallas_call x1, Pallas kernels, gather_input(): pl.pallas_call(functools.partial(gather_input_kernel, parts), out_shape=j...  67.9 us
    unnamed x290, local copies, waits for them, and re-layouts  59.8 us
    pallas_call x1, Pallas kernels, exchange_states(): pl.pallas_call(functools.partial(exchange_kernel, n_row, n_seq, False), o...  58.7 us
    pallas_call x2, Pallas kernels, swap_heads(): pl.pallas_call(functools.partial(swap_heads_kernel, n_row, n_x, collect),...  49.1 us
    pallas_call x1, Pallas kernels, adjoint_full(): pl.pallas_call(functools.partial(adjoint_full_kernel, states, chunk, len(...  49 us
  transfers between devices with their start and end apart: 14, of which 3 were waited for; matrix products, arithmetic and copies ran while one was open for 17% of the time, Pallas kernels for 44%

profile of v5, /device:TPU:6, one launch (start us, length us, event | category | flops | bytes accessed | tf_op | source)
XLA Modules:
  0.0 1076.0 jit_solution(2906858712214623964)
XLA Ops:
  11.7 67.9 %gather_input.1 = bf16[1536,6144]{1,0:T(8,128)(2,1)S(1)} custom-call(bf16[384,6144]{1,0:T(8,128)(2,1)S(1)} %copy-done.22), custom_call_target="tpu_custom_call" | custom-call | tf_op jit(solution)/shard_map/gather_input/pallas_call | solution.py:1417
  151.2 13.7 %scan_end.1 = f32[16,24,128]{2,1,0:T(8,128)S(1)} custom-call(f32[256,3072]{1,0:T(8,128)S(1)} %copy-done.2, bf16[256,3072]{1,0:T(8,128)(2,1)S(1)} %get-tuple-element.70.refs_1_.refs_2_.act_ref, f32[256,128]{1,0:T(8,128)S(1)} %broadcast_in_dim.67.refs_2_.refs_3_.keep_ref, f32[4096]{0:T(1024)S(1)} %reshape.425.refs_3_.refs_4_.in_ref, f32[16,24,128]{2,1,0:T(8,128)S(1)} %bitcast.136), custom_call_target="tpu_custom_call" | custom-call | tf_op jit(solution)/shard_map/scan_end/pallas_call | solution.py:136
  165.1 27.0 %exchange_states.1.refs_0_ = f32[16,24,128]{2,1,0:T(8,128)S(1)} custom-call(bf16[448,128]{1,0:T(8,128)(2,1)S(1)} %fusion.39.x_ref, f32[16,24,128]{2,1,0:T(8,128)S(1)} %bitcast.137), custom_call_target="tpu_custom_call" | custom-call | tf_op jit(solution)/shard_map/exchange_states/pallas_call | solution.py:1139
  200.3 19.5 %scan_out.1 = (f32[256,3072]{1,0:T(8,128)S(1)}, f32[8,16,24,128]{3,2,1,0:T(8,128)S(1)}) custom-call(f32[16,24,128]{2,1,0:T(8,128)S(1)} %copy-done.47, f32[256,3072]{1,0:T(8,128)S(1)} %copy-done.3, bf16[256,3072]{1,0:T(8,128)(2,1)S(1)} %get-tuple-element.70.refs_1_.refs_2_.act_ref, f32[256,128]{1,0:T(8,128)S(1)} %broadcast_in_dim.67.refs_2_.refs_3_.keep_ref, ...), custom_call_target="tpu_custom_call" | custom-call | tf_op jit(solution)/shard_map/scan_out/pallas_call | solution.py:155
  231.8 41.0 %mlp_forward.1 = (bf16[1024,1536]{1,0:T(8,128)(2,1)}, f32[256,1536]{1,0:T(8,128)}, bf16[1024,1024]{1,0:T(8,128)(2,1)}, f32[1024,1024]{1,0:T(8,128)}, f32[1024,1024]{1,0:T(8,128)}) custom-call(bf16[256,1536]{1,0:T(8,128)(2,1)} %multiply_convert_fusion.4.refs_0_, bf16[2,1024,1536]{2,1,0:T(8,128)(2,1)} %refs_1_.5, bf16[384,2048]{1,0:T(8,128)(2,1)} %pad_maximum_fusion.4.refs_2_, ...), custom_call_target="tpu_custom_call" | custom-call | tf_op jit(solution)/shard_map/mlp_forward/pallas_call | solution.py:1709
  279.1 74.7 %gather_seq.1 = (bf16[2048,1536]{1,0:T(8,128)(2,1)}, bf16[2048,1152]{1,0:T(8,128)(2,1)}, bf16[1536,2048]{1,0:T(8,128)(2,1)}) custom-call(bf16[256,1536]{1,0:T(8,128)(2,1)S(1)} %copy-done.34, bf16[2,384,8192]{2,1,0:T(8,128)(2,1)} %up_ref.1, bf16[1536,4608]{1,0:T(8,128)(2,1)} %weight_ref.3, f32[2048,128]{1,0:T(8,128)S(1)} %get-tuple-element.319.cos_ref.cos_all, ...), custom_call_target="tpu_custom_call" | custom-call | tf_op jit(solution)/shard_map/gather_seq/pallas_call | solution.py:966
  356.2 20.4 %attend.1 = (bf16[1024,384]{1,0:T(8,128)(2,1)S(1)}, f32[3,1024,1]{2,1,0:T(8,128)S(1)}) custom-call(s32[1]{0:T(128)} %bitcast.17.x_ref, s32[4]{0:T(128)S(1)} %copy-done.55, bf16[2048,1152]{1,0:T(8,128)(2,1)S(1)} %copy-done.1, bf16[2048,1152]{1,0:T(8,128)(2,1)S(1)} %copy-done.1, bf16[2048,1152]{1,0:T(8,128)(2,1)S(1)} %copy-done.1, s32[1024,1]{1,0:T(8,128)S(1)} %copy-done.23), custom_call_target="tpu_custom_call" | custom-call | flops 1610612736 | bytes 3145728 | tf_op jit(solution)/shard_map/attend/pallas_call | solution.py:437
  376.7 19.7 %collect_heads.1 = (bf16[256,1536]{1,0:T(8,128)(2,1)S(1)}, bf16[1024,768]{1,0:T(8,128)(2,1)S(1)}) custom-call(bf16[1024,384]{1,0:T(8,128)(2,1)S(1)} %get-tuple-element.76.x_ref.out_ref, bf16[256,3072]{1,0:T(8,128)(2,1)S(1)} %copy-done.17), custom_call_target="tpu_custom_call" | custom-call | tf_op jit(solution)/shard_map/collect_heads/pallas_call | solution.py:1250
  403.3 49.5 %mlp_both.1 = (bf16[1024,1536]{1,0:T(8,128)(2,1)}, f32[256,1536]{1,0:T(8,128)}, bf16[1024,1024]{1,0:T(8,128)(2,1)}, bf16[1024,2048]{1,0:T(8,128)(2,1)}, bf16[1024,1536]{1,0:T(8,128)(2,1)}) custom-call(bf16[256,1536]{1,0:T(8,128)(2,1)} %multiply_convert_fusion.2.refs_0_, bf16[2,1024,1536]{2,1,0:T(8,128)(2,1)} %refs_1_.5, ...), custom_call_target="tpu_custom_call" | custom-call | tf_op jit(solution)/shard_map/mlp_both/pallas_call | solution.py:1709
  460.2 29.5 %spread_heads.1 = (bf16[1024,384]{1,0:T(8,128)(2,1)S(1)}, bf16[1024,384]{1,0:T(8,128)(2,1)S(1)}, f32[256,1536]{1,0:T(8,128)S(1)}) custom-call(bf16[256,1536]{1,0:T(8,128)(2,1)S(1)} %convolution_convert_fusion.7.x_ref, bf16[256,1536]{1,0:T(8,128)(2,1)S(1)} %copy-done.49, bf16[1024,1536]{1,0:T(8,128)(2,1)S(1)} %copy-done.30), custom_call_target="tpu_custom_call" | custom-call | tf_op jit(solution)/shard_map/spread_heads/pallas_call | solution.py:1250
  490.7 29.5 %attend_back.1 = (bf16[1024,384]{1,0:T(8,128)(2,1)S(1)}, bf16[2048,384]{1,0:T(8,128)(2,1)S(1)}, bf16[2048,384]{1,0:T(8,128)(2,1)S(1)}) custom-call(s32[1]{0:T(128)} %bitcast.17.x_ref, s32[4]{0:T(128)S(1)} %copy-done.56, bf16[2048,1152]{1,0:T(8,128)(2,1)S(1)} %bitcast.135, bf16[2048,1152]{1,0:T(8,128)(2,1)S(1)} %bitcast.135, ...), custom_call_target="tpu_custom_call" | custom-call | flops 4026531840 | bytes 6291456 | tf_op jit(solution)/shard_map/attend_back/pallas_call | solution.py:526
  523.4 68.8 %reduce_seq.1 = (f32[256,1536]{1,0:T(8,128)S(1)}, bf16[1024,1536]{1,0:T(8,128)(2,1)S(1)}) custom-call(bf16[2048,1152]{1,0:T(8,128)(2,1)} %pad_maximum_fusion.x_ref, bf16[1536,4608]{1,0:T(8,128)(2,1)} %weight_ref.3, bf16[256,1536]{1,0:T(8,128)(2,1)S(1)} %fusion.58.rider_ref), custom_call_target="tpu_custom_call" | custom-call | tf_op jit(solution)/shard_map/reduce_seq/pallas_call | solution.py:1057
  595.0 11.3 %convolution_convert_fusion = bf16[1152,1536]{1,0:T(8,128)(2,1)} fusion(bf16[2048,1536]{1,0:T(8,128)(2,1)} %get-tuple-element.102, bf16[2048,384]{1,0:T(8,128)(2,1)S(1)} %get-tuple-element.87, bf16[2048,384]{1,0:T(8,128)(2,1)S(1)} %get-tuple-element.86, bf16[2048,384]{1,0:T(8,128)(2,1)S(1)} %bitcast_select_fusion), kind=kOutput, calls=%fused_computation.1 | convolution fusion | flops 7263682560 | bytes 14548992 | tf_op jit(solution)/shard_map/dot_general | solution.py:35
  611.7 14.1 %grad_blocks.3 = bf16[3072,1536]{1,0:T(8,128)(2,1)} custom-call(bf16[1024,2048]{1,0:T(8,128)(2,1)} %get-tuple-element.111.d_ref, bf16[1024,1536]{1,0:T(8,128)(2,1)S(1)} %copy-done.33, bf16[1024,1024]{1,0:T(8,128)(2,1)S(1)} %copy-done.37, bf16[1024,1536]{1,0:T(8,128)(2,1)S(1)} %copy-done.12), custom_call_target="tpu_custom_call" | custom-call | tf_op jit(solution)/shard_map/grad_blocks/pallas_call | solution.py:1444
  634.2 45.2 %mlp_backward.1 = (bf16[1024,1536]{1,0:T(8,128)(2,1)}, f32[256,1536]{1,0:T(8,128)}, bf16[1024,2048]{1,0:T(8,128)(2,1)}) custom-call(bf16[256,1536]{1,0:T(8,128)(2,1)} %get-tuple-element.265.refs_0_, bf16[2,1024,1536]{2,1,0:T(8,128)(2,1)} %refs_1_.5, bf16[384,2048]{1,0:T(8,128)(2,1)} %pad_maximum_fusion.4.refs_2_, ...), custom_call_target="tpu_custom_call" | custom-call | tf_op jit(solution)/shard_map/mlp_backward/pallas_call | solution.py:1709
  683.6 15.1 %fusion.3 = (bf16[3072]{0:T(1024)(128)(2,1)}, f32[256,3072]{1,0:T(8,128)}, bf16[256,3072]{1,0:T(8,128)(2,1)}, f32[256,3072]{1,0:T(8,128)}) fusion(bf16[256,3072]{1,0:T(8,128)(2,1)S(1)} %get-tuple-element.70.refs_1_.refs_2_.act_ref, f32[256,6144]{1,0:T(8,128)} %copy-done.8, f32[256,3072]{1,0:T(8,128)} %copy-done.28, f32[3072]{0:T(1024)S(1)} %copy-done.107, ...), kind=kOutput, calls=%fused_computation.16 | convolution fusion | flops 2429285376 | bytes 29116416 | tf_op jit(solution)/shard_map/dot_general | solution.py:41
  700.6 13.8 %adjoint_end.1 = f32[16,24,128]{2,1,0:T(8,128)S(1)} custom-call(f32[256,3072]{1,0:T(8,128)S(1)} %copy-done.4, f32[256,3072]{1,0:T(8,128)S(1)} %copy-done.10, f32[256,128]{1,0:T(8,128)S(1)} %broadcast_in_dim.67.refs_2_.refs_3_.keep_ref, f32[4096]{0:T(1024)S(1)} %copy-done.51, f32[16,24,128]{2,1,0:T(8,128)S(1)} %bitcast.139), custom_call_target="tpu_custom_call" | custom-call | tf_op jit(solution)/shard_map/adjoint_end/pallas_call | solution.py:215
  721.5 58.7 %exchange_states_back.1 = (f32[16,24,128]{2,1,0:T(8,128)S(1)}, bf16[8,256,384]{2,1,0:T(8,128)(2,1)S(1)}, bf16[1024,1536]{1,0:T(8,128)(2,1)S(1)}) custom-call(bf16[448,128]{1,0:T(8,128)(2,1)S(1)} %fusion.40.x_ref, f32[16,24,128]{2,1,0:T(8,128)S(1)} %bitcast.140, bf16[8,256,384]{2,1,0:T(8,128)(2,1)S(1)} %copy-done.19, ...), custom_call_target="tpu_custom_call" | custom-call | tf_op jit(solution)/shard_map/exchange_states_back/pallas_call | solution.py:1148
  791.9 15.2 %grad_blocks.2.refs_0_ = bf16[4224,1536]{1,0:T(8,128)(2,1)} custom-call(bf16[1024,2048]{1,0:T(8,128)(2,1)} %get-tuple-element.94.d_ref, bf16[1024,1536]{1,0:T(8,128)(2,1)S(1)} %copy-done.27, bf16[1024,1024]{1,0:T(8,128)(2,1)S(1)} %copy-done.35, bf16[1024,1536]{1,0:T(8,128)(2,1)S(1)} %copy-done.29, bf16[8,144,1536]{2,1,0:T(8,128)(2,1)} %pad_maximum_fusion.1.refs_0_), custom_call_target="tpu_custom_call" | custom-call | tf_op jit(solution)/shard_map/grad_blocks/pallas_call | solution.py:1444
  820.0 49.0 %adjoint_full.1 = (f32[256,3072]{1,0:T(8,128)}, f32[256,3072]{1,0:T(8,128)}, f32[4096,128]{1,0:T(8,128)S(1)}, f32[4096,128]{1,0:T(8,128)}, f32[16,24,128]{2,1,0:T(8,128)S(1)}) custom-call(f32[16,24,128]{2,1,0:T(8,128)S(1)} %copy-done.54, f32[8,16,24,128]{3,2,1,0:T(8,128)S(1)} %copy-done.39, f32[256,3072]{1,0:T(8,128)} %get-tuple-element.285.refs_0_.refs_1_.step_ref, ...), custom_call_target="tpu_custom_call" | custom-call | tf_op jit(solution)/shard_map/adjoint_full/pallas_call | solution.py:351
  880.3 12.3 %fusion.11 = (bf16[3072]{0:T(1024)(128)(2,1)S(1)}, bf16[3072]{0:T(1024)(128)(2,1)S(1)}, bf16[3072]{0:T(1024)(128)(2,1)S(1)}, bf16[3072]{0:T(1024)(128)(2,1)S(1)}...) fusion(f32[256,3072]{1,0:T(8,128)} %get-tuple-element.280, ...), kind=kOutput, calls=%fused_computation.25 | convolution fusion | flops 225887232 | bytes 32442368 | tf_op jit(solution)/shard_map/dot_general | solution.py:41
  953.5 12.7 %collective-permute-done.5 = bf16[48,1536]{1,0:T(8,128)(2,1)S(1)} collective-permute-done((bf16[48,1536]{1,0:T(8,128)(2,1)S(1)}, bf16[48,1536]{1,0:T(8,128)(2,1)S(1)}, u32[]{:S(2)}, u32[]{:S(2)}) %collective-permute-start.5) | collective-permute-done | bytes 147488 | tf_op jit(solution)/shard_map/ppermute | solution.py:2011
  970.2 48.8 %swap_and_reduce.1 = (bf16[8,256,384]{2,1,0:T(8,128)(2,1)S(1)}, f32[96,256]{1,0:T(8,128)S(1)}) custom-call(bf16[8,256,384]{2,1,0:T(8,128)(2,1)S(1)} %copy-done.18, bf16[3072,256]{1,0:T(8,128)(2,1)S(1)} %pad_maximum_fusion.8.packed_ref, bf16[144,1536]{1,0:T(8,128)(2,1)S(1)} %constant_dynamic-update-slice_fusion.refs_0_, ...), custom_call_target="tpu_custom_call" | custom-call | tf_op jit(solution)/shard_map/swap_and_reduce/pallas_call | solution.py:1324
  1032.7 26.0 %reduce_rows.1 = (f32[192,1536]{1,0:T(8,128)S(1)}, bf16[256,1536]{1,0:T(8,128)(2,1)S(1)}) custom-call(bf16[768,1536]{1,0:T(8,128)(2,1)S(1)} %pad_maximum_fusion.3.x_ref, bf16[256,1536]{1,0:T(8,128)(2,1)S(1)} %slice.198.ride_ref), custom_call_target="tpu_custom_call" | custom-call | tf_op jit(solution)/shard_map/reduce_rows/pallas_call | solution.py:822
  (486 shorter events, 274.0 us)
Async XLA Ops:
  7.2 132.1 %copy-start = (bf16[3072,128]{1,0:T(8,128)(2,1)S(1)}, bf16[3072,128]{1,0:T(8,128)(2,1)}, u32[]{:S(2)}) copy-start(bf16[3072,128]{1,0:T(8,128)(2,1)} %param.30) | copy-start | bytes 2359300
  7.2 269.5 %all-gather.3.cloned.1.call-start = ((), (), s32[]{:S(2)}) async-start(), calls=%async_computation.3 | async-start | bytes 7077888 | tf_op jit(solution)/shard_map/all_gather | solution.py:2074
  8.0 71.7 %copy-start.100 = (f32[1536]{0:T(1024)}, f32[1536]{0:T(1024)S(1)}, u32[]{:S(2)}) copy-start(f32[1536]{0:T(1024)S(1)} %convert_element_type.250) | copy-start | bytes 18436
  11.7 67.9 %copy-start.121 = (f32[256]{0:T(256)}, f32[256]{0:T(256)S(1)}, u32[]{:S(2)}) copy-start(f32[256]{0:T(256)S(1)} %add_rsqrt_fusion.3) | copy-start | bytes 3076
  11.7 74.4 %copy-start.74 = (bf16[1,256,1536]{2,1,0:T(8,128)(2,1)S(1)}, bf16[1,256,1536]{2,1,0:T(8,128)(2,1)}, u32[]{:S(2)}) copy-start(bf16[1,256,1536]{2,1,0:T(8,128)(2,1)} %param.25) | copy-start | bytes 2359300
  87.2 316.0 %all-gather.5.cloned.1.call-start = ((), (), s32[]{:S(2)}) async-start(), calls=%async_computation.4 | async-start | bytes 3932160 | tf_op jit(solution)/shard_map/all_gather | solution.py:2077
  99.9 31.4 %collective-permute-start = (bf16[3,3072]{1,0:T(4,128)(2,1)}, bf16[3,3072]{1,0:T(4,128)(2,1)}, u32[]{:S(2)}, u32[]{:S(2)}) collective-permute-start(bf16[3,3072]{1,0:T(4,128)(2,1)} %slice.265), channel_id=1, source_target_pairs={{0,1},{1,2},{2,3},{3,4},{4,5},{5,6},{6,7},{8,9},{9,10},{10,11},{11... | collective-permute-start | bytes 55304 | tf_op jit(solution)/shard_map/ppermute | solution.py:27
  109.4 122.4 %collective-permute-start.1 = (bf16[384,2048]{1,0:T(8,128)(2,1)}, bf16[384,2048]{1,0:T(8,128)(2,1)}, u32[]{:S(2)}, u32[]{:S(2)}) collective-permute-start(bf16[384,2048]{1,0:T(8,128)(2,1)} %pad_maximum_fusion.5), channel_id=1, source_target_pairs={{0,24},{8,0},{16,8},{24,16},{1,25},{9,1},{17,9},{25,17},{2,26},{10... | collective-permute-start | bytes 4718600 | tf_op jit(solution)/shard_map/ppermute | solution.py:1911
  112.1 119.7 %collective-permute-start.2 = (bf16[384,2048]{1,0:T(8,128)(2,1)}, bf16[384,2048]{1,0:T(8,128)(2,1)}, u32[]{:S(2)}, u32[]{:S(2)}) collective-permute-start(bf16[384,2048]{1,0:T(8,128)(2,1)} %pad_maximum_fusion.6), channel_id=1, source_target_pairs={{0,16},{8,24},{16,0},{24,8},{1,17},{9,25},{17,1},{25,9},{2,18},{10... | collective-permute-start | bytes 4718600 | tf_op jit(solution)/shard_map/ppermute | solution.py:1911
  113.7 118.1 %collective-permute-start.3 = (bf16[384,2048]{1,0:T(8,128)(2,1)}, bf16[384,2048]{1,0:T(8,128)(2,1)}, u32[]{:S(2)}, u32[]{:S(2)}) collective-permute-start(bf16[384,2048]{1,0:T(8,128)(2,1)} %pad_maximum_fusion.7), channel_id=1, source_target_pairs={{0,8},{8,16},{16,24},{24,0},{1,9},{9,17},{17,25},{25,1},{2,10},{10... | collective-permute-start | bytes 4718600 | tf_op jit(solution)/shard_map/ppermute | solution.py:1911
  113.9 693.2 %reduce-scatter.4.cloned.1.call-start = ((), (), s32[]{:S(2)}) async-start(), calls=%async_computation.5 | async-start | bytes 3981312 | tf_op jit(solution)/shard_map/reduce_scatter | solution.py:2179
  279.1 74.7 %copy-start.23 = (s32[1024,1]{1,0:T(8,128)S(1)}, s32[1024,1]{1,0:T(8,128)}, u32[]{:S(2)}) copy-start(s32[1024,1]{1,0:T(8,128)} %copy.139.first_ref) | copy-start | bytes 12292
  279.1 74.7 %copy-start.55 = (s32[4]{0:T(128)S(1)}, s32[4]{0:T(128)}, u32[]{:S(2)}) copy-start(s32[4]{0:T(128)} %get-tuple-element.307.low_ref) | copy-start | bytes 52
  403.3 49.5 %copy-start.94 = (f32[1536]{0:T(1024)S(1)}, f32[1536]{0:T(1024)}, u32[]{:S(2)}) copy-start(f32[1536]{0:T(1024)} %get-tuple-element.247) | copy-start | bytes 18436
  403.3 49.5 %copy-start.109 = (f32[256]{0:T(256)S(1)}, f32[256]{0:T(256)}, u32[]{:S(2)}) copy-start(f32[256]{0:T(256)} %copy-done.108) | copy-start | bytes 3076
  606.3 327.1 %reduce-scatter.6.cloned.1.call-start = ((), (), s32[]{:S(2)}) async-start(), calls=%async_computation.6 | async-start | bytes 10616832 | tf_op jit(solution)/shard_map/reduce_scatter | solution.py:1953
  625.9 405.5 %reduce-scatter.8.cloned.1.call-start = ((), (), s32[]{:S(2)}) async-start(), calls=%async_computation.7 | async-start | bytes 14598144 | tf_op jit(solution)/shard_map/reduce_scatter | solution.py:1953
  721.5 59.9 %copy-start.65 = (bf16[1024,384]{1,0:T(8,128)(2,1)S(1)}, bf16[1024,384]{1,0:T(8,128)(2,1)}, u32[]{:S(2)}) copy-start(bf16[1024,384]{1,0:T(8,128)(2,1)} %copy-done.64) | copy-start | bytes 2359300
  894.3 11.0 %collective-permute-start.4 = (bf16[3,3072]{1,0:T(4,128)(2,1)S(1)}, bf16[3,3072]{1,0:T(4,128)(2,1)S(1)}, u32[]{:S(2)}, u32[]{:S(2)}) collective-permute-start(bf16[3,3072]{1,0:T(4,128)(2,1)S(1)} %fusion.44), channel_id=1, source_target_pairs={{1,0},{2,1},{3,2},{4,3},{5,4},{6,5},{7,6},{9,8},{10,9},{11,10},{12... | collective-permute-start | bytes 55304 | tf_op jit(solution)/shard_map/ppermute | solution.py:27
  935.8 30.3 %collective-permute-start.5 = (bf16[48,1536]{1,0:T(8,128)(2,1)S(1)}, bf16[48,1536]{1,0:T(8,128)(2,1)S(1)}, u32[]{:S(2)}, u32[]{:S(2)}) collective-permute-start(bf16[48,1536]{1,0:T(8,128)(2,1)S(1)} %get-tuple-element.290), channel_id=1, source_target_pairs={{0,0},{2,3},{4,6},{6,8},{8,1},{10,4},{12,7},{14,9},{24,2},{26,5},{... | collective-permute-start | bytes 442376 | tf_op jit(solution)/shard_map/ppermute | solution.py:2011
  941.1 25.1 %collective-permute-start.6 = (bf16[48,1536]{1,0:T(8,128)(2,1)S(1)}, bf16[48,1536]{1,0:T(8,128)(2,1)S(1)}, u32[]{:S(2)}, u32[]{:S(2)}) collective-permute-start(bf16[48,1536]{1,0:T(8,128)(2,1)S(1)} %get-tuple-element.289), channel_id=1, source_target_pairs={{0,0},{2,3},{4,5},{6,8},{8,1},{10,4},{12,6},{14,9},{24,2},{26,13},... | collective-permute-start | bytes 442376 | tf_op jit(solution)/shard_map/ppermute | solution.py:2011
  944.2 22.0 %collective-permute-start.7 = (bf16[48,1536]{1,0:T(8,128)(2,1)S(1)}, bf16[48,1536]{1,0:T(8,128)(2,1)S(1)}, u32[]{:S(2)}, u32[]{:S(2)}) collective-permute-start(bf16[48,1536]{1,0:T(8,128)(2,1)S(1)} %get-tuple-element.288), channel_id=1, source_target_pairs={{0,0},{2,2},{4,5},{6,8},{8,1},{10,3},{12,6},{14,9},{24,10},{26,4},... | collective-permute-start | bytes 442376 | tf_op jit(solution)/shard_map/ppermute | solution.py:2011
  946.1 24.1 %collective-permute-start.8 = (bf16[256,1536]{1,0:T(8,128)(2,1)S(1)}, bf16[256,1536]{1,0:T(8,128)(2,1)S(1)}, u32[]{:S(2)}, u32[]{:S(2)}) collective-permute-start(bf16[256,1536]{1,0:T(8,128)(2,1)S(1)} %slice.196), channel_id=1, source_target_pairs={{0,0},{1,1},{2,2},{3,3},{4,16},{5,17},{6,18},{7,19},{8,20},{9,21},... | collective-permute-start | bytes 2359304 | tf_op jit(solution)/shard_map/ppermute | solution.py:1928
  970.2 50.8 %copy-start.31 = (bf16[256,1536]{1,0:T(8,128)(2,1)}, bf16[256,1536]{1,0:T(8,128)(2,1)S(1)}, u32[]{:S(2)}) copy-start(bf16[256,1536]{1,0:T(8,128)(2,1)S(1)} %collective-permute-done.8.refs_1_) | copy-start | bytes 2359300
  (131 other events, 1142.5 us)
Sparse Core Ops, SparseCore 0:
  87.4 68.8 all-gather.2
  157.9 40.7 all-gather.4
  606.4 31.4 reduce-scatter.3
  640.2 104.0 reduce-scatter.5
  807.4 139.4 reduce-scatter.7
